TPU v7x, 512 devices: a whole 4x8x8 slice. The times are simulated.
512 devices in a mesh: fsdp: 32 (over z, x_hi, core), dp: 16 (over y, x_lo).
Axes of the slice: x: 4 (x_hi: 2, x_lo: 2; x = x_hi * 2 + x_lo), y: 8, z: 8, core: 2. Of those that a mesh axis runs over, the one named last changes fastest.
Arguments:
- grad: bfloat16 [64, 1024, 1024], P(None, ('dp', 'fsdp')), may hold values from -64 to 64
- left_root: bfloat16 [64, 1024, 1024], P('fsdp', 'dp'), may hold values from -20 to 20, as said below
- right_root: bfloat16 [64, 1024, 1024], P('fsdp', 'dp'), may hold values from -20 to 20, as said below
- master: float32 [64, 1024, 1024], P('fsdp', 'dp'), may hold values from -6 to 6
- momentum: float32 [64, 1024, 1024], P('fsdp', 'dp'), may hold values from -6 to 6
- second: float32 [64, 1024, 1024], P('fsdp', 'dp'), may hold values from 0.25 to 4
Outputs:
- params: bfloat16 [64, 1024, 1024], P('fsdp')
- new_master: float32 [64, 1024, 1024], P('fsdp', 'dp')
- new_momentum: float32 [64, 1024, 1024], P('fsdp', 'dp')
- new_second: float32 [64, 1024, 1024], P('fsdp', 'dp')
Inputs may be any that keep to these rules, and one draw needn't show every extreme that they name: `left_root`: each block is symmetric. `right_root`: each block is symmetric.
All inputs are finite; a program needn't handle non-finite values.
Results may differ from a plain program's by a relative error of at most 0.0075.
Values may be sent and summed in bfloat16 or wider, within the bound.
No kernel may reach another device: no remote copies, remote signals or barrier semaphores. Data moves between devices by JAX's collectives and lax.ppermute only.
A program may use at most 64 MiB of HBM per device.

v0:
```python
import jax
import jax.numpy as jnp
from jax import lax
from jax.sharding import PartitionSpec as P

momentum_decay = 0.9
second_decay = 0.95
learn_rate = 0.05
adam_eps = 1e-08
norm_eps = 1e-06


def on_device(grad, left_root, right_root, master, momentum, second):
    owned = lax.all_to_all(grad, "fsdp", split_axis=0, concat_axis=1, tiled=True)
    grad_float = owned.astype(jnp.float32)
    new_second = second_decay * second + (1.0 - second_decay) * grad_float * grad_float
    adam_step = grad_float / (jnp.sqrt(new_second) + adam_eps)
    adam_squares = jnp.sum(adam_step * adam_step, axis=(1, 2))
    columns = left_root
    left_float = jnp.einsum(
        "bsk,bkn->bsn",
        columns,
        lax.all_gather(owned, "dp", axis=1, tiled=True),
        preferred_element_type=jnp.float32,
    )
    left_grad = left_float.astype(jnp.bfloat16)
    columns = left_grad
    precond = jnp.einsum(
        "bsk,bkn->bsn",
        columns,
        lax.all_gather(right_root, "dp", axis=1, tiled=True),
        preferred_element_type=jnp.float32,
    )
    precond_squares = jnp.sum(precond * precond, axis=(1, 2))
    adam_total, precond_total = lax.psum((adam_squares, precond_squares), "dp")
    graft = jnp.sqrt(adam_total / (precond_total + norm_eps))
    new_momentum = momentum_decay * momentum + graft[:, None, None] * precond
    new_master = master - learn_rate * new_momentum
    params = lax.all_gather(new_master.astype(jnp.bfloat16), "dp", axis=1, tiled=True)
    return (params, new_master, new_momentum, new_second)


def solution(mesh):
    in_specs = (
        P(None, ("dp", "fsdp"), None),
        P("fsdp", "dp", None),
        P("fsdp", "dp", None),
        P("fsdp", "dp", None),
        P("fsdp", "dp", None),
        P("fsdp", "dp", None),
    )
    out_specs = (
        P("fsdp", None, None),
        P("fsdp", "dp", None),
        P("fsdp", "dp", None),
        P("fsdp", "dp", None),
    )
    return jax.shard_map(
        on_device, mesh=mesh, in_specs=in_specs, out_specs=out_specs, check_vma=False
    )
```

profile of v0, /device:TPU:56, one launch (start us, length us, event | category | flops | bytes accessed | tf_op | source)
XLA Modules:
  0.0 372.8 jit_solution(17705603003438645187)
XLA Ops:
  7.2 0.0 copy-start
  7.2 0.0 all-gather.6.cloned.1.call-start
  7.2 0.7 all-gather.6.cloned.1.call-update
  7.9 0.0 all-gather.4.cloned.1.call-start
  8.0 26.8 %all_to_all.18 = bf16[64,2,1024]{2,1,0:T(2,128)(2,1)S(1)} all-to-all(bf16[64,2,1024]{2,1,0:T(2,128)(2,1)} %param.6), channel_id=1, replica_groups=mesh['fsdp'=32,'dp'=16] {'fsdp'}, dimensions={0} | all-to-all | bytes 524288 | tf_op jit(solution)/shard_map/all_to_all | solution.py:14
  34.7 0.2 copy.12
  34.9 0.8 all_to_all.16
  35.7 0.0 all-gather.4.cloned.1.call-update
  35.8 0.0 all-gather.8.cloned.1.call-start
  35.8 2.2 fusion.3
  38.0 0.0 copy-start.1
  38.0 0.0 copy-start.2
  38.0 77.7 %all-gather.6.cloned.1.call-done = bf16[2,1024,1024]{2,1,0:T(8,128)(2,1)} async-done(((bf16[2,64,1024]{2,1,0:T(8,128)(2,1)}), bf16[2,1024,1024]{2,1,0:T(8,128)(2,1)}) %all-gather.6.cloned.1.call-update) | async-done | bytes 4194320 | tf_op jit(solution)/shard_map/all_gather | solution.py:31
  115.7 104.1 %all-gather.4.cloned.1.call-done = bf16[2,1024,1024]{2,1,0:T(8,128)(2,1)} async-done(((bf16[2,64,1024]{2,1,0:T(8,128)(2,1)}), bf16[2,1024,1024]{2,1,0:T(8,128)(2,1)}) %all-gather.4.cloned.1.call-update) | async-done | bytes 4194320 | tf_op jit(solution)/shard_map/all_gather | solution.py:23
  219.9 0.0 copy-done
  219.9 5.1 %multiply_reduce_fusion = (f32[2]{0:T(128)S(1)}, f32[2,64,1024]{2,1,0:T(8,128)S(1)}) fusion(bf16[2,1024,1024]{2,1,0:T(8,128)(2,1)} %all-gather.6.cloned.1.call-done, bf16[2,64,1024]{2,1,0:T(8,128)(2,1)S(1)} %copy-done, bf16[2,1024,1024]{2,1,0:T(8,128)(2,1)} %all-gather.4.cloned.1.call-done), kind=kOutput, calls=%fused_computation.8 | convolution fusion | flops 537264128 | bytes 9175048 | tf_op jit(solution)/shard_map/bsk,bkn->bsn/dot_general | solution.py:28
  225.0 29.6 %all-reduce = (f32[2]{0:T(128)S(1)}, f32[2]{0:T(128)S(1)}) all-reduce(f32[2]{0:T(128)S(1)} %get-tuple-element.9, f32[2]{0:T(128)S(1)} %get-tuple-element.11), channel_id=1, replica_groups=mesh['fsdp'=32,'dp'=16] {'dp'}, use_global_device_ids=true, to_apply=%region_1.0 | all-reduce | flops 4 | bytes 32 | tf_op jit(solution)/shard_map/psum | solution.py:35
  254.6 0.0 copy-done.1
  254.6 0.0 copy-done.2
  254.6 1.3 fusion.5
  255.9 0.0 all-gather.8.cloned.1.call-update
  255.9 105.7 %all-gather.8.cloned.1.call-done = bf16[2,1024,1024]{2,1,0:T(8,128)(2,1)} async-done(((bf16[2,64,1024]{2,1,0:T(8,128)(2,1)}), bf16[2,1024,1024]{2,1,0:T(8,128)(2,1)}) %all-gather.8.cloned.1.call-update) | async-done | bytes 4194320 | tf_op jit(solution)/shard_map/all_gather | solution.py:39
  361.6 4.6 %copy.14 = bf16[2,1024,1024]{2,1,0:T(8,128)(2,1)} copy(bf16[2,1024,1024]{2,1,0:T(8,128)(2,1)} %all-gather.8.cloned.1.call-done) | data formatting | bytes 8388608
  (1 shorter events, 0.0 us)
Async XLA Ops:
  7.2 212.7 %copy-start = (bf16[2,64,1024]{2,1,0:T(8,128)(2,1)S(1)}, bf16[2,64,1024]{2,1,0:T(8,128)(2,1)}, u32[]{:S(2)}) copy-start(bf16[2,64,1024]{2,1,0:T(8,128)(2,1)} %param.7) | copy-start | bytes 786436
  7.2 108.5 %all-gather.6.cloned.1.call-start = ((), (), s32[]{:S(2)}) async-start(), calls=%async_computation.2 | async-start | bytes 4456448 | tf_op jit(solution)/shard_map/all_gather | solution.py:31
  7.9 211.9 %all-gather.4.cloned.1.call-start = ((), (), s32[]{:S(2)}) async-start(), calls=%async_computation.1 | async-start | bytes 4456448 | tf_op jit(solution)/shard_map/all_gather | solution.py:23
  35.8 325.8 %all-gather.8.cloned.1.call-start = ((), (), s32[]{:S(2)}) async-start(), calls=%async_computation.3 | async-start | bytes 4456448 | tf_op jit(solution)/shard_map/all_gather | solution.py:39
  38.0 216.6 %copy-start.1 = (f32[2,64,1024]{2,1,0:T(8,128)S(1)}, f32[2,64,1024]{2,1,0:T(8,128)}, u32[]{:S(2)}) copy-start(f32[2,64,1024]{2,1,0:T(8,128)} %param.9) | copy-start | bytes 1572868
  38.0 216.6 %copy-start.2 = (f32[2,64,1024]{2,1,0:T(8,128)S(1)}, f32[2,64,1024]{2,1,0:T(8,128)}, u32[]{:S(2)}) copy-start(f32[2,64,1024]{2,1,0:T(8,128)} %param.10) | copy-start | bytes 1572868
Sparse Core Ops, SparseCore 0:
  10.1 105.5 all-gather.5
  118.4 101.4 all-gather.3
  256.0 105.5 all-gather.7
where the time goes:
time: 376 us; the launch traced here: 373 us
  waiting for transfers between devices  288 us (77%)
  blocking collectives  56.4 us (15%)
  between operations  13.8 us (4%)
  local copies, waits for them, and re-layouts  5.64 us (2%)
  matrix products  5.15 us (1%)
    all_gather x1, waiting for transfers between devices, on_device(): lax.all_gather(new_master.astype(jnp.bfloat16), 'dp', axis=1, tiled=True)  106 us
    all_gather x1, waiting for transfers between devices, on_device(): lax.all_gather(owned, 'dp', axis=1, tiled=True)  104 us
    all_gather x1, waiting for transfers between devices, on_device(): lax.all_gather(right_root, 'dp', axis=1, tiled=True)  77.7 us
    psum x1, blocking collectives, on_device(): adam_total, precond_total = lax.psum((adam_squares, precond_squares), 'dp')  29.6 us
    all_to_all x1, blocking collectives, on_device(): lax.all_to_all(grad, 'fsdp', split_axis=0, concat_axis=1, tiled=True)  26.8 us
  transfers between devices with their start and end apart: 3, of which 3 were waited for; matrix products, arithmetic and copies ran while one was open for 1% of the time, Pallas kernels for 0%

commit v1 on v0

v1 whole, which is shorter than its diff:
```python
import jax
import jax.numpy as jnp
from jax import lax
from jax.experimental import pallas as pl
from jax.experimental.pallas import tpu as pltpu
from jax.sharding import Mesh, PartitionSpec as P

momentum_decay = 0.9
second_decay = 0.95
learn_rate = 0.05
adam_eps = 1e-08
norm_eps = 1e-06

Y = 8
OWNERS = ("z", "xh", "c")
GROUP = ("y", "xl")
SWAP = [(0, 1), (1, 0)]


def shift(step):
    return [(i, (i + step) % Y) for i in range(Y)]


def swap(x):
    return lax.ppermute(x, "xl", SWAP)


def ring(chunk):
    found = [(0, chunk)]
    ahead = behind = chunk
    for step in range(1, 5):
        ahead = lax.ppermute(ahead, "y", shift(1))
        found.append((-step, ahead))
        if step < 4:
            behind = lax.ppermute(behind, "y", shift(-1))
            found.append((step, behind))
    return found


def products_kernel(distances, y_ref, left_own, left_other, right, *refs):
    chunks = refs[: len(distances)]
    own, other, squares = refs[len(distances) :]
    rows = left_own.shape[0]
    depth = chunks[0].shape[0]
    y = y_ref[0]
    total = jnp.zeros((2 * rows, right.shape[0]), jnp.float32)
    for distance, chunk in zip(distances, chunks):
        at = pl.multiple_of(lax.rem(y + distance + Y, Y) * depth, depth)
        columns = jnp.concatenate(
            [left_own[:, pl.ds(at, depth)], left_other[:, pl.ds(at, depth)]], axis=0
        )
        total += jnp.dot(columns, chunk[...], preferred_element_type=jnp.float32)
    left_grad = total.astype(jnp.bfloat16)
    precond = jnp.dot(left_grad, right[...], preferred_element_type=jnp.float32)
    own[...] = precond[:rows]
    other[...] = precond[rows:]
    squares[...] = jnp.full(squares.shape, jnp.sum(precond * precond), jnp.float32)


def products(y, left_own, left_other, right, found):
    rows, width = left_own.shape
    vmem = pl.BlockSpec(memory_space=pltpu.VMEM)
    distances = [distance for distance, _ in found]

    def kernel(*refs):
        products_kernel(distances, *refs)

    return pl.pallas_call(
        kernel,
        out_shape=(
            jax.ShapeDtypeStruct((rows, width), jnp.float32),
            jax.ShapeDtypeStruct((rows, width), jnp.float32),
            jax.ShapeDtypeStruct((1, 128), jnp.float32),
        ),
        in_specs=[pl.BlockSpec(memory_space=pltpu.SMEM)] + [vmem] * (3 + len(found)),
        out_specs=(vmem, vmem, vmem),
        compiler_params=pltpu.CompilerParams(vmem_limit_bytes=24 * 1024 * 1024),
        cost_estimate=pl.CostEstimate(
            flops=8 * rows * width * width, bytes_accessed=6 * width * width, transcendentals=0
        ),
    )(y, left_own, left_other, right, *[chunk for _, chunk in found])


def on_device(grad, left_root, right_root, master, momentum, second):
    y = lax.axis_index("y")
    half = lax.axis_index("xl")
    rows = master.shape[1]
    width = master.shape[2]
    first = half == 0

    def pick(x, index):
        return lax.dynamic_index_in_dim(x, index, 0, keepdims=False)

    def ordered(own, other):
        return jnp.where(first, jnp.stack([own, other]), jnp.stack([other, own]))

    away = jnp.stack([pick(right_root, 1 - half), pick(left_root, 1 - half)])
    came = swap(away)
    right_pair = ordered(pick(right_root, half), came[0]).reshape(2 * rows, width)
    right = lax.all_gather(right_pair, "y", axis=0, tiled=True)

    spread = lax.all_to_all(grad, OWNERS + ("xl",), split_axis=0, concat_axis=1, tiled=True)
    pair = spread.reshape(-1, 2, grad.shape[1], width).swapaxes(0, 1).reshape(2 * rows, width)
    found = ring(pair)

    halves = pair.reshape(2, rows, width)
    other_grad = swap(pick(halves, 1 - half))
    owned = ordered(pick(halves, half), other_grad)
    grad_float = owned.astype(jnp.float32)
    new_second = second_decay * second + (1.0 - second_decay) * grad_float * grad_float
    adam_step = grad_float / (jnp.sqrt(new_second) + adam_eps)
    adam_squares = jnp.sum(adam_step * adam_step, axis=(1, 2))

    own, other, squares = products(y[None], pick(left_root, half), came[1], right, found)
    precond = ordered(own, swap(other))

    sums = jnp.concatenate([squares[:, :126], adam_squares[None, :]], axis=1)
    sums = jnp.broadcast_to(sums[None], (2 * Y, 1, 128))
    sums = lax.all_to_all(sums, GROUP, split_axis=0, concat_axis=0, tiled=True)
    sums = jnp.sum(sums.reshape(Y, 2, 128), axis=0)
    adam_total = sums[0, 126:] + sums[1, 126:]
    graft = jnp.sqrt(adam_total / (sums[:, 0] + norm_eps))

    new_momentum = momentum_decay * momentum + graft[:, None, None] * precond
    new_master = master - learn_rate * new_momentum

    rounded = new_master.astype(jnp.bfloat16)
    partner = swap(rounded)
    both = jnp.where(
        first,
        jnp.concatenate([rounded, partner], axis=1),
        jnp.concatenate([partner, rounded], axis=1),
    )
    params = jnp.zeros((2, Y, 2 * rows, width), jnp.bfloat16)
    for distance, chunk in ring(both):
        at = lax.rem(y + distance + Y, Y)
        params = lax.dynamic_update_slice(params, chunk[:, None], (0, at, 0, 0))
    params = params.reshape(2, 2 * Y * rows, width)
    return (params, new_master, new_momentum, new_second)


def solution(mesh):
    split = Mesh(mesh.devices.reshape(8, 2, 2, 8, 2), OWNERS + GROUP)
    state = P(OWNERS, GROUP, None)
    return jax.shard_map(
        on_device,
        mesh=split,
        in_specs=(P(None, GROUP + OWNERS, None),) + (state,) * 5,
        out_specs=(P(OWNERS, None, None), state, state, state),
        check_vma=False,
    )
```

time: 376 us -> 194 us (0.52)
  the two profiles are of different devices: /device:TPU:56 before, /device:TPU:6 now
where the time goes in v1:
time: 194 us
  waiting for transfers between devices  74.2 us (38%)
  starting transfers between devices  63.3 us (33%)
  blocking collectives  25.9 us (13%)
  between operations  14.5 us (7%)
  local copies, waits for them, and re-layouts  8.75 us (5%)
  other arithmetic  5.64 us (3%)
    ppermute x8, waiting for transfers between devices, ring(): ahead = lax.ppermute(ahead, 'y', shift(1))  54.8 us
    all_to_all x1, blocking collectives, on_device(): lax.all_to_all(grad, OWNERS + ('xl',), split_axis=0, concat_axis=1, tiled...  25.9 us
    ppermute x6, starting transfers between devices, ring(): behind = lax.ppermute(behind, 'y', shift(-1))  25.2 us
    ppermute x8, starting transfers between devices, ring(): ahead = lax.ppermute(ahead, 'y', shift(1))  21.9 us
    ppermute x4, waiting for transfers between devices, swap(): return lax.ppermute(x, 'xl', SWAP)  14 us
    ppermute x4, starting transfers between devices, swap(): return lax.ppermute(x, 'xl', SWAP)  9.82 us
    all_to_all x1, starting transfers between devices, on_device(): sums = lax.all_to_all(sums, GROUP, split_axis=0, concat_axis=0, tiled=True)  6.34 us
    all_to_all x1, waiting for transfers between devices, on_device(): sums = lax.all_to_all(sums, GROUP, split_axis=0, concat_axis=0, tiled=True)  5.06 us
  transfers between devices with their start and end apart: 20, of which 12 were waited for; matrix products, arithmetic and copies ran while one was open for 3% of the time, Pallas kernels for 0%

profile of v1, /device:TPU:6, one launch (start us, length us, event | category | flops | bytes accessed | tf_op | source)
XLA Modules:
  0.0 193.6 jit_solution(13101351961452277606)
XLA Ops:
  9.3 2.7 %collective-permute-start = (bf16[2,64,1024]{2,1,0:T(8,128)(2,1)S(1)}, bf16[2,64,1024]{2,1,0:T(8,128)(2,1)S(1)}, u32[]{:S(2)}, u32[]{:S(2)}) collective-permute-start(bf16[2,64,1024]{2,1,0:T(8,128)(2,1)S(1)} %pad_maximum_fusion), channel_id=1, source_target_pairs={{0,1},{1,0},{2,3},{3,2},{4,5},{5,4},{6,7},{7,6},{8,9},{9,8},{10,11... | collective-permute-start | bytes 786440 | tf_op jit(solution)/shard_map/ppermute | solution.py:25
  12.0 7.2 %collective-permute-done = bf16[2,64,1024]{2,1,0:T(8,128)(2,1)S(1)} collective-permute-done((bf16[2,64,1024]{2,1,0:T(8,128)(2,1)S(1)}, bf16[2,64,1024]{2,1,0:T(8,128)(2,1)S(1)}, u32[]{:S(2)}, u32[]{:S(2)}) %collective-permute-start) | collective-permute-done | bytes 262176 | tf_op jit(solution)/shard_map/ppermute | solution.py:25
  20.0 25.9 %all_to_all.14 = bf16[64,2,1024]{2,1,0:T(2,128)(2,1)S(1)} all-to-all(bf16[64,2,1024]{2,1,0:T(2,128)(2,1)} %param.6), channel_id=1, replica_groups=mesh['z'=8,'xh'=2,'c'=2,'y'=8,'xl'=2] {'z','xh','c','xl'}, dimensions={0} | all-to-all | bytes 524288 | tf_op jit(solution)/shard_map/all_to_all | solution.py:102
  46.2 3.5 %collective-permute-start.1 = (bf16[128,1024]{1,0:T(8,128)(2,1)S(1)}, bf16[128,1024]{1,0:T(8,128)(2,1)S(1)}, u32[]{:S(2)}, u32[]{:S(2)}) collective-permute-start(bf16[128,1024]{1,0:T(8,128)(2,1)S(1)} %reshape.107.refs_4_), channel_id=1, source_target_pairs={{0,2},{2,4},{4,6},{6,8},{8,10},{10,12},{12,14},{14,0},{1,3},{3,5},... | collective-permute-start | bytes 786440 | tf_op jit(solution)/shard_map/ppermute | solution.py:32
  49.7 3.8 %collective-permute-start.2 = (bf16[128,1024]{1,0:T(8,128)(2,1)S(1)}, bf16[128,1024]{1,0:T(8,128)(2,1)S(1)}, u32[]{:S(2)}, u32[]{:S(2)}) collective-permute-start(bf16[128,1024]{1,0:T(8,128)(2,1)S(1)} %reshape.107.refs_4_), channel_id=1, source_target_pairs={{0,14},{2,0},{4,2},{6,4},{8,6},{10,8},{12,10},{14,12},{1,15},{3,1}... | collective-permute-start | bytes 786440 | tf_op jit(solution)/shard_map/ppermute | solution.py:35
  53.5 10.1 %collective-permute-done.1.refs_5_ = bf16[128,1024]{1,0:T(8,128)(2,1)S(1)} collective-permute-done((bf16[128,1024]{1,0:T(8,128)(2,1)S(1)}, bf16[128,1024]{1,0:T(8,128)(2,1)S(1)}, u32[]{:S(2)}, u32[]{:S(2)}) %collective-permute-start.1) | collective-permute-done | bytes 262176 | tf_op jit(solution)/shard_map/ppermute | solution.py:32
  65.7 5.0 %collective-permute-start.4 = (bf16[128,1024]{1,0:T(8,128)(2,1)S(1)}, bf16[128,1024]{1,0:T(8,128)(2,1)S(1)}, u32[]{:S(2)}, u32[]{:S(2)}) collective-permute-start(bf16[128,1024]{1,0:T(8,128)(2,1)S(1)} %collective-permute-done.2.refs_6_), channel_id=1, source_target_pairs={{0,14},{2,0},{4,2},{6,4},{8,6},{10,8},{12,10},{14,12},{1,15},{3,1}... | collective-permute-start | bytes 786440 | tf_op jit(solution)/shard_map/ppermute | solution.py:35
  70.7 4.5 %collective-permute-done.3.refs_7_ = bf16[128,1024]{1,0:T(8,128)(2,1)S(1)} collective-permute-done((bf16[128,1024]{1,0:T(8,128)(2,1)S(1)}, bf16[128,1024]{1,0:T(8,128)(2,1)S(1)}, u32[]{:S(2)}, u32[]{:S(2)}) %collective-permute-start.3) | collective-permute-done | bytes 262176 | tf_op jit(solution)/shard_map/ppermute | solution.py:32
  78.3 2.7 %collective-permute-start.8 = (bf16[64,1024]{1,0:T(8,128)(2,1)}, bf16[64,1024]{1,0:T(8,128)(2,1)}, u32[]{:S(2)}, u32[]{:S(2)}) collective-permute-start(bf16[64,1024]{1,0:T(8,128)(2,1)} %get-tuple-element.15), channel_id=1, source_target_pairs={{0,1},{1,0},{2,3},{3,2},{4,5},{5,4},{6,7},{7,6},{8,9},{9,8},{10,11... | collective-permute-start | bytes 393224 | tf_op jit(solution)/shard_map/ppermute | solution.py:25
  81.0 4.8 %collective-permute-start.6 = (bf16[128,1024]{1,0:T(8,128)(2,1)S(1)}, bf16[128,1024]{1,0:T(8,128)(2,1)S(1)}, u32[]{:S(2)}, u32[]{:S(2)}) collective-permute-start(bf16[128,1024]{1,0:T(8,128)(2,1)S(1)} %collective-permute-done.4.refs_8_), channel_id=1, source_target_pairs={{0,14},{2,0},{4,2},{6,4},{8,6},{10,8},{12,10},{14,12},{1,15},{3,1}... | collective-permute-start | bytes 786440 | tf_op jit(solution)/shard_map/ppermute | solution.py:35
  89.9 5.4 %collective-permute-done.7.refs_11_ = bf16[128,1024]{1,0:T(8,128)(2,1)S(1)} collective-permute-done((bf16[128,1024]{1,0:T(8,128)(2,1)S(1)}, bf16[128,1024]{1,0:T(8,128)(2,1)S(1)}, u32[]{:S(2)}, u32[]{:S(2)}) %collective-permute-start.7) | collective-permute-done | bytes 262176 | tf_op jit(solution)/shard_map/ppermute | solution.py:32
  98.8 6.3 %all-to-all-start.1 = ((f32[16,1,128]{2,1,0:T(1,128)}), f32[16,1,128]{2,1,0:T(1,128)S(1)}, u32[]{:S(2)}, u32[]{:S(2)}) async-start(f32[16,1,128]{2,1,0:T(1,128)} %broadcast_in_dim.44), calls=%async_computation.1 | async-start | bytes 16384 | tf_op jit(solution)/shard_map/all_to_all | solution.py:119
  107.2 5.1 %all-to-all-done.1 = f32[16,1,128]{2,1,0:T(1,128)S(1)} async-done(((f32[16,1,128]{2,1,0:T(1,128)}), f32[16,1,128]{2,1,0:T(1,128)S(1)}, u32[]{:S(2)}, u32[]{:S(2)}) %all-to-all-start.1) | async-done | bytes 8224 | tf_op jit(solution)/shard_map/all_to_all | solution.py:119
  118.1 5.9 %collective-permute-done.10 = bf16[2,64,1024]{2,1,0:T(8,128)(2,1)S(1)} collective-permute-done((bf16[2,64,1024]{2,1,0:T(8,128)(2,1)S(1)}, bf16[2,64,1024]{2,1,0:T(8,128)(2,1)S(1)}, u32[]{:S(2)}, u32[]{:S(2)}) %collective-permute-start.10) | collective-permute-done | bytes 262176 | tf_op jit(solution)/shard_map/ppermute | solution.py:25
  124.1 3.4 %collective-permute-start.11 = (bf16[2,128,1024]{2,1,0:T(8,128)(2,1)S(1)}, bf16[2,128,1024]{2,1,0:T(8,128)(2,1)S(1)}, u32[]{:S(2)}, u32[]{:S(2)}) collective-permute-start(bf16[2,128,1024]{2,1,0:T(8,128)(2,1)S(1)} %maximum_select_fusion.2), channel_id=1, source_target_pairs={{0,2},{2,4},{4,6},{6,8},{8,10},{10,12},{12,14},{14,0},{1,3},{3,5},... | collective-permute-start | bytes 1572872 | tf_op jit(solution)/shard_map/ppermute | solution.py:32
  127.5 3.7 %collective-permute-start.12 = (bf16[2,128,1024]{2,1,0:T(8,128)(2,1)S(1)}, bf16[2,128,1024]{2,1,0:T(8,128)(2,1)S(1)}, u32[]{:S(2)}, u32[]{:S(2)}) collective-permute-start(bf16[2,128,1024]{2,1,0:T(8,128)(2,1)S(1)} %maximum_select_fusion.2), channel_id=1, source_target_pairs={{0,14},{2,0},{4,2},{6,4},{8,6},{10,8},{12,10},{14,12},{1,15},{3,1}... | collective-permute-start | bytes 1572872 | tf_op jit(solution)/shard_map/ppermute | solution.py:35
  131.1 7.9 %collective-permute-done.11 = bf16[2,128,1024]{2,1,0:T(8,128)(2,1)S(1)} collective-permute-done((bf16[2,128,1024]{2,1,0:T(8,128)(2,1)S(1)}, bf16[2,128,1024]{2,1,0:T(8,128)(2,1)S(1)}, u32[]{:S(2)}, u32[]{:S(2)}) %collective-permute-start.11) | collective-permute-done | bytes 524320 | tf_op jit(solution)/shard_map/ppermute | solution.py:32
  139.1 3.3 %collective-permute-start.13 = (bf16[2,128,1024]{2,1,0:T(8,128)(2,1)S(1)}, bf16[2,128,1024]{2,1,0:T(8,128)(2,1)S(1)}, u32[]{:S(2)}, u32[]{:S(2)}) collective-permute-start(bf16[2,128,1024]{2,1,0:T(8,128)(2,1)S(1)} %collective-permute-done.11), channel_id=1, source_target_pairs={{0,2},{2,4},{4,6},{6,8},{8,10},{10,12},{12,14},{14,0},{1,3},{3,5},... | collective-permute-start | bytes 1572872 | tf_op jit(solution)/shard_map/ppermute | solution.py:32
  142.5 3.9 %collective-permute-start.14 = (bf16[2,128,1024]{2,1,0:T(8,128)(2,1)S(1)}, bf16[2,128,1024]{2,1,0:T(8,128)(2,1)S(1)}, u32[]{:S(2)}, u32[]{:S(2)}) collective-permute-start(bf16[2,128,1024]{2,1,0:T(8,128)(2,1)S(1)} %collective-permute-done.12), channel_id=1, source_target_pairs={{0,14},{2,0},{4,2},{6,4},{8,6},{10,8},{12,10},{14,12},{1,15},{3,1}... | collective-permute-start | bytes 1572872 | tf_op jit(solution)/shard_map/ppermute | solution.py:35
  147.0 8.1 %collective-permute-done.13 = bf16[2,128,1024]{2,1,0:T(8,128)(2,1)S(1)} collective-permute-done((bf16[2,128,1024]{2,1,0:T(8,128)(2,1)S(1)}, bf16[2,128,1024]{2,1,0:T(8,128)(2,1)S(1)}, u32[]{:S(2)}, u32[]{:S(2)}) %collective-permute-start.13) | collective-permute-done | bytes 524320 | tf_op jit(solution)/shard_map/ppermute | solution.py:32
  155.1 3.1 %collective-permute-start.15 = (bf16[2,128,1024]{2,1,0:T(8,128)(2,1)S(1)}, bf16[2,128,1024]{2,1,0:T(8,128)(2,1)S(1)}, u32[]{:S(2)}, u32[]{:S(2)}) collective-permute-start(bf16[2,128,1024]{2,1,0:T(8,128)(2,1)S(1)} %collective-permute-done.13), channel_id=1, source_target_pairs={{0,2},{2,4},{4,6},{6,8},{8,10},{10,12},{12,14},{14,0},{1,3},{3,5},... | collective-permute-start | bytes 1572872 | tf_op jit(solution)/shard_map/ppermute | solution.py:32
  158.6 4.1 %collective-permute-start.16 = (bf16[2,128,1024]{2,1,0:T(8,128)(2,1)S(1)}, bf16[2,128,1024]{2,1,0:T(8,128)(2,1)S(1)}, u32[]{:S(2)}, u32[]{:S(2)}) collective-permute-start(bf16[2,128,1024]{2,1,0:T(8,128)(2,1)S(1)} %collective-permute-done.14), channel_id=1, source_target_pairs={{0,14},{2,0},{4,2},{6,4},{8,6},{10,8},{12,10},{14,12},{1,15},{3,1}... | collective-permute-start | bytes 1572872 | tf_op jit(solution)/shard_map/ppermute | solution.py:35
  162.7 9.7 %collective-permute-done.15 = bf16[2,128,1024]{2,1,0:T(8,128)(2,1)S(1)} collective-permute-done((bf16[2,128,1024]{2,1,0:T(8,128)(2,1)S(1)}, bf16[2,128,1024]{2,1,0:T(8,128)(2,1)S(1)}, u32[]{:S(2)}, u32[]{:S(2)}) %collective-permute-start.15) | collective-permute-done | bytes 524320 | tf_op jit(solution)/shard_map/ppermute | solution.py:32
  175.6 9.0 %collective-permute-done.17 = bf16[2,128,1024]{2,1,0:T(8,128)(2,1)S(1)} collective-permute-done((bf16[2,128,1024]{2,1,0:T(8,128)(2,1)S(1)}, bf16[2,128,1024]{2,1,0:T(8,128)(2,1)S(1)}, u32[]{:S(2)}, u32[]{:S(2)}) %collective-permute-start.17) | collective-permute-done | bytes 524320 | tf_op jit(solution)/shard_map/ppermute | solution.py:32
  (54 shorter events, 30.1 us)
Async XLA Ops:
  7.2 80.6 %copy-start.2 = (f32[2,64,1024]{2,1,0:T(8,128)S(1)}, f32[2,64,1024]{2,1,0:T(8,128)}, u32[]{:S(2)}) copy-start(f32[2,64,1024]{2,1,0:T(8,128)} %param.11) | copy-start | bytes 1572868
  7.2 88.1 %all-gather.2.cloned.1.call-start = ((), (), s32[]{:S(2)}) async-start(), calls=%async_computation.2 | async-start | bytes 2359296 | tf_op jit(solution)/shard_map/all_gather | solution.py:100
  9.3 9.9 %collective-permute-start = (bf16[2,64,1024]{2,1,0:T(8,128)(2,1)S(1)}, bf16[2,64,1024]{2,1,0:T(8,128)(2,1)S(1)}, u32[]{:S(2)}, u32[]{:S(2)}) collective-permute-start(bf16[2,64,1024]{2,1,0:T(8,128)(2,1)S(1)} %pad_maximum_fusion), channel_id=1, source_target_pairs={{0,1},{1,0},{2,3},{3,2},{4,5},{5,4},{6,7},{7,6},{8,9},{9,8},{10,11... | collective-permute-start | bytes 786440 | tf_op jit(solution)/shard_map/ppermute | solution.py:25
  20.0 93.4 %copy-start.3 = (f32[2,64,1024]{2,1,0:T(8,128)S(1)}, f32[2,64,1024]{2,1,0:T(8,128)}, u32[]{:S(2)}) copy-start(f32[2,64,1024]{2,1,0:T(8,128)} %param.9) | copy-start | bytes 1572868
  46.2 17.4 %collective-permute-start.1 = (bf16[128,1024]{1,0:T(8,128)(2,1)S(1)}, bf16[128,1024]{1,0:T(8,128)(2,1)S(1)}, u32[]{:S(2)}, u32[]{:S(2)}) collective-permute-start(bf16[128,1024]{1,0:T(8,128)(2,1)S(1)} %reshape.107.refs_4_), channel_id=1, source_target_pairs={{0,2},{2,4},{4,6},{6,8},{8,10},{10,12},{12,14},{14,0},{1,3},{3,5},... | collective-permute-start | bytes 786440 | tf_op jit(solution)/shard_map/ppermute | solution.py:32
  49.7 16.0 %collective-permute-start.2 = (bf16[128,1024]{1,0:T(8,128)(2,1)S(1)}, bf16[128,1024]{1,0:T(8,128)(2,1)S(1)}, u32[]{:S(2)}, u32[]{:S(2)}) collective-permute-start(bf16[128,1024]{1,0:T(8,128)(2,1)S(1)} %reshape.107.refs_4_), channel_id=1, source_target_pairs={{0,14},{2,0},{4,2},{6,4},{8,6},{10,8},{12,10},{14,12},{1,15},{3,1}... | collective-permute-start | bytes 786440 | tf_op jit(solution)/shard_map/ppermute | solution.py:35
  63.6 11.6 %collective-permute-start.3 = (bf16[128,1024]{1,0:T(8,128)(2,1)S(1)}, bf16[128,1024]{1,0:T(8,128)(2,1)S(1)}, u32[]{:S(2)}, u32[]{:S(2)}) collective-permute-start(bf16[128,1024]{1,0:T(8,128)(2,1)S(1)} %collective-permute-done.1.refs_5_), channel_id=1, source_target_pairs={{0,2},{2,4},{4,6},{6,8},{8,10},{10,12},{12,14},{14,0},{1,3},{3,5},... | collective-permute-start | bytes 786440 | tf_op jit(solution)/shard_map/ppermute | solution.py:32
  65.7 15.3 %collective-permute-start.4 = (bf16[128,1024]{1,0:T(8,128)(2,1)S(1)}, bf16[128,1024]{1,0:T(8,128)(2,1)S(1)}, u32[]{:S(2)}, u32[]{:S(2)}) collective-permute-start(bf16[128,1024]{1,0:T(8,128)(2,1)S(1)} %collective-permute-done.2.refs_6_), channel_id=1, source_target_pairs={{0,14},{2,0},{4,2},{6,4},{8,6},{10,8},{12,10},{14,12},{1,15},{3,1}... | collective-permute-start | bytes 786440 | tf_op jit(solution)/shard_map/ppermute | solution.py:35
  75.2 10.6 %collective-permute-start.5 = (bf16[128,1024]{1,0:T(8,128)(2,1)S(1)}, bf16[128,1024]{1,0:T(8,128)(2,1)S(1)}, u32[]{:S(2)}, u32[]{:S(2)}) collective-permute-start(bf16[128,1024]{1,0:T(8,128)(2,1)S(1)} %collective-permute-done.3.refs_7_), channel_id=1, source_target_pairs={{0,2},{2,4},{4,6},{6,8},{8,10},{10,12},{12,14},{14,0},{1,3},{3,5},... | collective-permute-start | bytes 786440 | tf_op jit(solution)/shard_map/ppermute | solution.py:32
  78.3 9.4 %collective-permute-start.8 = (bf16[64,1024]{1,0:T(8,128)(2,1)}, bf16[64,1024]{1,0:T(8,128)(2,1)}, u32[]{:S(2)}, u32[]{:S(2)}) collective-permute-start(bf16[64,1024]{1,0:T(8,128)(2,1)} %get-tuple-element.15), channel_id=1, source_target_pairs={{0,1},{1,0},{2,3},{3,2},{4,5},{5,4},{6,7},{7,6},{8,9},{9,8},{10,11... | collective-permute-start | bytes 393224 | tf_op jit(solution)/shard_map/ppermute | solution.py:25
  81.0 8.8 %collective-permute-start.6 = (bf16[128,1024]{1,0:T(8,128)(2,1)S(1)}, bf16[128,1024]{1,0:T(8,128)(2,1)S(1)}, u32[]{:S(2)}, u32[]{:S(2)}) collective-permute-start(bf16[128,1024]{1,0:T(8,128)(2,1)S(1)} %collective-permute-done.4.refs_8_), channel_id=1, source_target_pairs={{0,14},{2,0},{4,2},{6,4},{8,6},{10,8},{12,10},{14,12},{1,15},{3,1}... | collective-permute-start | bytes 786440 | tf_op jit(solution)/shard_map/ppermute | solution.py:35
  85.8 9.5 %collective-permute-start.7 = (bf16[128,1024]{1,0:T(8,128)(2,1)S(1)}, bf16[128,1024]{1,0:T(8,128)(2,1)S(1)}, u32[]{:S(2)}, u32[]{:S(2)}) collective-permute-start(bf16[128,1024]{1,0:T(8,128)(2,1)S(1)} %collective-permute-done.5.refs_9_), channel_id=1, source_target_pairs={{0,2},{2,4},{4,6},{6,8},{8,10},{10,12},{12,14},{14,0},{1,3},{3,5},... | collective-permute-start | bytes 786440 | tf_op jit(solution)/shard_map/ppermute | solution.py:32
  95.3 1.6 copy-start
  98.8 13.4 %all-to-all-start.1 = ((f32[16,1,128]{2,1,0:T(1,128)}), f32[16,1,128]{2,1,0:T(1,128)S(1)}, u32[]{:S(2)}, u32[]{:S(2)}) async-start(f32[16,1,128]{2,1,0:T(1,128)} %broadcast_in_dim.44), calls=%async_computation.1 | async-start | bytes 16384 | tf_op jit(solution)/shard_map/all_to_all | solution.py:119
  105.2 8.3 %collective-permute-start.9 = (f32[64,1024]{1,0:T(8,128)S(1)}, f32[64,1024]{1,0:T(8,128)S(1)}, u32[]{:S(2)}, u32[]{:S(2)}) collective-permute-start(f32[64,1024]{1,0:T(8,128)S(1)} %get-tuple-element.9), channel_id=1, source_target_pairs={{0,1},{1,0},{2,3},{3,2},{4,5},{5,4},{6,7},{7,6},{8,9},{9,8},{10,11... | collective-permute-start | bytes 786440 | tf_op jit(solution)/shard_map/ppermute | solution.py:25
  115.7 8.3 %collective-permute-start.10 = (bf16[2,64,1024]{2,1,0:T(8,128)(2,1)S(1)}, bf16[2,64,1024]{2,1,0:T(8,128)(2,1)S(1)}, u32[]{:S(2)}, u32[]{:S(2)}) collective-permute-start(bf16[2,64,1024]{2,1,0:T(8,128)(2,1)S(1)} %get-tuple-element.10), channel_id=1, source_target_pairs={{0,1},{1,0},{2,3},{3,2},{4,5},{5,4},{6,7},{7,6},{8,9},{9,8},{10,11... | collective-permute-start | bytes 786440 | tf_op jit(solution)/shard_map/ppermute | solution.py:25
  124.1 15.0 %collective-permute-start.11 = (bf16[2,128,1024]{2,1,0:T(8,128)(2,1)S(1)}, bf16[2,128,1024]{2,1,0:T(8,128)(2,1)S(1)}, u32[]{:S(2)}, u32[]{:S(2)}) collective-permute-start(bf16[2,128,1024]{2,1,0:T(8,128)(2,1)S(1)} %maximum_select_fusion.2), channel_id=1, source_target_pairs={{0,2},{2,4},{4,6},{6,8},{8,10},{10,12},{12,14},{14,0},{1,3},{3,5},... | collective-permute-start | bytes 1572872 | tf_op jit(solution)/shard_map/ppermute | solution.py:32
  127.5 15.0 %collective-permute-start.12 = (bf16[2,128,1024]{2,1,0:T(8,128)(2,1)S(1)}, bf16[2,128,1024]{2,1,0:T(8,128)(2,1)S(1)}, u32[]{:S(2)}, u32[]{:S(2)}) collective-permute-start(bf16[2,128,1024]{2,1,0:T(8,128)(2,1)S(1)} %maximum_select_fusion.2), channel_id=1, source_target_pairs={{0,14},{2,0},{4,2},{6,4},{8,6},{10,8},{12,10},{14,12},{1,15},{3,1}... | collective-permute-start | bytes 1572872 | tf_op jit(solution)/shard_map/ppermute | solution.py:35
  139.1 16.1 %collective-permute-start.13 = (bf16[2,128,1024]{2,1,0:T(8,128)(2,1)S(1)}, bf16[2,128,1024]{2,1,0:T(8,128)(2,1)S(1)}, u32[]{:S(2)}, u32[]{:S(2)}) collective-permute-start(bf16[2,128,1024]{2,1,0:T(8,128)(2,1)S(1)} %collective-permute-done.11), channel_id=1, source_target_pairs={{0,2},{2,4},{4,6},{6,8},{8,10},{10,12},{12,14},{14,0},{1,3},{3,5},... | collective-permute-start | bytes 1572872 | tf_op jit(solution)/shard_map/ppermute | solution.py:32
  142.5 16.1 %collective-permute-start.14 = (bf16[2,128,1024]{2,1,0:T(8,128)(2,1)S(1)}, bf16[2,128,1024]{2,1,0:T(8,128)(2,1)S(1)}, u32[]{:S(2)}, u32[]{:S(2)}) collective-permute-start(bf16[2,128,1024]{2,1,0:T(8,128)(2,1)S(1)} %collective-permute-done.12), channel_id=1, source_target_pairs={{0,14},{2,0},{4,2},{6,4},{8,6},{10,8},{12,10},{14,12},{1,15},{3,1}... | collective-permute-start | bytes 1572872 | tf_op jit(solution)/shard_map/ppermute | solution.py:35
  155.1 17.3 %collective-permute-start.15 = (bf16[2,128,1024]{2,1,0:T(8,128)(2,1)S(1)}, bf16[2,128,1024]{2,1,0:T(8,128)(2,1)S(1)}, u32[]{:S(2)}, u32[]{:S(2)}) collective-permute-start(bf16[2,128,1024]{2,1,0:T(8,128)(2,1)S(1)} %collective-permute-done.13), channel_id=1, source_target_pairs={{0,2},{2,4},{4,6},{6,8},{8,10},{10,12},{12,14},{14,0},{1,3},{3,5},... | collective-permute-start | bytes 1572872 | tf_op jit(solution)/shard_map/ppermute | solution.py:32
  158.6 17.0 %collective-permute-start.16 = (bf16[2,128,1024]{2,1,0:T(8,128)(2,1)S(1)}, bf16[2,128,1024]{2,1,0:T(8,128)(2,1)S(1)}, u32[]{:S(2)}, u32[]{:S(2)}) collective-permute-start(bf16[2,128,1024]{2,1,0:T(8,128)(2,1)S(1)} %collective-permute-done.14), channel_id=1, source_target_pairs={{0,14},{2,0},{4,2},{6,4},{8,6},{10,8},{12,10},{14,12},{1,15},{3,1}... | collective-permute-start | bytes 1572872 | tf_op jit(solution)/shard_map/ppermute | solution.py:35
  172.4 12.3 %collective-permute-start.17 = (bf16[2,128,1024]{2,1,0:T(8,128)(2,1)S(1)}, bf16[2,128,1024]{2,1,0:T(8,128)(2,1)S(1)}, u32[]{:S(2)}, u32[]{:S(2)}) collective-permute-start(bf16[2,128,1024]{2,1,0:T(8,128)(2,1)S(1)} %collective-permute-done.15), channel_id=1, source_target_pairs={{0,2},{2,4},{4,6},{6,8},{8,10},{10,12},{12,14},{14,0},{1,3},{3,5},... | collective-permute-start | bytes 1572872 | tf_op jit(solution)/shard_map/ppermute | solution.py:32
  184.7 2.0 %copy-start.1 = (bf16[2,8,128,1024]{3,2,1,0:T(8,128)(2,1)}, bf16[2,8,128,1024]{3,2,1,0:T(8,128)(2,1)S(1)}, u32[]{:S(2)}) copy-start(bf16[2,8,128,1024]{3,2,1,0:T(8,128)(2,1)S(1)} %bitcast_dynamic-update-slice_fusion) | copy-start | bytes 12582916
Sparse Core Ops, SparseCore 0:
  20.1 52.8 all-gather.1

commit v2 on v1

v2 whole, which is shorter than its diff:
```python
import jax
import jax.numpy as jnp
from jax import lax
from jax.experimental import pallas as pl
from jax.experimental.pallas import tpu as pltpu
from jax.sharding import Mesh, PartitionSpec as P

momentum_decay = 0.9
second_decay = 0.95
learn_rate = 0.05
adam_eps = 1e-08
norm_eps = 1e-06

Y = 8
OWNERS = ("z", "xh", "c")
GROUP = ("y", "xl")
SWAP = [(0, 1), (1, 0)]
VMEM = pl.BlockSpec(memory_space=pltpu.VMEM)
SMEM = pl.BlockSpec(memory_space=pltpu.SMEM)
PARAMS = pltpu.CompilerParams(vmem_limit_bytes=24 * 1024 * 1024)


def shift(step):
    return [(i, (i + step) % Y) for i in range(Y)]


def swap(x):
    return lax.ppermute(x, "xl", SWAP)


def ring(chunk):
    found = [(0, chunk)]
    ahead = behind = chunk
    for step in range(1, 5):
        ahead = lax.ppermute(ahead, "y", shift(1))
        found.append((-step, ahead))
        if step < 4:
            behind = lax.ppermute(behind, "y", shift(-1))
            found.append((step, behind))
    return found


def left_kernel(distances, place, left_own, left_other, *refs):
    chunks, out = refs[:-1], refs[-1]
    rows = left_own.shape[0]
    depth = chunks[0].shape[0]
    total = jnp.zeros((2 * rows, out.shape[1]), jnp.float32)
    for distance, chunk in zip(distances, chunks):
        at = pl.multiple_of(lax.rem(place[0] + distance + Y, Y) * depth, depth)
        columns = jnp.concatenate(
            [left_own[:, pl.ds(at, depth)], left_other[:, pl.ds(at, depth)]], axis=0
        )
        total += jnp.dot(columns, chunk[...], preferred_element_type=jnp.float32)
    rounded = total.astype(jnp.bfloat16)
    half = place[1]
    out[pl.ds(pl.multiple_of(half * rows, rows), rows), :] = rounded[:rows]
    out[pl.ds(pl.multiple_of((1 - half) * rows, rows), rows), :] = rounded[rows:]


def right_kernel(place, adam, mine, theirs, right, out, sums):
    depth = right.shape[0] * right.shape[2]
    half = place[1]
    squares = []
    for block in range(2):
        left_grad = jnp.where(half == block, mine[...], theirs[...])
        columns = right[:, block].reshape(depth, right.shape[3])
        part = lax.dot_general(
            left_grad, columns, (((1,), (1,)), ((), ())), preferred_element_type=jnp.float32
        )
        out[block] = part.astype(jnp.bfloat16)
        squares.append(jnp.sum(part * part))
    row = lax.broadcasted_iota(jnp.int32, (8, 128), 0)
    values = jnp.where(row < 2, jnp.where(row == 0, squares[0], squares[1]), jnp.where(row == 2, adam[0], adam[1]))
    for i in range(sums.shape[0]):
        sums[i] = values


def update_kernel(place, sums, mine, theirs, base_own, base_other, master, momentum, params, new_master, new_momentum, precond):
    rows, width = master.shape[1:]
    half = place[1]
    total = jnp.sum(sums[...], axis=0)
    own = pl.ds(pl.multiple_of(half * rows, rows), rows)
    other = pl.ds(pl.multiple_of((1 - half) * rows, rows), rows)
    low = lax.broadcasted_iota(jnp.int32, (2 * rows, 128), 1) < 64
    for block in range(2):
        graft = jnp.sqrt(total[2 + block : 3 + block] / (total[block : block + 1] + norm_eps))
        for i in range(Y // 2):
            cut = slice(i * 128, (i + 1) * 128)
            a = mine[block, :, cut].astype(jnp.float32)
            b = theirs[block, :, cut].astype(jnp.float32)
            first = jnp.where(half == 0, a, b)
            second = jnp.where(half == 0, b, a)
            even = jnp.where(low, first, pltpu.roll(second, 64, 1))
            odd = jnp.where(low, pltpu.roll(first, 64, 1), second)
            precond[:, 2 * i * 128 : (2 * i + 1) * 128] = graft * even
            precond[:, (2 * i + 1) * 128 : (2 * i + 2) * 128] = graft * odd
        ours = precond[own, :]
        moved = momentum_decay * momentum[block] + ours
        new_momentum[block] = moved
        new_master[block] = master[block] - learn_rate * moved
        params[block, own, :] = (base_own[block] - learn_rate * ours).astype(jnp.bfloat16)
        params[block, other, :] = (base_other[block] - learn_rate * precond[other, :]).astype(jnp.bfloat16)


def on_device(grad, left_root, right_root, master, momentum, second):
    y = lax.axis_index("y")
    half = lax.axis_index("xl")
    place = jnp.stack([y, half])
    _, rows, width = master.shape
    first = half == 0
    f32, bf16 = jnp.float32, jnp.bfloat16

    def pick(x, index):
        return lax.dynamic_index_in_dim(x, index, 0, keepdims=False)

    right = lax.all_gather(right_root, "y", axis=0, tiled=False)

    spread = lax.all_to_all(grad, OWNERS + ("xl",), split_axis=0, concat_axis=1, tiled=True)
    pair = spread.reshape(-1, 2, grad.shape[1], width).swapaxes(0, 1).reshape(2 * rows, width)
    found = ring(pair)

    left_other = swap(pick(left_root, 1 - half))
    base_own = master - (learn_rate * momentum_decay) * momentum
    base_other = swap(base_own)

    halves = pair.reshape(2, rows, width)
    other_grad = swap(pick(halves, 1 - half))
    own_grad = pick(halves, half)
    owned = jnp.where(first, jnp.stack([own_grad, other_grad]), jnp.stack([other_grad, own_grad]))
    grad_float = owned.astype(f32)
    new_second = second_decay * second + (1.0 - second_decay) * grad_float * grad_float
    adam_step = grad_float / (jnp.sqrt(new_second) + adam_eps)
    adam_squares = jnp.sum(adam_step * adam_step, axis=(1, 2))

    distances = [distance for distance, _ in found]
    left_grad = pl.pallas_call(
        lambda *refs: left_kernel(distances, *refs),
        out_shape=jax.ShapeDtypeStruct((2 * rows, width), bf16),
        in_specs=[SMEM] + [VMEM] * (2 + len(found)),
        out_specs=VMEM,
        compiler_params=PARAMS,
        cost_estimate=pl.CostEstimate(
            flops=4 * rows * width * width, bytes_accessed=3 * width * width, transcendentals=0
        ),
    )(place, pick(left_root, half), left_other, *[chunk for _, chunk in found])
    left_grad_other = swap(left_grad)

    part, sums = pl.pallas_call(
        right_kernel,
        out_shape=(
            jax.ShapeDtypeStruct((2, 2 * rows, width // 2), bf16),
            jax.ShapeDtypeStruct((2 * Y, 8, 128), f32),
        ),
        in_specs=[SMEM, SMEM] + [VMEM] * 3,
        out_specs=(VMEM, VMEM),
        compiler_params=PARAMS,
        cost_estimate=pl.CostEstimate(
            flops=4 * rows * width * width, bytes_accessed=3 * width * width, transcendentals=0
        ),
    )(place, adam_squares, left_grad, left_grad_other, right)
    part_other = swap(part)
    sums = lax.all_to_all(sums, GROUP, split_axis=0, concat_axis=0, tiled=True)

    both, new_master, new_momentum = pl.pallas_call(
        update_kernel,
        out_shape=(
            jax.ShapeDtypeStruct((2, 2 * rows, width), bf16),
            jax.ShapeDtypeStruct(master.shape, f32),
            jax.ShapeDtypeStruct(master.shape, f32),
        ),
        in_specs=[SMEM] + [VMEM] * 7,
        out_specs=(VMEM, VMEM, VMEM),
        scratch_shapes=[pltpu.VMEM((2 * rows, width), f32)],
        compiler_params=PARAMS,
        cost_estimate=pl.CostEstimate(
            flops=16 * rows * width, bytes_accessed=60 * rows * width, transcendentals=0
        ),
    )(place, sums, part, part_other, base_own, base_other, master, momentum)

    params = jnp.zeros((2, Y, 2 * rows, width), bf16)
    ahead = behind = both

    def put(params, chunk, block, distance):
        at = lax.rem(y + distance + Y, Y)
        return lax.dynamic_update_slice(params, chunk[:, None], (block, at, 0, 0))

    params = put(params, both, 0, 0)
    for step in range(1, 4):
        ahead = lax.ppermute(ahead, "y", shift(1))
        behind = lax.ppermute(behind, "y", shift(-1))
        params = put(params, ahead, 0, -step)
        params = put(params, behind, 0, step)
    params = put(params, lax.ppermute(ahead[:1], "y", shift(1)), 0, 4)
    params = put(params, lax.ppermute(behind[1:], "y", shift(-1)), 1, 4)
    params = params.reshape(2, 2 * Y * rows, width)
    return (params, new_master, new_momentum, new_second)


def solution(mesh):
    split = Mesh(mesh.devices.reshape(8, 2, 2, 8, 2), OWNERS + GROUP)
    state = P(OWNERS, GROUP, None)
    return jax.shard_map(
        on_device,
        mesh=split,
        in_specs=(P(None, GROUP + OWNERS, None),) + (state,) * 5,
        out_specs=(P(OWNERS, None, None), state, state, state),
        check_vma=False,
    )
```

time: 194 us -> 197 us (1.015)
  the two profiles are of different devices: /device:TPU:6 before, /device:TPU:56 now
where the time goes in v2:
time: 197 us; the launch traced here: 196 us
  starting transfers between devices  74.3 us (38%)
  waiting for transfers between devices  61 us (31%)
  blocking collectives  26.6 us (14%)
  between operations  14.5 us (7%)
  local copies, waits for them, and re-layouts  12.2 us (6%)
  Pallas kernels  5.39 us (3%)
  other arithmetic  2.45 us (1%)
    all_to_all x1, blocking collectives, on_device(): lax.all_to_all(grad, OWNERS + ('xl',), split_axis=0, concat_axis=1, tiled...  26.6 us
    ppermute x3, waiting for transfers between devices, on_device(): ahead = lax.ppermute(ahead, 'y', shift(1))  23.4 us
    ppermute x4, waiting for transfers between devices, ring(): ahead = lax.ppermute(ahead, 'y', shift(1))  19.2 us
    ppermute x5, starting transfers between devices, swap(): return lax.ppermute(x, 'xl', SWAP)  15.8 us
    ppermute x3, starting transfers between devices, on_device(): ahead = lax.ppermute(ahead, 'y', shift(1))  15.5 us
    ppermute x4, starting transfers between devices, ring(): ahead = lax.ppermute(ahead, 'y', shift(1))  15.1 us
    ppermute x3, starting transfers between devices, ring(): behind = lax.ppermute(behind, 'y', shift(-1))  8.53 us
    all_to_all x1, waiting for transfers between devices, on_device(): sums = lax.all_to_all(sums, GROUP, split_axis=0, concat_axis=0, tiled=True)  6.77 us
  transfers between devices with their start and end apart: 22, of which 13 were waited for; matrix products, arithmetic and copies ran while one was open for 4% of the time, Pallas kernels for 2%

profile of v2, /device:TPU:56, one launch (start us, length us, event | category | flops | bytes accessed | tf_op | source)
XLA Modules:
  0.0 196.3 jit_solution(14133251256870991767)
XLA Ops:
  7.9 26.6 %all_to_all.14 = bf16[64,2,1024]{2,1,0:T(2,128)(2,1)S(1)} all-to-all(bf16[64,2,1024]{2,1,0:T(2,128)(2,1)} %param.6), channel_id=1, replica_groups=mesh['z'=8,'xh'=2,'c'=2,'y'=8,'xl'=2] {'z','xh','c','xl'}, dimensions={0} | all-to-all | bytes 524288 | tf_op jit(solution)/shard_map/all_to_all | solution.py:118
  37.4 3.9 %collective-permute-start.3 = (bf16[128,1024]{1,0:T(8,128)(2,1)S(1)}, bf16[128,1024]{1,0:T(8,128)(2,1)S(1)}, u32[]{:S(2)}, u32[]{:S(2)}) collective-permute-start(bf16[128,1024]{1,0:T(8,128)(2,1)S(1)} %reshape.22.refs_3_), channel_id=1, source_target_pairs={{0,14},{2,0},{4,2},{6,4},{8,6},{10,8},{12,10},{14,12},{1,15},{3,1}... | collective-permute-start | bytes 786440 | tf_op jit(solution)/shard_map/ppermute | solution.py:38
  41.3 10.4 %collective-permute-done.2.refs_4_ = bf16[128,1024]{1,0:T(8,128)(2,1)S(1)} collective-permute-done((bf16[128,1024]{1,0:T(8,128)(2,1)S(1)}, bf16[128,1024]{1,0:T(8,128)(2,1)S(1)}, u32[]{:S(2)}, u32[]{:S(2)}) %collective-permute-start.2) | collective-permute-done | bytes 262176 | tf_op jit(solution)/shard_map/ppermute | solution.py:35
  51.7 3.1 %collective-permute-start.4 = (bf16[128,1024]{1,0:T(8,128)(2,1)S(1)}, bf16[128,1024]{1,0:T(8,128)(2,1)S(1)}, u32[]{:S(2)}, u32[]{:S(2)}) collective-permute-start(bf16[128,1024]{1,0:T(8,128)(2,1)S(1)} %collective-permute-done.2.refs_4_), channel_id=1, source_target_pairs={{0,2},{2,4},{4,6},{6,8},{8,10},{10,12},{12,14},{14,0},{1,3},{3,5},... | collective-permute-start | bytes 786440 | tf_op jit(solution)/shard_map/ppermute | solution.py:35
  54.9 2.7 %collective-permute-start.5 = (bf16[128,1024]{1,0:T(8,128)(2,1)S(1)}, bf16[128,1024]{1,0:T(8,128)(2,1)S(1)}, u32[]{:S(2)}, u32[]{:S(2)}) collective-permute-start(bf16[128,1024]{1,0:T(8,128)(2,1)S(1)} %collective-permute-done.3.refs_5_), channel_id=1, source_target_pairs={{0,14},{2,0},{4,2},{6,4},{8,6},{10,8},{12,10},{14,12},{1,15},{3,1}... | collective-permute-start | bytes 786440 | tf_op jit(solution)/shard_map/ppermute | solution.py:38
  57.5 5.4 %collective-permute-done.4.refs_6_ = bf16[128,1024]{1,0:T(8,128)(2,1)S(1)} collective-permute-done((bf16[128,1024]{1,0:T(8,128)(2,1)S(1)}, bf16[128,1024]{1,0:T(8,128)(2,1)S(1)}, u32[]{:S(2)}, u32[]{:S(2)}) %collective-permute-start.4) | collective-permute-done | bytes 262176 | tf_op jit(solution)/shard_map/ppermute | solution.py:35
  62.9 4.5 %collective-permute-start.6 = (bf16[128,1024]{1,0:T(8,128)(2,1)S(1)}, bf16[128,1024]{1,0:T(8,128)(2,1)S(1)}, u32[]{:S(2)}, u32[]{:S(2)}) collective-permute-start(bf16[128,1024]{1,0:T(8,128)(2,1)S(1)} %collective-permute-done.4.refs_6_), channel_id=1, source_target_pairs={{0,2},{2,4},{4,6},{6,8},{8,10},{10,12},{12,14},{14,0},{1,3},{3,5},... | collective-permute-start | bytes 786440 | tf_op jit(solution)/shard_map/ppermute | solution.py:35
  69.4 3.5 %collective-permute-done.6.refs_8_ = bf16[128,1024]{1,0:T(8,128)(2,1)S(1)} collective-permute-done((bf16[128,1024]{1,0:T(8,128)(2,1)S(1)}, bf16[128,1024]{1,0:T(8,128)(2,1)S(1)}, u32[]{:S(2)}, u32[]{:S(2)}) %collective-permute-start.6) | collective-permute-done | bytes 262176 | tf_op jit(solution)/shard_map/ppermute | solution.py:35
  72.9 5.6 %collective-permute-start.8 = (bf16[128,1024]{1,0:T(8,128)(2,1)S(1)}, bf16[128,1024]{1,0:T(8,128)(2,1)S(1)}, u32[]{:S(2)}, u32[]{:S(2)}) collective-permute-start(bf16[128,1024]{1,0:T(8,128)(2,1)S(1)} %collective-permute-done.6.refs_8_), channel_id=1, source_target_pairs={{0,2},{2,4},{4,6},{6,8},{8,10},{10,12},{12,14},{14,0},{1,3},{3,5},... | collective-permute-start | bytes 786440 | tf_op jit(solution)/shard_map/ppermute | solution.py:35
  80.1 3.5 %collective-permute-start.1 = (bf16[64,1024]{1,0:T(8,128)(2,1)}, bf16[64,1024]{1,0:T(8,128)(2,1)S(1)}, u32[]{:S(2)}, u32[]{:S(2)}) collective-permute-start(bf16[64,1024]{1,0:T(8,128)(2,1)} %get-tuple-element.16), channel_id=1, source_target_pairs={{0,1},{1,0},{2,3},{3,2},{4,5},{5,4},{6,7},{7,6},{8,9},{9,8},{10,11... | collective-permute-start | bytes 393224 | tf_op jit(solution)/shard_map/ppermute | solution.py:28
  92.3 3.5 %collective-permute-start.9 = (bf16[128,1024]{1,0:T(8,128)(2,1)S(1)}, bf16[128,1024]{1,0:T(8,128)(2,1)S(1)}, u32[]{:S(2)}, u32[]{:S(2)}) collective-permute-start(bf16[128,1024]{1,0:T(8,128)(2,1)S(1)} %shard_map.93.mine), channel_id=1, source_target_pairs={{0,1},{1,0},{2,3},{3,2},{4,5},{5,4},{6,7},{7,6},{8,9},{9,8},{10,11... | collective-permute-start | bytes 786440 | tf_op jit(solution)/shard_map/ppermute | solution.py:28
  96.0 2.3 %collective-permute-start.11 = (f32[2,64,1024]{2,1,0:T(8,128)S(1)}, f32[2,64,1024]{2,1,0:T(8,128)S(1)}, u32[]{:S(2)}, u32[]{:S(2)}) collective-permute-start(f32[2,64,1024]{2,1,0:T(8,128)S(1)} %multiply_subtract_fusion.base_own), channel_id=1, source_target_pairs={{0,1},{1,0},{2,3},{3,2},{4,5},{5,4},{6,7},{7,6},{8,9},{9,8},{10,11... | collective-permute-start | bytes 1572872 | tf_op jit(solution)/shard_map/ppermute | solution.py:28
  98.3 2.3 %fusion.2 = (f32[2]{0:T(128)S(1)}, f32[2,64,1024]{2,1,0:T(8,128)}) fusion(bf16[1,64,1024]{2,1,0:T(8,128)(2,1)S(1)} %get-tuple-element.19, bf16[1,64,1024]{2,1,0:T(8,128)(2,1)} %bitcast.5, pred[]{:T(512)S(6)} %eq.3, f32[2,64,1024]{2,1,0:T(8,128)} %param.11), kind=kLoop, calls=%fused_computation.12 | loop fusion | flops 1572862 | bytes 1310729 | tf_op jit(solution)/shard_map/reduce_sum | solution.py:133
  106.6 4.2 %collective-permute-start.10 = (bf16[2,128,512]{2,1,0:T(8,128)(2,1)S(1)}, bf16[2,128,512]{2,1,0:T(8,128)(2,1)S(1)}, u32[]{:S(2)}, u32[]{:S(2)}) collective-permute-start(bf16[2,128,512]{2,1,0:T(8,128)(2,1)S(1)} %get-tuple-element.10.mine), channel_id=1, source_target_pairs={{0,1},{1,0},{2,3},{3,2},{4,5},{5,4},{6,7},{7,6},{8,9},{9,8},{10,11... | collective-permute-start | bytes 786440 | tf_op jit(solution)/shard_map/ppermute | solution.py:28
  110.8 6.0 %all-to-all-start.1 = ((f32[16,8,128]{2,1,0:T(8,128)}), f32[16,8,128]{2,1,0:T(8,128)S(1)}, u32[]{:S(2)}, u32[]{:S(2)}) async-start(f32[16,8,128]{2,1,0:T(8,128)} %get-tuple-element.9), calls=%async_computation.1 | async-start | bytes 131072 | tf_op jit(solution)/shard_map/all_to_all | solution.py:162
  116.8 6.8 %all-to-all-done.1.sums = f32[16,8,128]{2,1,0:T(8,128)S(1)} async-done(((f32[16,8,128]{2,1,0:T(8,128)}), f32[16,8,128]{2,1,0:T(8,128)S(1)}, u32[]{:S(2)}, u32[]{:S(2)}) %all-to-all-start.1) | async-done | bytes 65568 | tf_op jit(solution)/shard_map/all_to_all | solution.py:162
  125.5 4.7 %collective-permute-start.12 = (bf16[2,128,1024]{2,1,0:T(8,128)(2,1)S(1)}, bf16[2,128,1024]{2,1,0:T(8,128)(2,1)S(1)}, u32[]{:S(2)}, u32[]{:S(2)}) collective-permute-start(bf16[2,128,1024]{2,1,0:T(8,128)(2,1)S(1)} %get-tuple-element.11), channel_id=1, source_target_pairs={{0,2},{2,4},{4,6},{6,8},{8,10},{10,12},{12,14},{14,0},{1,3},{3,5},... | collective-permute-start | bytes 1572872 | tf_op jit(solution)/shard_map/ppermute | solution.py:189
  132.1 8.4 %collective-permute-done.12 = bf16[2,128,1024]{2,1,0:T(8,128)(2,1)S(1)} collective-permute-done((bf16[2,128,1024]{2,1,0:T(8,128)(2,1)S(1)}, bf16[2,128,1024]{2,1,0:T(8,128)(2,1)S(1)}, u32[]{:S(2)}, u32[]{:S(2)}) %collective-permute-start.12) | collective-permute-done | bytes 524320 | tf_op jit(solution)/shard_map/ppermute | solution.py:189
  140.5 5.2 %collective-permute-start.14 = (bf16[2,128,1024]{2,1,0:T(8,128)(2,1)S(1)}, bf16[2,128,1024]{2,1,0:T(8,128)(2,1)S(1)}, u32[]{:S(2)}, u32[]{:S(2)}) collective-permute-start(bf16[2,128,1024]{2,1,0:T(8,128)(2,1)S(1)} %collective-permute-done.12), channel_id=1, source_target_pairs={{0,2},{2,4},{4,6},{6,8},{8,10},{10,12},{12,14},{14,0},{1,3},{3,5},... | collective-permute-start | bytes 1572872 | tf_op jit(solution)/shard_map/ppermute | solution.py:189
  148.7 8.2 %collective-permute-done.14 = bf16[2,128,1024]{2,1,0:T(8,128)(2,1)S(1)} collective-permute-done((bf16[2,128,1024]{2,1,0:T(8,128)(2,1)S(1)}, bf16[2,128,1024]{2,1,0:T(8,128)(2,1)S(1)}, u32[]{:S(2)}, u32[]{:S(2)}) %collective-permute-start.14) | collective-permute-done | bytes 524320 | tf_op jit(solution)/shard_map/ppermute | solution.py:189
  156.9 5.6 %collective-permute-start.16 = (bf16[2,128,1024]{2,1,0:T(8,128)(2,1)S(1)}, bf16[2,128,1024]{2,1,0:T(8,128)(2,1)S(1)}, u32[]{:S(2)}, u32[]{:S(2)}) collective-permute-start(bf16[2,128,1024]{2,1,0:T(8,128)(2,1)S(1)} %collective-permute-done.14), channel_id=1, source_target_pairs={{0,2},{2,4},{4,6},{6,8},{8,10},{10,12},{12,14},{14,0},{1,3},{3,5},... | collective-permute-start | bytes 1572872 | tf_op jit(solution)/shard_map/ppermute | solution.py:189
  165.1 6.8 %collective-permute-done.16 = bf16[2,128,1024]{2,1,0:T(8,128)(2,1)S(1)} collective-permute-done((bf16[2,128,1024]{2,1,0:T(8,128)(2,1)S(1)}, bf16[2,128,1024]{2,1,0:T(8,128)(2,1)S(1)}, u32[]{:S(2)}, u32[]{:S(2)}) %collective-permute-start.16) | collective-permute-done | bytes 524320 | tf_op jit(solution)/shard_map/ppermute | solution.py:189
  172.0 5.6 %collective-permute-start.18 = (bf16[1,128,1024]{2,1,0:T(8,128)(2,1)S(1)}, bf16[1,128,1024]{2,1,0:T(8,128)(2,1)S(1)}, u32[]{:S(2)}, u32[]{:S(2)}) collective-permute-start(bf16[1,128,1024]{2,1,0:T(8,128)(2,1)S(1)} %slice.8), channel_id=1, source_target_pairs={{0,2},{2,4},{4,6},{6,8},{8,10},{10,12},{12,14},{14,0},{1,3},{3,5},... | collective-permute-start | bytes 786440 | tf_op jit(solution)/shard_map/ppermute | solution.py:193
  181.5 5.9 %collective-permute-done.19 = bf16[1,128,1024]{2,1,0:T(8,128)(2,1)S(1)} collective-permute-done((bf16[1,128,1024]{2,1,0:T(8,128)(2,1)S(1)}, bf16[1,128,1024]{2,1,0:T(8,128)(2,1)S(1)}, u32[]{:S(2)}, u32[]{:S(2)}) %collective-permute-start.19) | collective-permute-done | bytes 262176 | tf_op jit(solution)/shard_map/ppermute | solution.py:194
  (59 shorter events, 37.2 us)
Async XLA Ops:
  7.2 88.7 %copy-start.2 = (f32[2,64,1024]{2,1,0:T(8,128)S(1)}, f32[2,64,1024]{2,1,0:T(8,128)}, u32[]{:S(2)}) copy-start(f32[2,64,1024]{2,1,0:T(8,128)} %momentum.1) | copy-start | bytes 1572868
  7.2 88.7 %copy-start.1 = (f32[2,64,1024]{2,1,0:T(8,128)S(1)}, f32[2,64,1024]{2,1,0:T(8,128)}, u32[]{:S(2)}) copy-start(f32[2,64,1024]{2,1,0:T(8,128)} %master.1) | copy-start | bytes 1572868
  7.2 95.7 %all-gather.3.cloned.1.call-start = ((), (), s32[]{:S(2)}) async-start(), calls=%async_computation.2 | async-start | bytes 2359296 | tf_op jit(solution)/shard_map/all_gather | solution.py:116
  35.5 16.2 %collective-permute-start.2 = (bf16[128,1024]{1,0:T(8,128)(2,1)S(1)}, bf16[128,1024]{1,0:T(8,128)(2,1)S(1)}, u32[]{:S(2)}, u32[]{:S(2)}) collective-permute-start(bf16[128,1024]{1,0:T(8,128)(2,1)S(1)} %reshape.22.refs_3_), channel_id=1, source_target_pairs={{0,2},{2,4},{4,6},{6,8},{8,10},{10,12},{12,14},{14,0},{1,3},{3,5},... | collective-permute-start | bytes 786440 | tf_op jit(solution)/shard_map/ppermute | solution.py:35
  37.4 17.4 %collective-permute-start.3 = (bf16[128,1024]{1,0:T(8,128)(2,1)S(1)}, bf16[128,1024]{1,0:T(8,128)(2,1)S(1)}, u32[]{:S(2)}, u32[]{:S(2)}) collective-permute-start(bf16[128,1024]{1,0:T(8,128)(2,1)S(1)} %reshape.22.refs_3_), channel_id=1, source_target_pairs={{0,14},{2,0},{4,2},{6,4},{8,6},{10,8},{12,10},{14,12},{1,15},{3,1}... | collective-permute-start | bytes 786440 | tf_op jit(solution)/shard_map/ppermute | solution.py:38
  51.7 11.2 %collective-permute-start.4 = (bf16[128,1024]{1,0:T(8,128)(2,1)S(1)}, bf16[128,1024]{1,0:T(8,128)(2,1)S(1)}, u32[]{:S(2)}, u32[]{:S(2)}) collective-permute-start(bf16[128,1024]{1,0:T(8,128)(2,1)S(1)} %collective-permute-done.2.refs_4_), channel_id=1, source_target_pairs={{0,2},{2,4},{4,6},{6,8},{8,10},{10,12},{12,14},{14,0},{1,3},{3,5},... | collective-permute-start | bytes 786440 | tf_op jit(solution)/shard_map/ppermute | solution.py:35
  54.9 12.6 %collective-permute-start.5 = (bf16[128,1024]{1,0:T(8,128)(2,1)S(1)}, bf16[128,1024]{1,0:T(8,128)(2,1)S(1)}, u32[]{:S(2)}, u32[]{:S(2)}) collective-permute-start(bf16[128,1024]{1,0:T(8,128)(2,1)S(1)} %collective-permute-done.3.refs_5_), channel_id=1, source_target_pairs={{0,14},{2,0},{4,2},{6,4},{8,6},{10,8},{12,10},{14,12},{1,15},{3,1}... | collective-permute-start | bytes 786440 | tf_op jit(solution)/shard_map/ppermute | solution.py:38
  62.9 9.9 %collective-permute-start.6 = (bf16[128,1024]{1,0:T(8,128)(2,1)S(1)}, bf16[128,1024]{1,0:T(8,128)(2,1)S(1)}, u32[]{:S(2)}, u32[]{:S(2)}) collective-permute-start(bf16[128,1024]{1,0:T(8,128)(2,1)S(1)} %collective-permute-done.4.refs_6_), channel_id=1, source_target_pairs={{0,2},{2,4},{4,6},{6,8},{8,10},{10,12},{12,14},{14,0},{1,3},{3,5},... | collective-permute-start | bytes 786440 | tf_op jit(solution)/shard_map/ppermute | solution.py:35
  67.4 22.0 %collective-permute-start.7 = (bf16[128,1024]{1,0:T(8,128)(2,1)S(1)}, bf16[128,1024]{1,0:T(8,128)(2,1)S(1)}, u32[]{:S(2)}, u32[]{:S(2)}) collective-permute-start(bf16[128,1024]{1,0:T(8,128)(2,1)S(1)} %collective-permute-done.5.refs_7_), channel_id=1, source_target_pairs={{0,14},{2,0},{4,2},{6,4},{8,6},{10,8},{12,10},{14,12},{1,15},{3,1}... | collective-permute-start | bytes 786440 | tf_op jit(solution)/shard_map/ppermute | solution.py:38
  72.9 16.6 %collective-permute-start.8 = (bf16[128,1024]{1,0:T(8,128)(2,1)S(1)}, bf16[128,1024]{1,0:T(8,128)(2,1)S(1)}, u32[]{:S(2)}, u32[]{:S(2)}) collective-permute-start(bf16[128,1024]{1,0:T(8,128)(2,1)S(1)} %collective-permute-done.6.refs_8_), channel_id=1, source_target_pairs={{0,2},{2,4},{4,6},{6,8},{8,10},{10,12},{12,14},{14,0},{1,3},{3,5},... | collective-permute-start | bytes 786440 | tf_op jit(solution)/shard_map/ppermute | solution.py:35
  80.1 9.3 %collective-permute-start.1 = (bf16[64,1024]{1,0:T(8,128)(2,1)}, bf16[64,1024]{1,0:T(8,128)(2,1)S(1)}, u32[]{:S(2)}, u32[]{:S(2)}) collective-permute-start(bf16[64,1024]{1,0:T(8,128)(2,1)} %get-tuple-element.16), channel_id=1, source_target_pairs={{0,1},{1,0},{2,3},{3,2},{4,5},{5,4},{6,7},{7,6},{8,9},{9,8},{10,11... | collective-permute-start | bytes 393224 | tf_op jit(solution)/shard_map/ppermute | solution.py:28
  87.1 11.2 %collective-permute-start = (bf16[64,1024]{1,0:T(8,128)(2,1)}, bf16[64,1024]{1,0:T(8,128)(2,1)}, u32[]{:S(2)}, u32[]{:S(2)}) collective-permute-start(bf16[64,1024]{1,0:T(8,128)(2,1)} %get-tuple-element.18), channel_id=1, source_target_pairs={{0,1},{1,0},{2,3},{3,2},{4,5},{5,4},{6,7},{7,6},{8,9},{9,8},{10,11... | collective-permute-start | bytes 393224 | tf_op jit(solution)/shard_map/ppermute | solution.py:28
  92.3 10.5 %collective-permute-start.9 = (bf16[128,1024]{1,0:T(8,128)(2,1)S(1)}, bf16[128,1024]{1,0:T(8,128)(2,1)S(1)}, u32[]{:S(2)}, u32[]{:S(2)}) collective-permute-start(bf16[128,1024]{1,0:T(8,128)(2,1)S(1)} %shard_map.93.mine), channel_id=1, source_target_pairs={{0,1},{1,0},{2,3},{3,2},{4,5},{5,4},{6,7},{7,6},{8,9},{9,8},{10,11... | collective-permute-start | bytes 786440 | tf_op jit(solution)/shard_map/ppermute | solution.py:28
  96.0 20.8 %collective-permute-start.11 = (f32[2,64,1024]{2,1,0:T(8,128)S(1)}, f32[2,64,1024]{2,1,0:T(8,128)S(1)}, u32[]{:S(2)}, u32[]{:S(2)}) collective-permute-start(f32[2,64,1024]{2,1,0:T(8,128)S(1)} %multiply_subtract_fusion.base_own), channel_id=1, source_target_pairs={{0,1},{1,0},{2,3},{3,2},{4,5},{5,4},{6,7},{7,6},{8,9},{9,8},{10,11... | collective-permute-start | bytes 1572872 | tf_op jit(solution)/shard_map/ppermute | solution.py:28
  106.6 17.0 %collective-permute-start.10 = (bf16[2,128,512]{2,1,0:T(8,128)(2,1)S(1)}, bf16[2,128,512]{2,1,0:T(8,128)(2,1)S(1)}, u32[]{:S(2)}, u32[]{:S(2)}) collective-permute-start(bf16[2,128,512]{2,1,0:T(8,128)(2,1)S(1)} %get-tuple-element.10.mine), channel_id=1, source_target_pairs={{0,1},{1,0},{2,3},{3,2},{4,5},{5,4},{6,7},{7,6},{8,9},{9,8},{10,11... | collective-permute-start | bytes 786440 | tf_op jit(solution)/shard_map/ppermute | solution.py:28
  110.8 12.8 %all-to-all-start.1 = ((f32[16,8,128]{2,1,0:T(8,128)}), f32[16,8,128]{2,1,0:T(8,128)S(1)}, u32[]{:S(2)}, u32[]{:S(2)}) async-start(f32[16,8,128]{2,1,0:T(8,128)} %get-tuple-element.9), calls=%async_computation.1 | async-start | bytes 131072 | tf_op jit(solution)/shard_map/all_to_all | solution.py:162
  125.5 15.0 %collective-permute-start.12 = (bf16[2,128,1024]{2,1,0:T(8,128)(2,1)S(1)}, bf16[2,128,1024]{2,1,0:T(8,128)(2,1)S(1)}, u32[]{:S(2)}, u32[]{:S(2)}) collective-permute-start(bf16[2,128,1024]{2,1,0:T(8,128)(2,1)S(1)} %get-tuple-element.11), channel_id=1, source_target_pairs={{0,2},{2,4},{4,6},{6,8},{8,10},{10,12},{12,14},{14,0},{1,3},{3,5},... | collective-permute-start | bytes 1572872 | tf_op jit(solution)/shard_map/ppermute | solution.py:189
  130.2 15.9 %collective-permute-start.13 = (bf16[2,128,1024]{2,1,0:T(8,128)(2,1)S(1)}, bf16[2,128,1024]{2,1,0:T(8,128)(2,1)S(1)}, u32[]{:S(2)}, u32[]{:S(2)}) collective-permute-start(bf16[2,128,1024]{2,1,0:T(8,128)(2,1)S(1)} %get-tuple-element.11), channel_id=1, source_target_pairs={{0,14},{2,0},{4,2},{6,4},{8,6},{10,8},{12,10},{14,12},{1,15},{3,1}... | collective-permute-start | bytes 1572872 | tf_op jit(solution)/shard_map/ppermute | solution.py:190
  140.5 16.3 %collective-permute-start.14 = (bf16[2,128,1024]{2,1,0:T(8,128)(2,1)S(1)}, bf16[2,128,1024]{2,1,0:T(8,128)(2,1)S(1)}, u32[]{:S(2)}, u32[]{:S(2)}) collective-permute-start(bf16[2,128,1024]{2,1,0:T(8,128)(2,1)S(1)} %collective-permute-done.12), channel_id=1, source_target_pairs={{0,2},{2,4},{4,6},{6,8},{8,10},{10,12},{12,14},{14,0},{1,3},{3,5},... | collective-permute-start | bytes 1572872 | tf_op jit(solution)/shard_map/ppermute | solution.py:189
  146.1 17.0 %collective-permute-start.15 = (bf16[2,128,1024]{2,1,0:T(8,128)(2,1)S(1)}, bf16[2,128,1024]{2,1,0:T(8,128)(2,1)S(1)}, u32[]{:S(2)}, u32[]{:S(2)}) collective-permute-start(bf16[2,128,1024]{2,1,0:T(8,128)(2,1)S(1)} %collective-permute-done.13), channel_id=1, source_target_pairs={{0,14},{2,0},{4,2},{6,4},{8,6},{10,8},{12,10},{14,12},{1,15},{3,1}... | collective-permute-start | bytes 1572872 | tf_op jit(solution)/shard_map/ppermute | solution.py:190
  156.9 15.1 %collective-permute-start.16 = (bf16[2,128,1024]{2,1,0:T(8,128)(2,1)S(1)}, bf16[2,128,1024]{2,1,0:T(8,128)(2,1)S(1)}, u32[]{:S(2)}, u32[]{:S(2)}) collective-permute-start(bf16[2,128,1024]{2,1,0:T(8,128)(2,1)S(1)} %collective-permute-done.14), channel_id=1, source_target_pairs={{0,2},{2,4},{4,6},{6,8},{8,10},{10,12},{12,14},{14,0},{1,3},{3,5},... | collective-permute-start | bytes 1572872 | tf_op jit(solution)/shard_map/ppermute | solution.py:189
  163.1 14.9 %collective-permute-start.17 = (bf16[2,128,1024]{2,1,0:T(8,128)(2,1)S(1)}, bf16[2,128,1024]{2,1,0:T(8,128)(2,1)S(1)}, u32[]{:S(2)}, u32[]{:S(2)}) collective-permute-start(bf16[2,128,1024]{2,1,0:T(8,128)(2,1)S(1)} %collective-permute-done.15), channel_id=1, source_target_pairs={{0,14},{2,0},{4,2},{6,4},{8,6},{10,8},{12,10},{14,12},{1,15},{3,1}... | collective-permute-start | bytes 1572872 | tf_op jit(solution)/shard_map/ppermute | solution.py:190
  172.0 9.5 %collective-permute-start.18 = (bf16[1,128,1024]{2,1,0:T(8,128)(2,1)S(1)}, bf16[1,128,1024]{2,1,0:T(8,128)(2,1)S(1)}, u32[]{:S(2)}, u32[]{:S(2)}) collective-permute-start(bf16[1,128,1024]{2,1,0:T(8,128)(2,1)S(1)} %slice.8), channel_id=1, source_target_pairs={{0,2},{2,4},{4,6},{6,8},{8,10},{10,12},{12,14},{14,0},{1,3},{3,5},... | collective-permute-start | bytes 786440 | tf_op jit(solution)/shard_map/ppermute | solution.py:193
  177.9 9.5 %collective-permute-start.19 = (bf16[1,128,1024]{2,1,0:T(8,128)(2,1)S(1)}, bf16[1,128,1024]{2,1,0:T(8,128)(2,1)S(1)}, u32[]{:S(2)}, u32[]{:S(2)}) collective-permute-start(bf16[1,128,1024]{2,1,0:T(8,128)(2,1)S(1)} %slice.9), channel_id=1, source_target_pairs={{0,14},{2,0},{4,2},{6,4},{8,6},{10,8},{12,10},{14,12},{1,15},{3,1}... | collective-permute-start | bytes 786440 | tf_op jit(solution)/shard_map/ppermute | solution.py:194
  (5 other events, 6.0 us)
Sparse Core Ops, SparseCore 0:
  10.1 50.7 all-gather.2

commit v3 on v2

v3 whole, which is shorter than its diff:
```python
import jax
import jax.numpy as jnp
from jax import lax
from jax.experimental import pallas as pl
from jax.experimental.pallas import tpu as pltpu
from jax.sharding import Mesh, PartitionSpec as P

momentum_decay = 0.9
second_decay = 0.95
learn_rate = 0.05
adam_eps = 1e-08
norm_eps = 1e-06

Y = 8
OWNERS = ("z", "xh", "c")
GROUP = ("y", "xl")
SWAP = [(0, 1), (1, 0)]
VMEM = pl.BlockSpec(memory_space=pltpu.VMEM)
PARAMS = pltpu.CompilerParams(vmem_limit_bytes=24 * 1024 * 1024)


def swap(x):
    return lax.ppermute(x, "xl", SWAP)


def hop(x, way):
    pairs = [(c * Y + i, c * Y + (i + (way if c == 0 else -way)) % Y) for c in range(2) for i in range(Y)]
    return lax.ppermute(x, ("c", "y"), pairs)


def after(x, *others):
    return lax.optimization_barrier((x, *others))


def left_kernel(distances, place, left_own, left_other, *refs):
    chunks, out = refs[:-1], refs[-1]
    rows = left_own.shape[1]
    depth = chunks[0].shape[0]
    half = place[1]
    total = jnp.zeros((2 * rows, out.shape[1]), jnp.float32)
    for distance, chunk in zip(distances, chunks):
        at = lax.rem(place[0] + place[2] * distance + Y, Y)
        at = pl.multiple_of(at * depth, depth)
        columns = jnp.concatenate(
            [left_own[half, :, pl.ds(at, depth)], left_other[half, :, pl.ds(at, depth)]], axis=0
        )
        total += jnp.dot(columns, chunk[...], preferred_element_type=jnp.float32)
    rounded = total.astype(jnp.bfloat16)
    out[pl.ds(pl.multiple_of(half * rows, rows), rows), :] = rounded[:rows]
    out[pl.ds(pl.multiple_of((1 - half) * rows, rows), rows), :] = rounded[rows:]


def adam_kernel(place, mine, theirs, second, new_second, squares):
    rows = second.shape[1]
    half = place[1]
    own = pl.ds(pl.multiple_of(half * rows, rows), rows)
    ours, others = mine[own, :], theirs[own, :]
    for block in range(2):
        grad = jnp.where(half == block, ours, others).astype(jnp.float32)
        moment = second_decay * second[block] + (1.0 - second_decay) * grad * grad
        new_second[block] = moment
        step = grad / (jnp.sqrt(moment) + adam_eps)
        squares[block] = jnp.full(squares.shape[1:], jnp.sum(step * step), jnp.float32)


def right_kernel(place, mine, theirs, right, adam, out, sums):
    depth = right.shape[0] * right.shape[2]
    half = place[1]
    squares = []
    for block in range(2):
        left_grad = jnp.where(half == block, mine[...], theirs[...])
        columns = right[:, block].reshape(depth, right.shape[3])
        part = lax.dot_general(
            left_grad, columns, (((1,), (1,)), ((), ())), preferred_element_type=jnp.float32
        )
        out[block] = part.astype(jnp.bfloat16)
        squares.append(jnp.sum(part * part))
    row = lax.broadcasted_iota(jnp.int32, (8, 128), 0)
    values = jnp.where(row < 2, jnp.where(row == 0, squares[0], squares[1]), jnp.where(row == 2, adam[0][:1], adam[1][:1]))
    for i in range(sums.shape[0]):
        sums[i] = values


def update_kernel(place, sums, mine, theirs, base_own, base_other, master, momentum, params, new_master, new_momentum, precond):
    rows, width = master.shape[1:]
    half = place[1]
    total = jnp.sum(sums[...], axis=0)
    own = pl.ds(pl.multiple_of(half * rows, rows), rows)
    other = pl.ds(pl.multiple_of((1 - half) * rows, rows), rows)
    low = lax.broadcasted_iota(jnp.int32, (2 * rows, 128), 1) < 64
    for block in range(2):
        graft = jnp.sqrt(total[2 + block : 3 + block] / (total[block : block + 1] + norm_eps))
        for i in range(Y // 2):
            cut = slice(i * 128, (i + 1) * 128)
            a = mine[block, :, cut].astype(jnp.float32)
            b = theirs[block, :, cut].astype(jnp.float32)
            first = jnp.where(half == 0, a, b)
            second = jnp.where(half == 0, b, a)
            even = jnp.where(low, first, pltpu.roll(second, 64, 1))
            odd = jnp.where(low, pltpu.roll(first, 64, 1), second)
            precond[:, 2 * i * 128 : (2 * i + 1) * 128] = graft * even
            precond[:, (2 * i + 1) * 128 : (2 * i + 2) * 128] = graft * odd
        ours = precond[own, :]
        moved = momentum_decay * momentum[block] + ours
        new_momentum[block] = moved
        new_master[block] = master[block] - learn_rate * moved
        params[block, own, :] = (base_own[block] - learn_rate * ours).astype(jnp.bfloat16)
        params[block, other, :] = (base_other[block] - learn_rate * precond[other, :]).astype(jnp.bfloat16)


def call(kernel, out_shape, operands, flops=0, scratch_shapes=()):
    leaves = jax.tree.leaves(out_shape)
    moved = sum(x.size * x.dtype.itemsize for x in (*operands, *leaves))
    return pl.pallas_call(
        kernel,
        out_shape=out_shape,
        in_specs=[pl.BlockSpec(memory_space=pltpu.SMEM)] + [VMEM] * (len(operands) - 1),
        out_specs=jax.tree.map(lambda _: VMEM, out_shape),
        scratch_shapes=scratch_shapes,
        compiler_params=PARAMS,
        cost_estimate=pl.CostEstimate(flops=flops, bytes_accessed=moved, transcendentals=0),
    )(*operands)


def on_device(grad, left_root, right_root, master, momentum, second):
    y = lax.axis_index("y")
    half = lax.axis_index("xl")
    sign = 1 - 2 * lax.axis_index("c")
    place = jnp.stack([y, half, sign])
    _, rows, width = master.shape
    shape = jax.ShapeDtypeStruct
    f32, bf16 = jnp.float32, jnp.bfloat16

    right = lax.all_gather(right_root, "y", axis=0, tiled=False)

    spread = lax.all_to_all(grad, OWNERS + ("xl",), split_axis=0, concat_axis=1, tiled=True)
    pair = spread.reshape(-1, 2, grad.shape[1], width).swapaxes(0, 1).reshape(2 * rows, width)

    up1, down1 = hop(pair, 1), hop(pair, -1)
    base = master - (learn_rate * momentum_decay) * momentum
    up1, left, base = after(up1, left_root, base)
    left_other, base_other, pair_other = swap(left), swap(base), swap(pair)
    up2, down2 = hop(up1, 1), hop(down1, -1)
    up2, left_other = after(up2, left_other)
    up3, down3 = hop(up2, 1), hop(down2, -1)
    up3, down3, pair_other, base_other, right = after(up3, down3, pair_other, base_other, right)
    new_second, squares = call(
        adam_kernel,
        (shape(second.shape, f32), shape((2, 8, 128), f32)),
        (place, pair, pair_other, second),
    )
    up4 = hop(up3, 1)
    up4, squares = after(up4, squares)
    chunks = (pair, up1, down1, up2, down2, up3, down3, up4)
    distances = (0, -1, 1, -2, 2, -3, 3, -4)

    flops = 4 * rows * width * width
    left_grad = call(
        lambda *refs: left_kernel(distances, *refs),
        shape((2 * rows, width), bf16),
        (place, left_root, left_other, *chunks),
        flops,
    )
    part, sums = call(
        right_kernel,
        (shape((2, 2 * rows, width // 2), bf16), shape((2 * Y, 8, 128), f32)),
        (place, left_grad, swap(left_grad), right, squares),
        flops,
    )
    part_other = swap(part)
    sums = lax.all_to_all(sums, GROUP, split_axis=0, concat_axis=0, tiled=True)

    both, new_master, new_momentum = call(
        update_kernel,
        (shape((2, 2 * rows, width), bf16), shape(master.shape, f32), shape(master.shape, f32)),
        (place, sums, part, part_other, base, base_other, master, momentum),
        scratch_shapes=[pltpu.VMEM((2 * rows, width), f32)],
    )

    params = jnp.zeros((2, Y, 2 * rows, width), bf16)

    def put(params, chunk, block, distance):
        at = lax.rem(y + sign * distance + Y, Y)
        return lax.dynamic_update_slice(params, chunk[:, None], (block, at, 0, 0))

    params = put(params, both, 0, 0)
    up = down = both
    for step in range(1, 4):
        up, down = hop(up, 1), hop(down, -1)
        params = put(params, up, 0, -step)
        params = put(params, down, 0, step)
    params = put(params, hop(up[:1], 1), 0, 4)
    params = put(params, hop(down[1:], -1), 1, 4)
    params = params.reshape(2, 2 * Y * rows, width)
    return (params, new_master, new_momentum, new_second)


def solution(mesh):
    split = Mesh(mesh.devices.reshape(8, 2, 2, 8, 2), OWNERS + GROUP)
    state = P(OWNERS, GROUP, None)
    return jax.shard_map(
        on_device,
        mesh=split,
        in_specs=(P(None, GROUP + OWNERS, None),) + (state,) * 5,
        out_specs=(P(OWNERS, None, None), state, state, state),
        check_vma=False,
    )
```

time: 197 us -> 204 us (1.036); the launches traced: 196 us -> 201 us
  blocking collectives: 26.6 us -> 39.8 us
  starting transfers between devices: 74.3 us -> 61.8 us
  local copies, waits for them, and re-layouts: 12.2 us -> 18.4 us
  waiting for transfers between devices: 61 us -> 57.9 us
    all_to_all x0 -> x1, blocking collectives: none -> 13.2 us  [on_device(): sums = lax.all_to_all(sums, GROUP, split_axis=0, concat_axis=0, tiled=True)]
    ppermute x5, waiting for transfers between devices: 2.24 us -> 13.9 us  [swap(): return lax.ppermute(x, 'xl', SWAP)]
    unnamed x14 -> x48, local copies, waits for them, and re-layouts: 5.95 us -> 17.2 us
    ppermute x15, waiting for transfers between devices: 51.3 us -> 43.3 us  [hop(): return lax.ppermute(x, ('c', 'y'), pairs)]
    all_to_all x1 -> x0, waiting for transfers between devices: 6.77 us -> none  [on_device(): sums = lax.all_to_all(sums, GROUP, split_axis=0, concat_axis=0, tiled=True)]
    all_to_all x1 -> x0, starting transfers between devices: 6 us -> none  [on_device(): sums = lax.all_to_all(sums, GROUP, split_axis=0, concat_axis=0, tiled=True)]
    ppermute x15, starting transfers between devices: 52.4 us -> 48.7 us  [hop(): return lax.ppermute(x, ('c', 'y'), pairs)]
    squeeze x2 -> x0, local copies, waits for them, and re-layouts: 3.29 us -> none  [pick(): return lax.dynamic_index_in_dim(x, index, 0, keepdims=False)]
  transfers between devices with their start and end apart: 22 -> 21, of which waited for: 13 -> 11; matrix products, arithmetic and copies ran while one was open for 4% -> 1% of each run, Pallas kernels for 2% -> 1%
where the time goes in v3:
time: 204 us; the launch traced here: 201 us
  starting transfers between devices  61.8 us (30%)
  waiting for transfers between devices  57.9 us (28%)
  blocking collectives  39.8 us (20%)
  local copies, waits for them, and re-layouts  18.4 us (9%)
  between operations  14.5 us (7%)
  Pallas kernels  6.91 us (3%)
    ppermute x15, starting transfers between devices, hop(): return lax.ppermute(x, ('c', 'y'), pairs)  48.7 us
    ppermute x15, waiting for transfers between devices, hop(): return lax.ppermute(x, ('c', 'y'), pairs)  43.3 us
    all_to_all x1, blocking collectives, on_device(): lax.all_to_all(grad, OWNERS + ('xl',), split_axis=0, concat_axis=1, tiled...  26.6 us
    unnamed x48, local copies, waits for them, and re-layouts  17.2 us
    ppermute x5, waiting for transfers between devices, swap(): return lax.ppermute(x, 'xl', SWAP)  13.9 us
    all_to_all x1, blocking collectives, on_device(): sums = lax.all_to_all(sums, GROUP, split_axis=0, concat_axis=0, tiled=True)  13.2 us
    ppermute x5, starting transfers between devices, swap(): return lax.ppermute(x, 'xl', SWAP)  13 us
    pallas_call x4, Pallas kernels, call(): pl.pallas_call(kernel, out_shape=out_shape, in_specs=[pl.BlockSpec(memory...  6.91 us
  transfers between devices with their start and end apart: 21, of which 11 were waited for; matrix products, arithmetic and copies ran while one was open for 1% of the time, Pallas kernels for 1%

profile of v3, /device:TPU:56, one launch (start us, length us, event | category | flops | bytes accessed | tf_op | source)
XLA Modules:
  0.0 200.6 jit_solution(2267679548010391279)
XLA Ops:
  7.9 26.6 %all_to_all.14 = bf16[64,2,1024]{2,1,0:T(2,128)(2,1)S(1)} all-to-all(bf16[64,2,1024]{2,1,0:T(2,128)(2,1)} %param.6), channel_id=1, replica_groups=mesh['z'=8,'xh'=2,'c'=2,'y'=8,'xl'=2] {'z','xh','c','xl'}, dimensions={0} | all-to-all | bytes 524288 | tf_op jit(solution)/shard_map/all_to_all | solution.py:136
  36.8 3.9 %collective-permute-start.3 = (bf16[128,1024]{1,0:T(8,128)(2,1)S(1)}, bf16[128,1024]{1,0:T(8,128)(2,1)S(1)}, u32[]{:S(2)}, u32[]{:S(2)}) collective-permute-start(bf16[128,1024]{1,0:T(8,128)(2,1)S(1)} %reshape.22.mine.refs_3_), channel_id=1, source_target_pairs={{0,14},{2,0},{4,2},{6,4},{8,6},{10,8},{12,10},{14,12},{16,18},{18,... | collective-permute-start | bytes 786440 | tf_op jit(solution)/shard_map/ppermute | solution.py:28
  42.1 8.4 %collective-permute-done.refs_4_ = bf16[128,1024]{1,0:T(8,128)(2,1)S(1)} collective-permute-done((bf16[128,1024]{1,0:T(8,128)(2,1)S(1)}, bf16[128,1024]{1,0:T(8,128)(2,1)S(1)}, u32[]{:S(2)}, u32[]{:S(2)}) %collective-permute-start) | collective-permute-done | bytes 262176 | tf_op jit(solution)/shard_map/ppermute | solution.py:28
  53.0 3.0 %collective-permute-start.2 = (bf16[2,64,1024]{2,1,0:T(8,128)(2,1)}, bf16[2,64,1024]{2,1,0:T(8,128)(2,1)S(1)}, u32[]{:S(2)}, u32[]{:S(2)}) collective-permute-start(bf16[2,64,1024]{2,1,0:T(8,128)(2,1)} %refs_1_.1), channel_id=1, source_target_pairs={{0,1},{1,0},{2,3},{3,2},{4,5},{5,4},{6,7},{7,6},{8,9},{9,8},{10,11... | collective-permute-start | bytes 786440 | tf_op jit(solution)/shard_map/ppermute | solution.py:23
  56.0 2.9 %collective-permute-start.8 = (f32[2,64,1024]{2,1,0:T(8,128)S(1)}, f32[2,64,1024]{2,1,0:T(8,128)S(1)}, u32[]{:S(2)}, u32[]{:S(2)}) collective-permute-start(f32[2,64,1024]{2,1,0:T(8,128)S(1)} %multiply_subtract_fusion.base_own), channel_id=1, source_target_pairs={{0,1},{1,0},{2,3},{3,2},{4,5},{5,4},{6,7},{7,6},{8,9},{9,8},{10,11... | collective-permute-start | bytes 1572872 | tf_op jit(solution)/shard_map/ppermute | solution.py:23
  59.7 3.9 %collective-permute-start.4 = (bf16[128,1024]{1,0:T(8,128)(2,1)S(1)}, bf16[128,1024]{1,0:T(8,128)(2,1)S(1)}, u32[]{:S(2)}, u32[]{:S(2)}) collective-permute-start(bf16[128,1024]{1,0:T(8,128)(2,1)S(1)} %collective-permute-done.3.refs_5_), channel_id=1, source_target_pairs={{0,14},{2,0},{4,2},{6,4},{8,6},{10,8},{12,10},{14,12},{16,18},{18,... | collective-permute-start | bytes 786440 | tf_op jit(solution)/shard_map/ppermute | solution.py:28
  64.3 2.5 %collective-permute-start.7 = (bf16[128,1024]{1,0:T(8,128)(2,1)S(1)}, bf16[128,1024]{1,0:T(8,128)(2,1)S(1)}, u32[]{:S(2)}, u32[]{:S(2)}) collective-permute-start(bf16[128,1024]{1,0:T(8,128)(2,1)S(1)} %reshape.22.mine.refs_3_), channel_id=1, source_target_pairs={{0,1},{1,0},{2,3},{3,2},{4,5},{5,4},{6,7},{7,6},{8,9},{9,8},{10,11... | collective-permute-start | bytes 786440 | tf_op jit(solution)/shard_map/ppermute | solution.py:23
  67.5 3.6 %collective-permute-start.5 = (bf16[128,1024]{1,0:T(8,128)(2,1)S(1)}, bf16[128,1024]{1,0:T(8,128)(2,1)}, u32[]{:S(2)}, u32[]{:S(2)}) collective-permute-start(bf16[128,1024]{1,0:T(8,128)(2,1)S(1)} %collective-permute-done.1.refs_6_), channel_id=1, source_target_pairs={{0,2},{2,4},{4,6},{6,8},{8,10},{10,12},{12,14},{14,0},{16,30},{18,... | collective-permute-start | bytes 786440 | tf_op jit(solution)/shard_map/ppermute | solution.py:28
  71.9 2.2 %collective-permute-start.6 = (bf16[128,1024]{1,0:T(8,128)(2,1)S(1)}, bf16[128,1024]{1,0:T(8,128)(2,1)S(1)}, u32[]{:S(2)}, u32[]{:S(2)}) collective-permute-start(bf16[128,1024]{1,0:T(8,128)(2,1)S(1)} %collective-permute-done.4.refs_7_), channel_id=1, source_target_pairs={{0,14},{2,0},{4,2},{6,4},{8,6},{10,8},{12,10},{14,12},{16,18},{18,... | collective-permute-start | bytes 786440 | tf_op jit(solution)/shard_map/ppermute | solution.py:28
  74.7 6.3 %collective-permute-done.7.theirs = bf16[128,1024]{1,0:T(8,128)(2,1)S(1)} collective-permute-done((bf16[128,1024]{1,0:T(8,128)(2,1)S(1)}, bf16[128,1024]{1,0:T(8,128)(2,1)S(1)}, u32[]{:S(2)}, u32[]{:S(2)}) %collective-permute-start.7) | collective-permute-done | bytes 262176 | tf_op jit(solution)/shard_map/ppermute | solution.py:23
  89.1 2.9 %collective-permute-done.9.refs_10_ = bf16[128,1024]{1,0:T(8,128)(2,1)} collective-permute-done((bf16[128,1024]{1,0:T(8,128)(2,1)}, bf16[128,1024]{1,0:T(8,128)(2,1)}, u32[]{:S(2)}, u32[]{:S(2)}) %collective-permute-start.9) | collective-permute-done | bytes 262176 | tf_op jit(solution)/shard_map/ppermute | solution.py:28
  100.3 2.5 %collective-permute-start.10 = (bf16[128,1024]{1,0:T(8,128)(2,1)S(1)}, bf16[128,1024]{1,0:T(8,128)(2,1)S(1)}, u32[]{:S(2)}, u32[]{:S(2)}) collective-permute-start(bf16[128,1024]{1,0:T(8,128)(2,1)S(1)} %shard_map.94.mine), channel_id=1, source_target_pairs={{0,1},{1,0},{2,3},{3,2},{4,5},{5,4},{6,7},{7,6},{8,9},{9,8},{10,11... | collective-permute-start | bytes 786440 | tf_op jit(solution)/shard_map/ppermute | solution.py:23
  102.9 7.6 %collective-permute-done.10.theirs = bf16[128,1024]{1,0:T(8,128)(2,1)S(1)} collective-permute-done((bf16[128,1024]{1,0:T(8,128)(2,1)S(1)}, bf16[128,1024]{1,0:T(8,128)(2,1)S(1)}, u32[]{:S(2)}, u32[]{:S(2)}) %collective-permute-start.10) | collective-permute-done | bytes 262176 | tf_op jit(solution)/shard_map/ppermute | solution.py:23
  112.0 2.2 %collective-permute-start.11 = (bf16[2,128,512]{2,1,0:T(8,128)(2,1)S(1)}, bf16[2,128,512]{2,1,0:T(8,128)(2,1)S(1)}, u32[]{:S(2)}, u32[]{:S(2)}) collective-permute-start(bf16[2,128,512]{2,1,0:T(8,128)(2,1)S(1)} %get-tuple-element.36.mine), channel_id=1, source_target_pairs={{0,1},{1,0},{2,3},{3,2},{4,5},{5,4},{6,7},{7,6},{8,9},{9,8},{10,11... | collective-permute-start | bytes 786440 | tf_op jit(solution)/shard_map/ppermute | solution.py:23
  114.2 13.2 %all_to_all.15.sums = f32[16,8,128]{2,1,0:T(8,128)S(1)} all-to-all(f32[16,8,128]{2,1,0:T(8,128)S(1)} %get-tuple-element.35), channel_id=1, replica_groups=mesh['z'=8,'xh'=2,'c'=2,'y'=8,'xl'=2] {'y','xl'}, dimensions={0} | all-to-all | bytes 131072 | tf_op jit(solution)/shard_map/all_to_all | solution.py:171
  129.5 4.6 %collective-permute-start.12 = (bf16[2,128,1024]{2,1,0:T(8,128)(2,1)S(1)}, bf16[2,128,1024]{2,1,0:T(8,128)(2,1)S(1)}, u32[]{:S(2)}, u32[]{:S(2)}) collective-permute-start(bf16[2,128,1024]{2,1,0:T(8,128)(2,1)S(1)} %get-tuple-element.38), channel_id=1, source_target_pairs={{0,2},{2,4},{4,6},{6,8},{8,10},{10,12},{12,14},{14,0},{16,30},{18,... | collective-permute-start | bytes 1572872 | tf_op jit(solution)/shard_map/ppermute | solution.py:28
  136.1 7.6 %collective-permute-done.12 = bf16[2,128,1024]{2,1,0:T(8,128)(2,1)S(1)} collective-permute-done((bf16[2,128,1024]{2,1,0:T(8,128)(2,1)S(1)}, bf16[2,128,1024]{2,1,0:T(8,128)(2,1)S(1)}, u32[]{:S(2)}, u32[]{:S(2)}) %collective-permute-start.12) | collective-permute-done | bytes 524320 | tf_op jit(solution)/shard_map/ppermute | solution.py:28
  143.7 5.6 %collective-permute-start.14 = (bf16[2,128,1024]{2,1,0:T(8,128)(2,1)S(1)}, bf16[2,128,1024]{2,1,0:T(8,128)(2,1)S(1)}, u32[]{:S(2)}, u32[]{:S(2)}) collective-permute-start(bf16[2,128,1024]{2,1,0:T(8,128)(2,1)S(1)} %collective-permute-done.12), channel_id=1, source_target_pairs={{0,2},{2,4},{4,6},{6,8},{8,10},{10,12},{12,14},{14,0},{16,30},{18,... | collective-permute-start | bytes 1572872 | tf_op jit(solution)/shard_map/ppermute | solution.py:28
  153.0 4.9 %collective-permute-done.14 = bf16[2,128,1024]{2,1,0:T(8,128)(2,1)S(1)} collective-permute-done((bf16[2,128,1024]{2,1,0:T(8,128)(2,1)S(1)}, bf16[2,128,1024]{2,1,0:T(8,128)(2,1)S(1)}, u32[]{:S(2)}, u32[]{:S(2)}) %collective-permute-start.14) | collective-permute-done | bytes 524320 | tf_op jit(solution)/shard_map/ppermute | solution.py:28
  157.9 5.6 %collective-permute-start.16 = (bf16[2,128,1024]{2,1,0:T(8,128)(2,1)S(1)}, bf16[2,128,1024]{2,1,0:T(8,128)(2,1)S(1)}, u32[]{:S(2)}, u32[]{:S(2)}) collective-permute-start(bf16[2,128,1024]{2,1,0:T(8,128)(2,1)S(1)} %collective-permute-done.14), channel_id=1, source_target_pairs={{0,2},{2,4},{4,6},{6,8},{8,10},{10,12},{12,14},{14,0},{16,30},{18,... | collective-permute-start | bytes 1572872 | tf_op jit(solution)/shard_map/ppermute | solution.py:28
  163.5 4.3 %collective-permute-done.15 = bf16[2,128,1024]{2,1,0:T(8,128)(2,1)S(1)} collective-permute-done((bf16[2,128,1024]{2,1,0:T(8,128)(2,1)S(1)}, bf16[2,128,1024]{2,1,0:T(8,128)(2,1)S(1)}, u32[]{:S(2)}, u32[]{:S(2)}) %collective-permute-start.15) | collective-permute-done | bytes 524320 | tf_op jit(solution)/shard_map/ppermute | solution.py:28
  171.2 5.6 %collective-permute-start.18 = (bf16[1,128,1024]{2,1,0:T(8,128)(2,1)S(1)}, bf16[1,128,1024]{2,1,0:T(8,128)(2,1)S(1)}, u32[]{:S(2)}, u32[]{:S(2)}) collective-permute-start(bf16[1,128,1024]{2,1,0:T(8,128)(2,1)S(1)} %slice.8), channel_id=1, source_target_pairs={{0,2},{2,4},{4,6},{6,8},{8,10},{10,12},{12,14},{14,0},{16,30},{18,... | collective-permute-start | bytes 786440 | tf_op jit(solution)/shard_map/ppermute | solution.py:28
  176.9 5.4 %collective-permute-done.17 = bf16[2,128,1024]{2,1,0:T(8,128)(2,1)S(1)} collective-permute-done((bf16[2,128,1024]{2,1,0:T(8,128)(2,1)S(1)}, bf16[2,128,1024]{2,1,0:T(8,128)(2,1)S(1)}, u32[]{:S(2)}, u32[]{:S(2)}) %collective-permute-start.17) | collective-permute-done | bytes 524320 | tf_op jit(solution)/shard_map/ppermute | solution.py:28
  184.3 7.4 %collective-permute-done.19 = bf16[1,128,1024]{2,1,0:T(8,128)(2,1)S(1)} collective-permute-done((bf16[1,128,1024]{2,1,0:T(8,128)(2,1)S(1)}, bf16[1,128,1024]{2,1,0:T(8,128)(2,1)S(1)}, u32[]{:S(2)}, u32[]{:S(2)}) %collective-permute-start.19) | collective-permute-done | bytes 262176 | tf_op jit(solution)/shard_map/ppermute | solution.py:28
  (89 shorter events, 43.5 us)
Async XLA Ops:
  7.2 76.1 %all-gather.3.cloned.1.call-start = ((), (), s32[]{:S(2)}) async-start(), calls=%async_computation.2 | async-start | bytes 2359296 | tf_op jit(solution)/shard_map/all_gather | solution.py:134
  34.8 92.7 %copy-start.1 = (f32[2,64,1024]{2,1,0:T(8,128)S(1)}, f32[2,64,1024]{2,1,0:T(8,128)}, u32[]{:S(2)}) copy-start(f32[2,64,1024]{2,1,0:T(8,128)} %master.1) | copy-start | bytes 1572868
  34.8 92.7 %copy-start.2 = (f32[2,64,1024]{2,1,0:T(8,128)S(1)}, f32[2,64,1024]{2,1,0:T(8,128)}, u32[]{:S(2)}) copy-start(f32[2,64,1024]{2,1,0:T(8,128)} %momentum.1) | copy-start | bytes 1572868
  34.8 15.6 %collective-permute-start = (bf16[128,1024]{1,0:T(8,128)(2,1)S(1)}, bf16[128,1024]{1,0:T(8,128)(2,1)S(1)}, u32[]{:S(2)}, u32[]{:S(2)}) collective-permute-start(bf16[128,1024]{1,0:T(8,128)(2,1)S(1)} %reshape.22.mine.refs_3_), channel_id=1, source_target_pairs={{0,2},{2,4},{4,6},{6,8},{8,10},{10,12},{12,14},{14,0},{16,30},{18,... | collective-permute-start | bytes 786440 | tf_op jit(solution)/shard_map/ppermute | solution.py:28
  36.8 22.8 %collective-permute-start.3 = (bf16[128,1024]{1,0:T(8,128)(2,1)S(1)}, bf16[128,1024]{1,0:T(8,128)(2,1)S(1)}, u32[]{:S(2)}, u32[]{:S(2)}) collective-permute-start(bf16[128,1024]{1,0:T(8,128)(2,1)S(1)} %reshape.22.mine.refs_3_), channel_id=1, source_target_pairs={{0,14},{2,0},{4,2},{6,4},{8,6},{10,8},{12,10},{14,12},{16,18},{18,... | collective-permute-start | bytes 786440 | tf_op jit(solution)/shard_map/ppermute | solution.py:28
  50.4 16.4 %collective-permute-start.1 = (bf16[128,1024]{1,0:T(8,128)(2,1)S(1)}, bf16[128,1024]{1,0:T(8,128)(2,1)S(1)}, u32[]{:S(2)}, u32[]{:S(2)}) collective-permute-start(bf16[128,1024]{1,0:T(8,128)(2,1)S(1)} %collective-permute-done.refs_4_), channel_id=1, source_target_pairs={{0,2},{2,4},{4,6},{6,8},{8,10},{10,12},{12,14},{14,0},{16,30},{18,... | collective-permute-start | bytes 786440 | tf_op jit(solution)/shard_map/ppermute | solution.py:28
  53.0 13.7 %collective-permute-start.2 = (bf16[2,64,1024]{2,1,0:T(8,128)(2,1)}, bf16[2,64,1024]{2,1,0:T(8,128)(2,1)S(1)}, u32[]{:S(2)}, u32[]{:S(2)}) collective-permute-start(bf16[2,64,1024]{2,1,0:T(8,128)(2,1)} %refs_1_.1), channel_id=1, source_target_pairs={{0,1},{1,0},{2,3},{3,2},{4,5},{5,4},{6,7},{7,6},{8,9},{9,8},{10,11... | collective-permute-start | bytes 786440 | tf_op jit(solution)/shard_map/ppermute | solution.py:23
  56.0 25.7 %collective-permute-start.8 = (f32[2,64,1024]{2,1,0:T(8,128)S(1)}, f32[2,64,1024]{2,1,0:T(8,128)S(1)}, u32[]{:S(2)}, u32[]{:S(2)}) collective-permute-start(f32[2,64,1024]{2,1,0:T(8,128)S(1)} %multiply_subtract_fusion.base_own), channel_id=1, source_target_pairs={{0,1},{1,0},{2,3},{3,2},{4,5},{5,4},{6,7},{7,6},{8,9},{9,8},{10,11... | collective-permute-start | bytes 1572872 | tf_op jit(solution)/shard_map/ppermute | solution.py:23
  59.7 12.2 %collective-permute-start.4 = (bf16[128,1024]{1,0:T(8,128)(2,1)S(1)}, bf16[128,1024]{1,0:T(8,128)(2,1)S(1)}, u32[]{:S(2)}, u32[]{:S(2)}) collective-permute-start(bf16[128,1024]{1,0:T(8,128)(2,1)S(1)} %collective-permute-done.3.refs_5_), channel_id=1, source_target_pairs={{0,14},{2,0},{4,2},{6,4},{8,6},{10,8},{12,10},{14,12},{16,18},{18,... | collective-permute-start | bytes 786440 | tf_op jit(solution)/shard_map/ppermute | solution.py:28
  64.3 16.7 %collective-permute-start.7 = (bf16[128,1024]{1,0:T(8,128)(2,1)S(1)}, bf16[128,1024]{1,0:T(8,128)(2,1)S(1)}, u32[]{:S(2)}, u32[]{:S(2)}) collective-permute-start(bf16[128,1024]{1,0:T(8,128)(2,1)S(1)} %reshape.22.mine.refs_3_), channel_id=1, source_target_pairs={{0,1},{1,0},{2,3},{3,2},{4,5},{5,4},{6,7},{7,6},{8,9},{9,8},{10,11... | collective-permute-start | bytes 786440 | tf_op jit(solution)/shard_map/ppermute | solution.py:23
  67.5 15.0 %collective-permute-start.5 = (bf16[128,1024]{1,0:T(8,128)(2,1)S(1)}, bf16[128,1024]{1,0:T(8,128)(2,1)}, u32[]{:S(2)}, u32[]{:S(2)}) collective-permute-start(bf16[128,1024]{1,0:T(8,128)(2,1)S(1)} %collective-permute-done.1.refs_6_), channel_id=1, source_target_pairs={{0,2},{2,4},{4,6},{6,8},{8,10},{10,12},{12,14},{14,0},{16,30},{18,... | collective-permute-start | bytes 786440 | tf_op jit(solution)/shard_map/ppermute | solution.py:28
  71.9 10.7 %collective-permute-start.6 = (bf16[128,1024]{1,0:T(8,128)(2,1)S(1)}, bf16[128,1024]{1,0:T(8,128)(2,1)S(1)}, u32[]{:S(2)}, u32[]{:S(2)}) collective-permute-start(bf16[128,1024]{1,0:T(8,128)(2,1)S(1)} %collective-permute-done.4.refs_7_), channel_id=1, source_target_pairs={{0,14},{2,0},{4,2},{6,4},{8,6},{10,8},{12,10},{14,12},{16,18},{18,... | collective-permute-start | bytes 786440 | tf_op jit(solution)/shard_map/ppermute | solution.py:28
  83.2 8.7 %collective-permute-start.9 = (bf16[128,1024]{1,0:T(8,128)(2,1)}, bf16[128,1024]{1,0:T(8,128)(2,1)}, u32[]{:S(2)}, u32[]{:S(2)}) collective-permute-start(bf16[128,1024]{1,0:T(8,128)(2,1)} %collective-permute-done.5.refs_8_), channel_id=1, source_target_pairs={{0,2},{2,4},{4,6},{6,8},{8,10},{10,12},{12,14},{14,0},{16,30},{18,... | collective-permute-start | bytes 786440 | tf_op jit(solution)/shard_map/ppermute | solution.py:28
  85.3 42.2 %copy-start.4 = (f32[2,64,1024]{2,1,0:T(8,128)S(1)}, f32[2,64,1024]{2,1,0:T(8,128)}, u32[]{:S(2)}) copy-start(f32[2,64,1024]{2,1,0:T(8,128)} %copy-done.3) | copy-start | bytes 1572868
  100.3 10.1 %collective-permute-start.10 = (bf16[128,1024]{1,0:T(8,128)(2,1)S(1)}, bf16[128,1024]{1,0:T(8,128)(2,1)S(1)}, u32[]{:S(2)}, u32[]{:S(2)}) collective-permute-start(bf16[128,1024]{1,0:T(8,128)(2,1)S(1)} %shard_map.94.mine), channel_id=1, source_target_pairs={{0,1},{1,0},{2,3},{3,2},{4,5},{5,4},{6,7},{7,6},{8,9},{9,8},{10,11... | collective-permute-start | bytes 786440 | tf_op jit(solution)/shard_map/ppermute | solution.py:23
  112.0 15.5 %collective-permute-start.11 = (bf16[2,128,512]{2,1,0:T(8,128)(2,1)S(1)}, bf16[2,128,512]{2,1,0:T(8,128)(2,1)S(1)}, u32[]{:S(2)}, u32[]{:S(2)}) collective-permute-start(bf16[2,128,512]{2,1,0:T(8,128)(2,1)S(1)} %get-tuple-element.36.mine), channel_id=1, source_target_pairs={{0,1},{1,0},{2,3},{3,2},{4,5},{5,4},{6,7},{7,6},{8,9},{9,8},{10,11... | collective-permute-start | bytes 786440 | tf_op jit(solution)/shard_map/ppermute | solution.py:23
  129.5 14.2 %collective-permute-start.12 = (bf16[2,128,1024]{2,1,0:T(8,128)(2,1)S(1)}, bf16[2,128,1024]{2,1,0:T(8,128)(2,1)S(1)}, u32[]{:S(2)}, u32[]{:S(2)}) collective-permute-start(bf16[2,128,1024]{2,1,0:T(8,128)(2,1)S(1)} %get-tuple-element.38), channel_id=1, source_target_pairs={{0,2},{2,4},{4,6},{6,8},{8,10},{10,12},{12,14},{14,0},{16,30},{18,... | collective-permute-start | bytes 1572872 | tf_op jit(solution)/shard_map/ppermute | solution.py:28
  134.1 16.2 %collective-permute-start.13 = (bf16[2,128,1024]{2,1,0:T(8,128)(2,1)S(1)}, bf16[2,128,1024]{2,1,0:T(8,128)(2,1)S(1)}, u32[]{:S(2)}, u32[]{:S(2)}) collective-permute-start(bf16[2,128,1024]{2,1,0:T(8,128)(2,1)S(1)} %get-tuple-element.38), channel_id=1, source_target_pairs={{0,14},{2,0},{4,2},{6,4},{8,6},{10,8},{12,10},{14,12},{16,18},{18,... | collective-permute-start | bytes 1572872 | tf_op jit(solution)/shard_map/ppermute | solution.py:28
  143.7 14.2 %collective-permute-start.14 = (bf16[2,128,1024]{2,1,0:T(8,128)(2,1)S(1)}, bf16[2,128,1024]{2,1,0:T(8,128)(2,1)S(1)}, u32[]{:S(2)}, u32[]{:S(2)}) collective-permute-start(bf16[2,128,1024]{2,1,0:T(8,128)(2,1)S(1)} %collective-permute-done.12), channel_id=1, source_target_pairs={{0,2},{2,4},{4,6},{6,8},{8,10},{10,12},{12,14},{14,0},{16,30},{18,... | collective-permute-start | bytes 1572872 | tf_op jit(solution)/shard_map/ppermute | solution.py:28
  150.4 17.4 %collective-permute-start.15 = (bf16[2,128,1024]{2,1,0:T(8,128)(2,1)S(1)}, bf16[2,128,1024]{2,1,0:T(8,128)(2,1)S(1)}, u32[]{:S(2)}, u32[]{:S(2)}) collective-permute-start(bf16[2,128,1024]{2,1,0:T(8,128)(2,1)S(1)} %collective-permute-done.13), channel_id=1, source_target_pairs={{0,14},{2,0},{4,2},{6,4},{8,6},{10,8},{12,10},{14,12},{16,18},{18,... | collective-permute-start | bytes 1572872 | tf_op jit(solution)/shard_map/ppermute | solution.py:28
  157.9 13.3 %collective-permute-start.16 = (bf16[2,128,1024]{2,1,0:T(8,128)(2,1)S(1)}, bf16[2,128,1024]{2,1,0:T(8,128)(2,1)S(1)}, u32[]{:S(2)}, u32[]{:S(2)}) collective-permute-start(bf16[2,128,1024]{2,1,0:T(8,128)(2,1)S(1)} %collective-permute-done.14), channel_id=1, source_target_pairs={{0,2},{2,4},{4,6},{6,8},{8,10},{10,12},{12,14},{14,0},{16,30},{18,... | collective-permute-start | bytes 1572872 | tf_op jit(solution)/shard_map/ppermute | solution.py:28
  167.8 14.4 %collective-permute-start.17 = (bf16[2,128,1024]{2,1,0:T(8,128)(2,1)S(1)}, bf16[2,128,1024]{2,1,0:T(8,128)(2,1)S(1)}, u32[]{:S(2)}, u32[]{:S(2)}) collective-permute-start(bf16[2,128,1024]{2,1,0:T(8,128)(2,1)S(1)} %collective-permute-done.15), channel_id=1, source_target_pairs={{0,14},{2,0},{4,2},{6,4},{8,6},{10,8},{12,10},{14,12},{16,18},{18,... | collective-permute-start | bytes 1572872 | tf_op jit(solution)/shard_map/ppermute | solution.py:28
  171.2 13.0 %collective-permute-start.18 = (bf16[1,128,1024]{2,1,0:T(8,128)(2,1)S(1)}, bf16[1,128,1024]{2,1,0:T(8,128)(2,1)S(1)}, u32[]{:S(2)}, u32[]{:S(2)}) collective-permute-start(bf16[1,128,1024]{2,1,0:T(8,128)(2,1)S(1)} %slice.8), channel_id=1, source_target_pairs={{0,2},{2,4},{4,6},{6,8},{8,10},{10,12},{12,14},{14,0},{16,30},{18,... | collective-permute-start | bytes 786440 | tf_op jit(solution)/shard_map/ppermute | solution.py:28
  182.3 9.5 %collective-permute-start.19 = (bf16[1,128,1024]{2,1,0:T(8,128)(2,1)S(1)}, bf16[1,128,1024]{2,1,0:T(8,128)(2,1)S(1)}, u32[]{:S(2)}, u32[]{:S(2)}) collective-permute-start(bf16[1,128,1024]{2,1,0:T(8,128)(2,1)S(1)} %slice.9), channel_id=1, source_target_pairs={{0,14},{2,0},{4,2},{6,4},{8,6},{10,8},{12,10},{14,12},{16,18},{18,... | collective-permute-start | bytes 786440 | tf_op jit(solution)/shard_map/ppermute | solution.py:28
  (21 other events, 84.5 us)
Sparse Core Ops, SparseCore 0:
  10.1 51.0 all-gather.2

commit v4 on v3

v4 whole, which is shorter than its diff:
```python
import jax
import jax.numpy as jnp
from jax import lax
from jax.experimental import pallas as pl
from jax.experimental.pallas import tpu as pltpu
from jax.sharding import Mesh, PartitionSpec as P

momentum_decay = 0.9
second_decay = 0.95
learn_rate = 0.05
adam_eps = 1e-08
norm_eps = 1e-06

Y = 8
OWNERS = ("z", "xh", "c")
GROUP = ("y", "xl")
SWAP = [(0, 1), (1, 0)]
VMEM = pl.BlockSpec(memory_space=pltpu.VMEM)
SMEM = pl.BlockSpec(memory_space=pltpu.SMEM)
ANY = pl.BlockSpec(memory_space=pl.ANY)
PARAMS = pltpu.CompilerParams(vmem_limit_bytes=12 * 1024 * 1024)


def swap(x):
    return lax.ppermute(x, "xl", SWAP)


def hop(x, way):
    return lax.ppermute(x, "y", [(i, (i + way) % Y) for i in range(Y)])


def adam_kernel(place, mine, theirs, second, *refs):
    new_second, squares = refs[-2:]
    rows = second.shape[1]
    half = place[1]
    ours = mine[pl.ds(pl.multiple_of(half * rows, rows), rows), :]
    others = theirs[pl.ds(pl.multiple_of(half * rows, rows), rows), :]
    for block in range(2):
        grad = jnp.where(half == block, ours, others).astype(jnp.float32)
        moment = second_decay * second[block] + (1.0 - second_decay) * grad * grad
        new_second[block] = moment
        step = grad / (jnp.sqrt(moment) + adam_eps)
        squares[block] = jnp.full(squares.shape[1:], jnp.sum(step * step), jnp.float32)


def left_kernel(distances, place, left_own, swapped, *refs):
    chunks, out = refs[: len(distances)], refs[-1]
    rows = left_own.shape[1]
    depth = chunks[0].shape[0]
    half = place[1]
    total = jnp.zeros((2 * rows, out.shape[1]), jnp.float32)
    for distance, chunk in zip(distances, chunks):
        at = pl.multiple_of(lax.rem(place[0] + distance + Y, Y) * depth, depth)
        columns = jnp.concatenate(
            [left_own[half, :, pl.ds(at, depth)], swapped[:rows, pl.ds(at, depth)]], axis=0
        )
        total += jnp.dot(columns, chunk[...], preferred_element_type=jnp.float32)
    rounded = total.astype(jnp.bfloat16)
    out[pl.ds(pl.multiple_of(half * rows, rows), rows), :] = rounded[:rows]
    out[pl.ds(pl.multiple_of((1 - half) * rows, rows), rows), :] = rounded[rows:]


def right_kernel(place, left_grads, adam, right, out, sums):
    depth = right.shape[0] * right.shape[2]
    squares = []
    for block in range(2):
        columns = right[:, block].reshape(depth, right.shape[3])
        part = lax.dot_general(
            left_grads[block], columns, (((1,), (1,)), ((), ())), preferred_element_type=jnp.float32
        )
        out[block] = part.astype(jnp.bfloat16)
        squares.append(jnp.sum(part * part))
    row = lax.broadcasted_iota(jnp.int32, (8, 128), 0)
    values = jnp.where(
        row < 2, jnp.where(row == 0, squares[0], squares[1]), jnp.where(row == 2, adam[0][:1], adam[1][:1])
    )
    for i in range(sums.shape[0]):
        sums[i] = values


def grafted(place, sums, mine, theirs, block, precond):
    half = place[1]
    total = jnp.sum(sums[...], axis=0)
    graft = jnp.sqrt(total[2 + block : 3 + block] / (total[block : block + 1] + norm_eps))
    low = lax.broadcasted_iota(jnp.int32, (precond.shape[0], 128), 1) < 64
    for i in range(Y // 2):
        cut = slice(i * 128, (i + 1) * 128)
        a = mine[block, :, cut].astype(jnp.float32)
        b = theirs[block, :, cut].astype(jnp.float32)
        first = jnp.where(half == 0, a, b)
        second = jnp.where(half == 0, b, a)
        even = jnp.where(low, first, pltpu.roll(second, 64, 1))
        odd = jnp.where(low, pltpu.roll(first, 64, 1), second)
        precond[:, 2 * i * 128 : (2 * i + 1) * 128] = graft * even
        precond[:, (2 * i + 1) * 128 : (2 * i + 2) * 128] = graft * odd


def update_kernel(
    place, sums, mine, theirs, base, swapped, master, momentum, params, new_master, new_momentum, precond
):
    rows = master.shape[1]
    own = pl.ds(pl.multiple_of(place[1] * rows, rows), rows)
    other = pl.ds(pl.multiple_of((1 - place[1]) * rows, rows), rows)
    for block in range(2):
        grafted(place, sums, mine, theirs, block, precond)
        ours = precond[own, :]
        params[block, own, :] = (base[block] - learn_rate * ours).astype(jnp.bfloat16)
        high = swapped[(1 + block) * rows : (2 + block) * rows, :].astype(jnp.float32)
        low = swapped[(3 + block) * rows : (4 + block) * rows, :].astype(jnp.float32)
        params[block, other, :] = (high + low - learn_rate * precond[other, :]).astype(jnp.bfloat16)
        moved = momentum_decay * momentum[block] + ours
        new_momentum[block] = moved
        new_master[block] = master[block] - learn_rate * moved


def call(kernel, out_shape, operands, flops=0, ready=(), through=None, scratch_shapes=()):
    moved = sum(x.size * x.dtype.itemsize for x in operands)
    in_specs = [SMEM] + [VMEM] * (len(operands) - 1) + [ANY] * len(ready)
    operands, out_shape = tuple(operands) + tuple(ready), tuple(out_shape)
    out_specs = [VMEM] * len(out_shape)
    aliases = {}
    if through is not None:
        aliases = {len(operands): len(out_shape)}
        operands += (through,)
        out_shape += (jax.ShapeDtypeStruct(through.shape, through.dtype),)
        in_specs.append(ANY)
        out_specs.append(ANY)
    return pl.pallas_call(
        kernel,
        out_shape=out_shape,
        in_specs=in_specs,
        out_specs=tuple(out_specs),
        scratch_shapes=scratch_shapes,
        input_output_aliases=aliases,
        compiler_params=PARAMS,
        cost_estimate=pl.CostEstimate(flops=flops, bytes_accessed=2 * moved, transcendentals=0),
    )(*operands)


def on_device(grad, left_root, right_root, master, momentum, second):
    place = jnp.stack([lax.axis_index("y"), lax.axis_index("xl")])
    _, rows, width = master.shape
    shape = jax.ShapeDtypeStruct
    f32, bf16 = jnp.float32, jnp.bfloat16

    right = lax.all_gather(right_root, "y", axis=0, tiled=False)

    value = master - (learn_rate * momentum_decay) * momentum
    high = value.astype(bf16)
    low = (value - high.astype(f32)).astype(bf16)
    base = high.astype(f32) + low.astype(f32)
    left_away = jnp.where(place[1] == 0, left_root[1], left_root[0])
    swapped = swap(jnp.concatenate([left_away[None], high, low]).reshape(5 * rows, width))

    spread = lax.all_to_all(grad, OWNERS + ("xl",), split_axis=0, concat_axis=1, tiled=True)
    pair = spread.reshape(-1, 2, grad.shape[1], width).swapaxes(0, 1).reshape(2 * rows, width)

    up1, down1 = hop(pair, 1), hop(pair, -1)
    up2, down2 = hop(up1, 1), hop(down1, -1)
    up3, down3 = hop(up2, 1), hop(down2, -1)
    up4 = hop(up3, 1)
    chunks = (pair, up1, down1, up2, down2, up3, down3, up4)
    distances = (0, -1, 1, -2, 2, -3, 3, -4)
    new_second, squares = call(
        adam_kernel,
        (shape(second.shape, f32), shape((2, 8, 128), f32)),
        (place, pair, swap(pair), second),
        ready=(right[0, 0, :16, :128],),
    )

    flops = 4 * rows * width * width
    (left_grad,) = call(
        lambda *refs: left_kernel(distances, *refs),
        (shape((2 * rows, width), bf16),),
        (place, left_root, swapped, *chunks),
        flops,
        ready=(squares,),
    )
    part, sums = call(
        right_kernel,
        (shape((2, 2 * rows, width // 2), bf16), shape((2 * Y, 8, 128), f32)),
        (place, lax.all_gather(left_grad, "xl", axis=0, tiled=False), squares, right),
        flops,
    )
    part_other = swap(part)
    sums = lax.all_to_all(sums, GROUP, split_axis=0, concat_axis=0, tiled=True)

    both, new_master, new_momentum = call(
        update_kernel,
        (shape((2, 2 * rows, width), bf16), shape(master.shape, f32), shape(master.shape, f32)),
        (place, sums, part, part_other, base, swapped, master, momentum),
        scratch_shapes=[pltpu.VMEM((2 * rows, width), f32)],
    )

    params = jnp.zeros((2, Y, 2 * rows, width), bf16)

    def put(params, chunk, block, distance):
        at = lax.rem(place[0] + distance + Y, Y)
        return lax.dynamic_update_slice(params, chunk[:, None], (block, at, 0, 0))

    params = put(params, both, 0, 0)
    up = down = both
    for step in range(1, 4):
        up, down = hop(up, 1), hop(down, -1)
        params = put(params, up, 0, -step)
        params = put(params, down, 0, step)
    params = put(params, hop(up[:1], 1), 0, 4)
    params = put(params, hop(down[1:], -1), 1, 4)
    params = params.reshape(2, 2 * Y * rows, width)
    return (params, new_master, new_momentum, new_second)


def solution(mesh):
    split = Mesh(mesh.devices.reshape(8, 2, 2, 8, 2), OWNERS + GROUP)
    state = P(OWNERS, GROUP, None)
    return jax.shard_map(
        on_device,
        mesh=split,
        in_specs=(P(None, GROUP + OWNERS, None),) + (state,) * 5,
        out_specs=(P(OWNERS, None, None), state, state, state),
        check_vma=False,
    )
```

time: 204 us -> 182 us (0.89); the launches traced: 201 us -> 181 us
  blocking collectives: 39.8 us -> 22.2 us
  local copies, waits for them, and re-layouts: 18.4 us -> 5 us
  starting transfers between devices: 61.8 us -> 74.9 us
  waiting for transfers between devices: 57.9 us -> 53.9 us
    all_to_all x1 -> x0, blocking collectives: 26.6 us -> none  [on_device(): lax.all_to_all(grad, OWNERS + ('xl',), split_axis=0, concat_axis=1, tiled...]
    unnamed x48 -> x16, local copies, waits for them, and re-layouts: 17.2 us -> 2.98 us
    all_to_all x0 -> x1, starting transfers between devices: none -> 13.8 us  [on_device(): lax.all_to_all(grad, OWNERS + ('xl',), split_axis=0, concat_axis=1, tiled...]
    ppermute x5 -> x3, waiting for transfers between devices: 13.9 us -> 0.81 us  [swap(): return lax.ppermute(x, 'xl', SWAP)]
    all_to_all x0 -> x1, waiting for transfers between devices: none -> 12.8 us  [on_device(): lax.all_to_all(grad, OWNERS + ('xl',), split_axis=0, concat_axis=1, tiled...]
    all_gather x0 -> x1, blocking collectives: none -> 7.05 us  [on_device(): lax.all_gather(left_grad, 'xl', axis=0, tiled=False)]
    ppermute x5 -> x3, starting transfers between devices: 13 us -> 9.09 us  [swap(): return lax.ppermute(x, 'xl', SWAP)]
    ppermute x15, waiting for transfers between devices: 43.3 us -> 39.7 us  [hop(): return lax.ppermute(x, 'y', [(i, (i + way) % Y) for i in range(Y)])]
  transfers between devices with their start and end apart: 21 -> 20, of which waited for: 11 -> 14; matrix products, arithmetic and copies ran while one was open for 1% -> 3% of each run, Pallas kernels for 1% -> 1%
where the time goes in v4:
time: 182 us; the launch traced here: 181 us
  starting transfers between devices  74.9 us (41%)
  waiting for transfers between devices  53.9 us (30%)
  blocking collectives  22.2 us (12%)
  between operations  14.4 us (8%)
  Pallas kernels  7.31 us (4%)
  local copies, waits for them, and re-layouts  5 us (3%)
  other arithmetic  3.3 us (2%)
    ppermute x15, starting transfers between devices, hop(): return lax.ppermute(x, 'y', [(i, (i + way) % Y) for i in range(Y)])  52 us
    ppermute x15, waiting for transfers between devices, hop(): return lax.ppermute(x, 'y', [(i, (i + way) % Y) for i in range(Y)])  39.7 us
    all_to_all x1, blocking collectives, on_device(): sums = lax.all_to_all(sums, GROUP, split_axis=0, concat_axis=0, tiled=True)  15.2 us
    all_to_all x1, starting transfers between devices, on_device(): lax.all_to_all(grad, OWNERS + ('xl',), split_axis=0, concat_axis=1, tiled...  13.8 us
    all_to_all x1, waiting for transfers between devices, on_device(): lax.all_to_all(grad, OWNERS + ('xl',), split_axis=0, concat_axis=1, tiled...  12.8 us
    ppermute x3, starting transfers between devices, swap(): return lax.ppermute(x, 'xl', SWAP)  9.09 us
    pallas_call x4, Pallas kernels, call(): pl.pallas_call(kernel, out_shape=out_shape, in_specs=in_specs, out_specs=...  7.31 us
    all_gather x1, blocking collectives, on_device(): lax.all_gather(left_grad, 'xl', axis=0, tiled=False)  7.05 us
  transfers between devices with their start and end apart: 20, of which 14 were waited for; matrix products, arithmetic and copies ran while one was open for 3% of the time, Pallas kernels for 1%

profile of v4, /device:TPU:56, one launch (start us, length us, event | category | flops | bytes accessed | tf_op | source)
XLA Modules:
  0.0 181.1 jit_solution(14678214722464361308)
XLA Ops:
  7.9 13.8 %all-to-all-start = ((bf16[64,2,1024]{2,1,0:T(2,128)(2,1)}), bf16[64,2,1024]{2,1,0:T(2,128)(2,1)S(1)}, u32[]{:S(2)}, u32[]{:S(2)}) async-start(bf16[64,2,1024]{2,1,0:T(2,128)(2,1)} %param.6), calls=%async_computation | async-start | bytes 524288 | tf_op jit(solution)/shard_map/all_to_all | solution.py:155
  21.7 12.8 %all-to-all-done = bf16[64,2,1024]{2,1,0:T(2,128)(2,1)S(1)} async-done(((bf16[64,2,1024]{2,1,0:T(2,128)(2,1)}), bf16[64,2,1024]{2,1,0:T(2,128)(2,1)S(1)}, u32[]{:S(2)}, u32[]{:S(2)}) %all-to-all-start) | async-done | bytes 262176 | tf_op jit(solution)/shard_map/all_to_all | solution.py:155
  38.1 3.9 %collective-permute-start.2 = (bf16[128,1024]{1,0:T(8,128)(2,1)S(1)}, bf16[128,1024]{1,0:T(8,128)(2,1)}, u32[]{:S(2)}, u32[]{:S(2)}) collective-permute-start(bf16[128,1024]{1,0:T(8,128)(2,1)S(1)} %reshape.26.mine.refs_3_), channel_id=1, source_target_pairs={{0,14},{2,0},{4,2},{6,4},{8,6},{10,8},{12,10},{14,12},{1,15},{3,1}... | collective-permute-start | bytes 786440 | tf_op jit(solution)/shard_map/ppermute | solution.py:29
  42.0 9.3 %collective-permute-done.1.refs_4_ = bf16[128,1024]{1,0:T(8,128)(2,1)S(1)} collective-permute-done((bf16[128,1024]{1,0:T(8,128)(2,1)S(1)}, bf16[128,1024]{1,0:T(8,128)(2,1)S(1)}, u32[]{:S(2)}, u32[]{:S(2)}) %collective-permute-start.1) | collective-permute-done | bytes 262176 | tf_op jit(solution)/shard_map/ppermute | solution.py:29
  51.3 3.0 %collective-permute-start.3 = (bf16[128,1024]{1,0:T(8,128)(2,1)S(1)}, bf16[128,1024]{1,0:T(8,128)(2,1)}, u32[]{:S(2)}, u32[]{:S(2)}) collective-permute-start(bf16[128,1024]{1,0:T(8,128)(2,1)S(1)} %collective-permute-done.1.refs_4_), channel_id=1, source_target_pairs={{0,2},{2,4},{4,6},{6,8},{8,10},{10,12},{12,14},{14,0},{1,3},{3,5},... | collective-permute-start | bytes 786440 | tf_op jit(solution)/shard_map/ppermute | solution.py:29
  56.2 2.8 %collective-permute-start = (bf16[320,1024]{1,0:T(8,128)(2,1)}, bf16[320,1024]{1,0:T(8,128)(2,1)S(1)}, u32[]{:S(2)}, u32[]{:S(2)}) collective-permute-start(bf16[320,1024]{1,0:T(8,128)(2,1)} %bitcast.2), channel_id=1, source_target_pairs={{0,1},{1,0},{2,3},{3,2},{4,5},{5,4},{6,7},{7,6},{8,9},{9,8},{10,11... | collective-permute-start | bytes 1966088 | tf_op jit(solution)/shard_map/ppermute | solution.py:25
  59.0 2.5 %collective-permute-start.4 = (bf16[128,1024]{1,0:T(8,128)(2,1)}, bf16[128,1024]{1,0:T(8,128)(2,1)}, u32[]{:S(2)}, u32[]{:S(2)}) collective-permute-start(bf16[128,1024]{1,0:T(8,128)(2,1)} %collective-permute-done.2.refs_5_), channel_id=1, source_target_pairs={{0,14},{2,0},{4,2},{6,4},{8,6},{10,8},{12,10},{14,12},{1,15},{3,1}... | collective-permute-start | bytes 786440 | tf_op jit(solution)/shard_map/ppermute | solution.py:29
  62.9 4.4 %collective-permute-start.5 = (bf16[128,1024]{1,0:T(8,128)(2,1)}, bf16[128,1024]{1,0:T(8,128)(2,1)}, u32[]{:S(2)}, u32[]{:S(2)}) collective-permute-start(bf16[128,1024]{1,0:T(8,128)(2,1)} %collective-permute-done.3.refs_6_), channel_id=1, source_target_pairs={{0,2},{2,4},{4,6},{6,8},{8,10},{10,12},{12,14},{14,0},{1,3},{3,5},... | collective-permute-start | bytes 786440 | tf_op jit(solution)/shard_map/ppermute | solution.py:29
  67.4 3.3 %collective-permute-start.8 = (bf16[128,1024]{1,0:T(8,128)(2,1)S(1)}, bf16[128,1024]{1,0:T(8,128)(2,1)S(1)}, u32[]{:S(2)}, u32[]{:S(2)}) collective-permute-start(bf16[128,1024]{1,0:T(8,128)(2,1)S(1)} %reshape.26.mine.refs_3_), channel_id=1, source_target_pairs={{0,1},{1,0},{2,3},{3,2},{4,5},{5,4},{6,7},{7,6},{8,9},{9,8},{10,11... | collective-permute-start | bytes 786440 | tf_op jit(solution)/shard_map/ppermute | solution.py:25
  73.3 5.6 %collective-permute-start.7 = (bf16[128,1024]{1,0:T(8,128)(2,1)}, bf16[128,1024]{1,0:T(8,128)(2,1)}, u32[]{:S(2)}, u32[]{:S(2)}) collective-permute-start(bf16[128,1024]{1,0:T(8,128)(2,1)} %collective-permute-done.5.refs_8_), channel_id=1, source_target_pairs={{0,2},{2,4},{4,6},{6,8},{8,10},{10,12},{12,14},{14,0},{1,3},{3,5},... | collective-permute-start | bytes 786440 | tf_op jit(solution)/shard_map/ppermute | solution.py:29
  84.9 2.0 %shard_map.94 = bf16[128,1024]{1,0:T(8,128)(2,1)S(1)} custom-call(s32[2]{0:T(128)S(1)} %pad_add_fusion.place.refs_0_, bf16[2,64,1024]{2,1,0:T(8,128)(2,1)S(1)} %copy-done.3, bf16[320,1024]{1,0:T(8,128)(2,1)S(1)} %collective-permute-done.refs_2_.swapped, bf16[128,1024]{1,0:T(8,128)(2,1)S(1)} %reshape.26.mine.refs_3_, bf16[128,1024]{1,0:T(8,128)(2,1)S(1)} %copy-done.6, ...), custom_call_target="tpu_custom_call" | custom-call | flops 268435456 | bytes 6029328 | tf_op jit(solution)/shard_map/pallas_call | solution.py:128
  87.0 7.0 %all-gather.1 = bf16[256,1024]{1,0:T(8,128)(2,1)S(1)} all-gather(bf16[128,1024]{1,0:T(8,128)(2,1)S(1)} %shard_map.94), channel_id=3, replica_groups=mesh['z'=8,'xh'=2,'c'=2,'y'=8,'xl'=2] {'xl'}, dimensions={0}, use_global_device_ids=true | all-gather | bytes 786432 | tf_op jit(solution)/shard_map/all_gather | solution.py:182
  95.6 3.0 %collective-permute-start.9 = (bf16[2,128,512]{2,1,0:T(8,128)(2,1)S(1)}, bf16[2,128,512]{2,1,0:T(8,128)(2,1)S(1)}, u32[]{:S(2)}, u32[]{:S(2)}) collective-permute-start(bf16[2,128,512]{2,1,0:T(8,128)(2,1)S(1)} %get-tuple-element.13.mine), channel_id=1, source_target_pairs={{0,1},{1,0},{2,3},{3,2},{4,5},{5,4},{6,7},{7,6},{8,9},{9,8},{10,11... | collective-permute-start | bytes 786440 | tf_op jit(solution)/shard_map/ppermute | solution.py:25
  98.5 15.2 %all_to_all.14.sums = f32[16,8,128]{2,1,0:T(8,128)S(1)} all-to-all(f32[16,8,128]{2,1,0:T(8,128)S(1)} %get-tuple-element.12), channel_id=1, replica_groups=mesh['z'=8,'xh'=2,'c'=2,'y'=8,'xl'=2] {'y','xl'}, dimensions={0} | all-to-all | bytes 131072 | tf_op jit(solution)/shard_map/all_to_all | solution.py:186
  113.7 2.1 %shard_map.96 = (bf16[2,128,1024]{2,1,0:T(8,128)(2,1)S(1)}, f32[2,64,1024]{2,1,0:T(8,128)}, f32[2,64,1024]{2,1,0:T(8,128)}) custom-call(s32[2]{0:T(128)S(1)} %pad_add_fusion.place.refs_0_, f32[16,8,128]{2,1,0:T(8,128)S(1)} %all_to_all.14.sums, bf16[2,128,512]{2,1,0:T(8,128)(2,1)S(1)} %get-tuple-element.13.mine, ...), custom_call_target="tpu_custom_call" | custom-call | bytes 5636112 | tf_op jit(solution)/shard_map/pallas_call | solution.py:128
  115.9 4.6 %collective-permute-start.10 = (bf16[2,128,1024]{2,1,0:T(8,128)(2,1)S(1)}, bf16[2,128,1024]{2,1,0:T(8,128)(2,1)S(1)}, u32[]{:S(2)}, u32[]{:S(2)}) collective-permute-start(bf16[2,128,1024]{2,1,0:T(8,128)(2,1)S(1)} %get-tuple-element.14), channel_id=1, source_target_pairs={{0,2},{2,4},{4,6},{6,8},{8,10},{10,12},{12,14},{14,0},{1,3},{3,5},... | collective-permute-start | bytes 1572872 | tf_op jit(solution)/shard_map/ppermute | solution.py:29
  122.4 5.6 %collective-permute-done.10 = bf16[2,128,1024]{2,1,0:T(8,128)(2,1)S(1)} collective-permute-done((bf16[2,128,1024]{2,1,0:T(8,128)(2,1)S(1)}, bf16[2,128,1024]{2,1,0:T(8,128)(2,1)S(1)}, u32[]{:S(2)}, u32[]{:S(2)}) %collective-permute-start.10) | collective-permute-done | bytes 524320 | tf_op jit(solution)/shard_map/ppermute | solution.py:29
  128.0 5.2 %collective-permute-start.12 = (bf16[2,128,1024]{2,1,0:T(8,128)(2,1)S(1)}, bf16[2,128,1024]{2,1,0:T(8,128)(2,1)S(1)}, u32[]{:S(2)}, u32[]{:S(2)}) collective-permute-start(bf16[2,128,1024]{2,1,0:T(8,128)(2,1)S(1)} %collective-permute-done.10), channel_id=1, source_target_pairs={{0,2},{2,4},{4,6},{6,8},{8,10},{10,12},{12,14},{14,0},{1,3},{3,5},... | collective-permute-start | bytes 1572872 | tf_op jit(solution)/shard_map/ppermute | solution.py:29
  136.1 5.3 %collective-permute-done.12 = bf16[2,128,1024]{2,1,0:T(8,128)(2,1)S(1)} collective-permute-done((bf16[2,128,1024]{2,1,0:T(8,128)(2,1)S(1)}, bf16[2,128,1024]{2,1,0:T(8,128)(2,1)S(1)}, u32[]{:S(2)}, u32[]{:S(2)}) %collective-permute-start.12) | collective-permute-done | bytes 524320 | tf_op jit(solution)/shard_map/ppermute | solution.py:29
  141.5 5.6 %collective-permute-start.14 = (bf16[2,128,1024]{2,1,0:T(8,128)(2,1)S(1)}, bf16[2,128,1024]{2,1,0:T(8,128)(2,1)S(1)}, u32[]{:S(2)}, u32[]{:S(2)}) collective-permute-start(bf16[2,128,1024]{2,1,0:T(8,128)(2,1)S(1)} %collective-permute-done.12), channel_id=1, source_target_pairs={{0,2},{2,4},{4,6},{6,8},{8,10},{10,12},{12,14},{14,0},{1,3},{3,5},... | collective-permute-start | bytes 1572872 | tf_op jit(solution)/shard_map/ppermute | solution.py:29
  149.7 6.7 %collective-permute-done.14 = bf16[2,128,1024]{2,1,0:T(8,128)(2,1)S(1)} collective-permute-done((bf16[2,128,1024]{2,1,0:T(8,128)(2,1)S(1)}, bf16[2,128,1024]{2,1,0:T(8,128)(2,1)S(1)}, u32[]{:S(2)}, u32[]{:S(2)}) %collective-permute-start.14) | collective-permute-done | bytes 524320 | tf_op jit(solution)/shard_map/ppermute | solution.py:29
  156.4 5.6 %collective-permute-start.16 = (bf16[1,128,1024]{2,1,0:T(8,128)(2,1)S(1)}, bf16[1,128,1024]{2,1,0:T(8,128)(2,1)S(1)}, u32[]{:S(2)}, u32[]{:S(2)}) collective-permute-start(bf16[1,128,1024]{2,1,0:T(8,128)(2,1)S(1)} %slice.21), channel_id=1, source_target_pairs={{0,2},{2,4},{4,6},{6,8},{8,10},{10,12},{12,14},{14,0},{1,3},{3,5},... | collective-permute-start | bytes 786440 | tf_op jit(solution)/shard_map/ppermute | solution.py:29
  165.9 6.3 %collective-permute-done.17 = bf16[1,128,1024]{2,1,0:T(8,128)(2,1)S(1)} collective-permute-done((bf16[1,128,1024]{2,1,0:T(8,128)(2,1)S(1)}, bf16[1,128,1024]{2,1,0:T(8,128)(2,1)S(1)}, u32[]{:S(2)}, u32[]{:S(2)}) %collective-permute-start.17) | collective-permute-done | bytes 262176 | tf_op jit(solution)/shard_map/ppermute | solution.py:29
  172.3 2.0 %copy-done.7 = bf16[2,8,128,1024]{3,2,1,0:T(8,128)(2,1)} copy-done((bf16[2,8,128,1024]{3,2,1,0:T(8,128)(2,1)}, bf16[2,8,128,1024]{3,2,1,0:T(8,128)(2,1)S(1)}, u32[]{:S(2)}) %copy-start.7) | copy-done | bytes 4194328
  (58 shorter events, 28.9 us)
Async XLA Ops:
  7.2 76.8 %copy-start.3 = (bf16[2,64,1024]{2,1,0:T(8,128)(2,1)S(1)}, bf16[2,64,1024]{2,1,0:T(8,128)(2,1)}, u32[]{:S(2)}) copy-start(bf16[2,64,1024]{2,1,0:T(8,128)(2,1)} %refs_1_.1) | copy-start | bytes 786436
  7.2 73.4 %copy-start.4 = (f32[2,64,1024]{2,1,0:T(8,128)S(1)}, f32[2,64,1024]{2,1,0:T(8,128)}, u32[]{:S(2)}) copy-start(f32[2,64,1024]{2,1,0:T(8,128)} %second.1) | copy-start | bytes 1572868
  7.2 71.8 %all-gather.4.cloned.1.call-start = ((), (), s32[]{:S(2)}) async-start(), calls=%async_computation.2 | async-start | bytes 2359296 | tf_op jit(solution)/shard_map/all_gather | solution.py:146
  7.9 26.6 %all-to-all-start = ((bf16[64,2,1024]{2,1,0:T(2,128)(2,1)}), bf16[64,2,1024]{2,1,0:T(2,128)(2,1)S(1)}, u32[]{:S(2)}, u32[]{:S(2)}) async-start(bf16[64,2,1024]{2,1,0:T(2,128)(2,1)} %param.6), calls=%async_computation | async-start | bytes 524288 | tf_op jit(solution)/shard_map/all_to_all | solution.py:155
  34.8 16.5 %collective-permute-start.1 = (bf16[128,1024]{1,0:T(8,128)(2,1)S(1)}, bf16[128,1024]{1,0:T(8,128)(2,1)S(1)}, u32[]{:S(2)}, u32[]{:S(2)}) collective-permute-start(bf16[128,1024]{1,0:T(8,128)(2,1)S(1)} %reshape.26.mine.refs_3_), channel_id=1, source_target_pairs={{0,2},{2,4},{4,6},{6,8},{8,10},{10,12},{12,14},{14,0},{1,3},{3,5},... | collective-permute-start | bytes 786440 | tf_op jit(solution)/shard_map/ppermute | solution.py:29
  38.1 20.9 %collective-permute-start.2 = (bf16[128,1024]{1,0:T(8,128)(2,1)S(1)}, bf16[128,1024]{1,0:T(8,128)(2,1)}, u32[]{:S(2)}, u32[]{:S(2)}) collective-permute-start(bf16[128,1024]{1,0:T(8,128)(2,1)S(1)} %reshape.26.mine.refs_3_), channel_id=1, source_target_pairs={{0,14},{2,0},{4,2},{6,4},{8,6},{10,8},{12,10},{14,12},{1,15},{3,1}... | collective-permute-start | bytes 786440 | tf_op jit(solution)/shard_map/ppermute | solution.py:29
  51.3 11.6 %collective-permute-start.3 = (bf16[128,1024]{1,0:T(8,128)(2,1)S(1)}, bf16[128,1024]{1,0:T(8,128)(2,1)}, u32[]{:S(2)}, u32[]{:S(2)}) collective-permute-start(bf16[128,1024]{1,0:T(8,128)(2,1)S(1)} %collective-permute-done.1.refs_4_), channel_id=1, source_target_pairs={{0,2},{2,4},{4,6},{6,8},{8,10},{10,12},{12,14},{14,0},{1,3},{3,5},... | collective-permute-start | bytes 786440 | tf_op jit(solution)/shard_map/ppermute | solution.py:29
  56.2 57.6 %copy-start.1 = (f32[2,64,1024]{2,1,0:T(8,128)S(1)}, f32[2,64,1024]{2,1,0:T(8,128)}, u32[]{:S(2)}) copy-start(f32[2,64,1024]{2,1,0:T(8,128)} %master.1) | copy-start | bytes 1572868
  56.2 57.6 %copy-start.2 = (f32[2,64,1024]{2,1,0:T(8,128)S(1)}, f32[2,64,1024]{2,1,0:T(8,128)}, u32[]{:S(2)}) copy-start(f32[2,64,1024]{2,1,0:T(8,128)} %momentum.1) | copy-start | bytes 1572868
  56.2 26.1 %collective-permute-start = (bf16[320,1024]{1,0:T(8,128)(2,1)}, bf16[320,1024]{1,0:T(8,128)(2,1)S(1)}, u32[]{:S(2)}, u32[]{:S(2)}) collective-permute-start(bf16[320,1024]{1,0:T(8,128)(2,1)} %bitcast.2), channel_id=1, source_target_pairs={{0,1},{1,0},{2,3},{3,2},{4,5},{5,4},{6,7},{7,6},{8,9},{9,8},{10,11... | collective-permute-start | bytes 1966088 | tf_op jit(solution)/shard_map/ppermute | solution.py:25
  59.0 11.7 %collective-permute-start.4 = (bf16[128,1024]{1,0:T(8,128)(2,1)}, bf16[128,1024]{1,0:T(8,128)(2,1)}, u32[]{:S(2)}, u32[]{:S(2)}) collective-permute-start(bf16[128,1024]{1,0:T(8,128)(2,1)} %collective-permute-done.2.refs_5_), channel_id=1, source_target_pairs={{0,14},{2,0},{4,2},{6,4},{8,6},{10,8},{12,10},{14,12},{1,15},{3,1}... | collective-permute-start | bytes 786440 | tf_op jit(solution)/shard_map/ppermute | solution.py:29
  62.9 10.4 %collective-permute-start.5 = (bf16[128,1024]{1,0:T(8,128)(2,1)}, bf16[128,1024]{1,0:T(8,128)(2,1)}, u32[]{:S(2)}, u32[]{:S(2)}) collective-permute-start(bf16[128,1024]{1,0:T(8,128)(2,1)} %collective-permute-done.3.refs_6_), channel_id=1, source_target_pairs={{0,2},{2,4},{4,6},{6,8},{8,10},{10,12},{12,14},{14,0},{1,3},{3,5},... | collective-permute-start | bytes 786440 | tf_op jit(solution)/shard_map/ppermute | solution.py:29
  67.4 13.2 %collective-permute-start.8 = (bf16[128,1024]{1,0:T(8,128)(2,1)S(1)}, bf16[128,1024]{1,0:T(8,128)(2,1)S(1)}, u32[]{:S(2)}, u32[]{:S(2)}) collective-permute-start(bf16[128,1024]{1,0:T(8,128)(2,1)S(1)} %reshape.26.mine.refs_3_), channel_id=1, source_target_pairs={{0,1},{1,0},{2,3},{3,2},{4,5},{5,4},{6,7},{7,6},{8,9},{9,8},{10,11... | collective-permute-start | bytes 786440 | tf_op jit(solution)/shard_map/ppermute | solution.py:25
  70.7 11.5 %collective-permute-start.6 = (bf16[128,1024]{1,0:T(8,128)(2,1)}, bf16[128,1024]{1,0:T(8,128)(2,1)}, u32[]{:S(2)}, u32[]{:S(2)}) collective-permute-start(bf16[128,1024]{1,0:T(8,128)(2,1)} %collective-permute-done.4.refs_7_), channel_id=1, source_target_pairs={{0,14},{2,0},{4,2},{6,4},{8,6},{10,8},{12,10},{14,12},{1,15},{3,1}... | collective-permute-start | bytes 786440 | tf_op jit(solution)/shard_map/ppermute | solution.py:29
  73.3 10.7 %collective-permute-start.7 = (bf16[128,1024]{1,0:T(8,128)(2,1)}, bf16[128,1024]{1,0:T(8,128)(2,1)}, u32[]{:S(2)}, u32[]{:S(2)}) collective-permute-start(bf16[128,1024]{1,0:T(8,128)(2,1)} %collective-permute-done.5.refs_8_), channel_id=1, source_target_pairs={{0,2},{2,4},{4,6},{6,8},{8,10},{10,12},{12,14},{14,0},{1,3},{3,5},... | collective-permute-start | bytes 786440 | tf_op jit(solution)/shard_map/ppermute | solution.py:29
  95.6 18.2 %collective-permute-start.9 = (bf16[2,128,512]{2,1,0:T(8,128)(2,1)S(1)}, bf16[2,128,512]{2,1,0:T(8,128)(2,1)S(1)}, u32[]{:S(2)}, u32[]{:S(2)}) collective-permute-start(bf16[2,128,512]{2,1,0:T(8,128)(2,1)S(1)} %get-tuple-element.13.mine), channel_id=1, source_target_pairs={{0,1},{1,0},{2,3},{3,2},{4,5},{5,4},{6,7},{7,6},{8,9},{9,8},{10,11... | collective-permute-start | bytes 786440 | tf_op jit(solution)/shard_map/ppermute | solution.py:25
  115.9 12.2 %collective-permute-start.10 = (bf16[2,128,1024]{2,1,0:T(8,128)(2,1)S(1)}, bf16[2,128,1024]{2,1,0:T(8,128)(2,1)S(1)}, u32[]{:S(2)}, u32[]{:S(2)}) collective-permute-start(bf16[2,128,1024]{2,1,0:T(8,128)(2,1)S(1)} %get-tuple-element.14), channel_id=1, source_target_pairs={{0,2},{2,4},{4,6},{6,8},{8,10},{10,12},{12,14},{14,0},{1,3},{3,5},... | collective-permute-start | bytes 1572872 | tf_op jit(solution)/shard_map/ppermute | solution.py:29
  120.5 13.0 %collective-permute-start.11 = (bf16[2,128,1024]{2,1,0:T(8,128)(2,1)S(1)}, bf16[2,128,1024]{2,1,0:T(8,128)(2,1)S(1)}, u32[]{:S(2)}, u32[]{:S(2)}) collective-permute-start(bf16[2,128,1024]{2,1,0:T(8,128)(2,1)S(1)} %get-tuple-element.14), channel_id=1, source_target_pairs={{0,14},{2,0},{4,2},{6,4},{8,6},{10,8},{12,10},{14,12},{1,15},{3,1}... | collective-permute-start | bytes 1572872 | tf_op jit(solution)/shard_map/ppermute | solution.py:29
  128.0 13.5 %collective-permute-start.12 = (bf16[2,128,1024]{2,1,0:T(8,128)(2,1)S(1)}, bf16[2,128,1024]{2,1,0:T(8,128)(2,1)S(1)}, u32[]{:S(2)}, u32[]{:S(2)}) collective-permute-start(bf16[2,128,1024]{2,1,0:T(8,128)(2,1)S(1)} %collective-permute-done.10), channel_id=1, source_target_pairs={{0,2},{2,4},{4,6},{6,8},{8,10},{10,12},{12,14},{14,0},{1,3},{3,5},... | collective-permute-start | bytes 1572872 | tf_op jit(solution)/shard_map/ppermute | solution.py:29
  133.5 14.1 %collective-permute-start.13 = (bf16[2,128,1024]{2,1,0:T(8,128)(2,1)S(1)}, bf16[2,128,1024]{2,1,0:T(8,128)(2,1)S(1)}, u32[]{:S(2)}, u32[]{:S(2)}) collective-permute-start(bf16[2,128,1024]{2,1,0:T(8,128)(2,1)S(1)} %collective-permute-done.11), channel_id=1, source_target_pairs={{0,14},{2,0},{4,2},{6,4},{8,6},{10,8},{12,10},{14,12},{1,15},{3,1}... | collective-permute-start | bytes 1572872 | tf_op jit(solution)/shard_map/ppermute | solution.py:29
  141.5 14.9 %collective-permute-start.14 = (bf16[2,128,1024]{2,1,0:T(8,128)(2,1)S(1)}, bf16[2,128,1024]{2,1,0:T(8,128)(2,1)S(1)}, u32[]{:S(2)}, u32[]{:S(2)}) collective-permute-start(bf16[2,128,1024]{2,1,0:T(8,128)(2,1)S(1)} %collective-permute-done.12), channel_id=1, source_target_pairs={{0,2},{2,4},{4,6},{6,8},{8,10},{10,12},{12,14},{14,0},{1,3},{3,5},... | collective-permute-start | bytes 1572872 | tf_op jit(solution)/shard_map/ppermute | solution.py:29
  147.6 15.1 %collective-permute-start.15 = (bf16[2,128,1024]{2,1,0:T(8,128)(2,1)S(1)}, bf16[2,128,1024]{2,1,0:T(8,128)(2,1)S(1)}, u32[]{:S(2)}, u32[]{:S(2)}) collective-permute-start(bf16[2,128,1024]{2,1,0:T(8,128)(2,1)S(1)} %collective-permute-done.13), channel_id=1, source_target_pairs={{0,14},{2,0},{4,2},{6,4},{8,6},{10,8},{12,10},{14,12},{1,15},{3,1}... | collective-permute-start | bytes 1572872 | tf_op jit(solution)/shard_map/ppermute | solution.py:29
  156.4 9.5 %collective-permute-start.16 = (bf16[1,128,1024]{2,1,0:T(8,128)(2,1)S(1)}, bf16[1,128,1024]{2,1,0:T(8,128)(2,1)S(1)}, u32[]{:S(2)}, u32[]{:S(2)}) collective-permute-start(bf16[1,128,1024]{2,1,0:T(8,128)(2,1)S(1)} %slice.21), channel_id=1, source_target_pairs={{0,2},{2,4},{4,6},{6,8},{8,10},{10,12},{12,14},{14,0},{1,3},{3,5},... | collective-permute-start | bytes 786440 | tf_op jit(solution)/shard_map/ppermute | solution.py:29
  162.7 9.5 %collective-permute-start.17 = (bf16[1,128,1024]{2,1,0:T(8,128)(2,1)S(1)}, bf16[1,128,1024]{2,1,0:T(8,128)(2,1)S(1)}, u32[]{:S(2)}, u32[]{:S(2)}) collective-permute-start(bf16[1,128,1024]{2,1,0:T(8,128)(2,1)S(1)} %slice.22), channel_id=1, source_target_pairs={{0,14},{2,0},{4,2},{6,4},{8,6},{10,8},{12,10},{14,12},{1,15},{3,1}... | collective-permute-start | bytes 786440 | tf_op jit(solution)/shard_map/ppermute | solution.py:29
  (4 other events, 25.7 us)
Sparse Core Ops, SparseCore 0:
  10.1 50.7 all-gather.3

commit v5 on v4

--- a/solution.py
+++ b/solution.py
@@ -74,8 +74,12 @@
     values = jnp.where(
         row < 2, jnp.where(row == 0, squares[0], squares[1]), jnp.where(row == 2, adam[0][:1], adam[1][:1])
     )
-    for i in range(sums.shape[0]):
-        sums[i] = values
+    sums[...] = values
+
+
+def pair_sums_kernel(place, both, part, out, handed):
+    for i in range(out.shape[0]):
+        out[i] = both[0] + both[1]
 
 
 def grafted(place, sums, mine, theirs, block, precond):
@@ -137,6 +141,10 @@
     )(*operands)
 
 
+def later(place, x, *ready):
+    return call(lambda *refs: None, (), (place,), ready=ready, through=x)[0]
+
+
 def on_device(grad, left_root, right_root, master, momentum, second):
     place = jnp.stack([lax.axis_index("y"), lax.axis_index("xl")])
     _, rows, width = master.shape
@@ -150,12 +158,15 @@
     low = (value - high.astype(f32)).astype(bf16)
     base = high.astype(f32) + low.astype(f32)
     left_away = jnp.where(place[1] == 0, left_root[1], left_root[0])
-    swapped = swap(jnp.concatenate([left_away[None], high, low]).reshape(5 * rows, width))
+    away = jnp.concatenate([left_away[None], high, low]).reshape(5 * rows, width)
 
     spread = lax.all_to_all(grad, OWNERS + ("xl",), split_axis=0, concat_axis=1, tiled=True)
     pair = spread.reshape(-1, 2, grad.shape[1], width).swapaxes(0, 1).reshape(2 * rows, width)
 
+    pair = later(place, pair, away, base)
     up1, down1 = hop(pair, 1), hop(pair, -1)
+    swapped = swap(away)
+    down1 = later(place, down1, swapped)
     up2, down2 = hop(up1, 1), hop(down1, -1)
     up3, down3 = hop(up2, 1), hop(down2, -1)
     up4 = hop(up3, 1)
@@ -178,12 +189,18 @@
     )
     part, sums = call(
         right_kernel,
-        (shape((2, 2 * rows, width // 2), bf16), shape((2 * Y, 8, 128), f32)),
+        (shape((2, 2 * rows, width // 2), bf16), shape((8, 128), f32)),
         (place, lax.all_gather(left_grad, "xl", axis=0, tiled=False), squares, right),
         flops,
     )
+    sums, part = call(
+        pair_sums_kernel,
+        (shape((Y, 8, 128), f32),),
+        (place, lax.all_gather(sums, "xl", axis=0, tiled=False)),
+        through=part,
+    )
     part_other = swap(part)
-    sums = lax.all_to_all(sums, GROUP, split_axis=0, concat_axis=0, tiled=True)
+    sums = lax.all_to_all(sums, "y", split_axis=0, concat_axis=0, tiled=True)
 
     both, new_master, new_momentum = call(
         update_kernel,

time: 182 us -> 189 us (1.038)
  starting transfers between devices: 74.9 us -> 77 us
  blocking collectives: 22.2 us -> 24.2 us
    ppermute x15, waiting for transfers between devices: 39.7 us -> 46.4 us  [hop(): return lax.ppermute(x, 'y', [(i, (i + way) % Y) for i in range(Y)])]
    all_to_all x1, waiting for transfers between devices: 12.8 us -> 6.81 us  [on_device(): lax.all_to_all(grad, OWNERS + ('xl',), split_axis=0, concat_axis=1, tiled...]
    all_gather x0 -> x1, blocking collectives: none -> 4.34 us  [on_device(): lax.all_gather(sums, 'xl', axis=0, tiled=False)]
    all_to_all x1, blocking collectives: 15.2 us -> 12.8 us  [on_device(): sums = lax.all_to_all(sums, 'y', split_axis=0, concat_axis=0, tiled=True)]
    pallas_call x4 -> x7, Pallas kernels: 7.31 us -> 9.19 us  [call(): pl.pallas_call(kernel, out_shape=out_shape, in_specs=in_specs, out_specs=...]
    unnamed x16 -> x20, local copies, waits for them, and re-layouts: 2.98 us -> 4.64 us
  transfers between devices with their start and end apart: 20 -> 20, of which waited for: 14 -> 13; matrix products, arithmetic and copies ran while one was open for 3% -> 2% of each run, Pallas kernels for 1% -> 2%
where the time goes in v5:
time: 189 us; the launch traced here: 188 us
  starting transfers between devices  77 us (41%)
  waiting for transfers between devices  53.9 us (29%)
  blocking collectives  24.2 us (13%)
  between operations  14.5 us (8%)
  Pallas kernels  9.19 us (5%)
  local copies, waits for them, and re-layouts  6.65 us (4%)
  other arithmetic  2.49 us (1%)
    ppermute x15, starting transfers between devices, hop(): return lax.ppermute(x, 'y', [(i, (i + way) % Y) for i in range(Y)])  52.7 us
    ppermute x15, waiting for transfers between devices, hop(): return lax.ppermute(x, 'y', [(i, (i + way) % Y) for i in range(Y)])  46.4 us
    all_to_all x1, starting transfers between devices, on_device(): lax.all_to_all(grad, OWNERS + ('xl',), split_axis=0, concat_axis=1, tiled...  13.9 us
    all_to_all x1, blocking collectives, on_device(): sums = lax.all_to_all(sums, 'y', split_axis=0, concat_axis=0, tiled=True)  12.8 us
    ppermute x3, starting transfers between devices, swap(): return lax.ppermute(x, 'xl', SWAP)  10.3 us
    pallas_call x7, Pallas kernels, call(): pl.pallas_call(kernel, out_shape=out_shape, in_specs=in_specs, out_specs=...  9.19 us
    all_gather x1, blocking collectives, on_device(): lax.all_gather(left_grad, 'xl', axis=0, tiled=False)  7.05 us
    all_to_all x1, waiting for transfers between devices, on_device(): lax.all_to_all(grad, OWNERS + ('xl',), split_axis=0, concat_axis=1, tiled...  6.81 us
  transfers between devices with their start and end apart: 20, of which 13 were waited for; matrix products, arithmetic and copies ran while one was open for 2% of the time, Pallas kernels for 2%

profile of v5, /device:TPU:56, one launch (start us, length us, event | category | flops | bytes accessed | tf_op | source)
XLA Modules:
  0.0 187.9 jit_solution(7996604597283483798)
XLA Ops:
  7.9 13.9 %all-to-all-start = ((bf16[64,2,1024]{2,1,0:T(2,128)(2,1)}), bf16[64,2,1024]{2,1,0:T(2,128)(2,1)S(1)}, u32[]{:S(2)}, u32[]{:S(2)}) async-start(bf16[64,2,1024]{2,1,0:T(2,128)(2,1)} %param.6), calls=%async_computation | async-start | bytes 524288 | tf_op jit(solution)/shard_map/all_to_all | solution.py:163
  24.3 3.5 %collective-permute-start = (bf16[320,1024]{1,0:T(8,128)(2,1)S(1)}, bf16[320,1024]{1,0:T(8,128)(2,1)S(1)}, u32[]{:S(2)}, u32[]{:S(2)}) collective-permute-start(bf16[320,1024]{1,0:T(8,128)(2,1)S(1)} %bitcast.45), channel_id=1, source_target_pairs={{0,1},{1,0},{2,3},{3,2},{4,5},{5,4},{6,7},{7,6},{8,9},{9,8},{10,11... | collective-permute-start | bytes 1966088 | tf_op jit(solution)/shard_map/ppermute | solution.py:25
  27.9 6.8 %all-to-all-done = bf16[64,2,1024]{2,1,0:T(2,128)(2,1)S(1)} async-done(((bf16[64,2,1024]{2,1,0:T(2,128)(2,1)}), bf16[64,2,1024]{2,1,0:T(2,128)(2,1)S(1)}, u32[]{:S(2)}, u32[]{:S(2)}) %all-to-all-start) | async-done | bytes 262176 | tf_op jit(solution)/shard_map/all_to_all | solution.py:163
  37.4 4.0 %collective-permute-start.2 = (bf16[128,1024]{1,0:T(8,128)(2,1)S(1)}, bf16[128,1024]{1,0:T(8,128)(2,1)S(1)}, u32[]{:S(2)}, u32[]{:S(2)}) collective-permute-start(bf16[128,1024]{1,0:T(8,128)(2,1)S(1)} %shard_map.93.mine.refs_3_), channel_id=1, source_target_pairs={{0,14},{2,0},{4,2},{6,4},{8,6},{10,8},{12,10},{14,12},{1,15},{3,1}... | collective-permute-start | bytes 786440 | tf_op jit(solution)/shard_map/ppermute | solution.py:29
  41.4 10.3 %collective-permute-done.1.refs_4_ = bf16[128,1024]{1,0:T(8,128)(2,1)S(1)} collective-permute-done((bf16[128,1024]{1,0:T(8,128)(2,1)S(1)}, bf16[128,1024]{1,0:T(8,128)(2,1)S(1)}, u32[]{:S(2)}, u32[]{:S(2)}) %collective-permute-start.1) | collective-permute-done | bytes 262176 | tf_op jit(solution)/shard_map/ppermute | solution.py:29
  51.7 3.1 %collective-permute-start.3 = (bf16[128,1024]{1,0:T(8,128)(2,1)S(1)}, bf16[128,1024]{1,0:T(8,128)(2,1)S(1)}, u32[]{:S(2)}, u32[]{:S(2)}) collective-permute-start(bf16[128,1024]{1,0:T(8,128)(2,1)S(1)} %collective-permute-done.1.refs_4_), channel_id=1, source_target_pairs={{0,2},{2,4},{4,6},{6,8},{8,10},{10,12},{12,14},{14,0},{1,3},{3,5},... | collective-permute-start | bytes 786440 | tf_op jit(solution)/shard_map/ppermute | solution.py:29
  55.4 2.9 %collective-permute-start.4 = (bf16[128,1024]{1,0:T(8,128)(2,1)S(1)}, bf16[128,1024]{1,0:T(8,128)(2,1)}, u32[]{:S(2)}, u32[]{:S(2)}) collective-permute-start(bf16[128,1024]{1,0:T(8,128)(2,1)S(1)} %shard_map.94.refs_5_), channel_id=1, source_target_pairs={{0,14},{2,0},{4,2},{6,4},{8,6},{10,8},{12,10},{14,12},{1,15},{3,1}... | collective-permute-start | bytes 786440 | tf_op jit(solution)/shard_map/ppermute | solution.py:29
  58.3 4.6 %collective-permute-done.3.refs_6_ = bf16[128,1024]{1,0:T(8,128)(2,1)S(1)} collective-permute-done((bf16[128,1024]{1,0:T(8,128)(2,1)S(1)}, bf16[128,1024]{1,0:T(8,128)(2,1)S(1)}, u32[]{:S(2)}, u32[]{:S(2)}) %collective-permute-start.3) | collective-permute-done | bytes 262176 | tf_op jit(solution)/shard_map/ppermute | solution.py:29
  62.9 4.5 %collective-permute-start.5 = (bf16[128,1024]{1,0:T(8,128)(2,1)S(1)}, bf16[128,1024]{1,0:T(8,128)(2,1)}, u32[]{:S(2)}, u32[]{:S(2)}) collective-permute-start(bf16[128,1024]{1,0:T(8,128)(2,1)S(1)} %collective-permute-done.3.refs_6_), channel_id=1, source_target_pairs={{0,2},{2,4},{4,6},{6,8},{8,10},{10,12},{12,14},{14,0},{1,3},{3,5},... | collective-permute-start | bytes 786440 | tf_op jit(solution)/shard_map/ppermute | solution.py:29
  68.1 3.3 %collective-permute-start.8 = (bf16[128,1024]{1,0:T(8,128)(2,1)S(1)}, bf16[128,1024]{1,0:T(8,128)(2,1)}, u32[]{:S(2)}, u32[]{:S(2)}) collective-permute-start(bf16[128,1024]{1,0:T(8,128)(2,1)S(1)} %shard_map.93.mine.refs_3_), channel_id=1, source_target_pairs={{0,1},{1,0},{2,3},{3,2},{4,5},{5,4},{6,7},{7,6},{8,9},{9,8},{10,11... | collective-permute-start | bytes 786440 | tf_op jit(solution)/shard_map/ppermute | solution.py:25
  73.4 5.2 %collective-permute-start.7 = (bf16[128,1024]{1,0:T(8,128)(2,1)}, bf16[128,1024]{1,0:T(8,128)(2,1)}, u32[]{:S(2)}, u32[]{:S(2)}) collective-permute-start(bf16[128,1024]{1,0:T(8,128)(2,1)} %collective-permute-done.5.refs_8_), channel_id=1, source_target_pairs={{0,2},{2,4},{4,6},{6,8},{8,10},{10,12},{12,14},{14,0},{1,3},{3,5},... | collective-permute-start | bytes 786440 | tf_op jit(solution)/shard_map/ppermute | solution.py:29
  87.5 7.0 %all-gather.1 = bf16[256,1024]{1,0:T(8,128)(2,1)S(1)} all-gather(bf16[128,1024]{1,0:T(8,128)(2,1)S(1)} %shard_map.96), channel_id=3, replica_groups=mesh['z'=8,'xh'=2,'c'=2,'y'=8,'xl'=2] {'xl'}, dimensions={0}, use_global_device_ids=true | all-gather | bytes 786432 | tf_op jit(solution)/shard_map/all_gather | solution.py:193
  96.0 4.3 %all-gather.2 = f32[16,128]{1,0:T(8,128)S(1)} all-gather(f32[8,128]{1,0:T(8,128)S(1)} %get-tuple-element.14), channel_id=4, replica_groups=mesh['z'=8,'xh'=2,'c'=2,'y'=8,'xl'=2] {'xl'}, dimensions={0}, use_global_device_ids=true | all-gather | bytes 12288 | tf_op jit(solution)/shard_map/all_gather | solution.py:199
  100.9 3.5 %collective-permute-start.9 = (bf16[2,128,512]{2,1,0:T(8,128)(2,1)S(1)}, bf16[2,128,512]{2,1,0:T(8,128)(2,1)S(1)}, u32[]{:S(2)}, u32[]{:S(2)}) collective-permute-start(bf16[2,128,512]{2,1,0:T(8,128)(2,1)S(1)} %get-tuple-element.17.mine), channel_id=1, source_target_pairs={{0,1},{1,0},{2,3},{3,2},{4,5},{5,4},{6,7},{7,6},{8,9},{9,8},{10,11... | collective-permute-start | bytes 786440 | tf_op jit(solution)/shard_map/ppermute | solution.py:25
  104.5 12.8 %all_to_all.14.sums = f32[8,8,128]{2,1,0:T(8,128)S(1)} all-to-all(f32[8,8,128]{2,1,0:T(8,128)S(1)} %get-tuple-element.16), channel_id=1, replica_groups=mesh['z'=8,'xh'=2,'c'=2,'y'=8,'xl'=2] {'y'}, dimensions={0} | all-to-all | bytes 65536 | tf_op jit(solution)/shard_map/all_to_all | solution.py:203
  117.3 2.1 %shard_map.99 = (bf16[2,128,1024]{2,1,0:T(8,128)(2,1)S(1)}, f32[2,64,1024]{2,1,0:T(8,128)}, f32[2,64,1024]{2,1,0:T(8,128)}) custom-call(s32[2]{0:T(128)S(1)} %pad_add_fusion.refs_0_.place, f32[8,8,128]{2,1,0:T(8,128)S(1)} %all_to_all.14.sums, bf16[2,128,512]{2,1,0:T(8,128)(2,1)S(1)} %get-tuple-element.17.mine, ...), custom_call_target="tpu_custom_call" | custom-call | bytes 5570576 | tf_op jit(solution)/shard_map/pallas_call | solution.py:132
  119.4 4.8 %collective-permute-start.10 = (bf16[2,128,1024]{2,1,0:T(8,128)(2,1)S(1)}, bf16[2,128,1024]{2,1,0:T(8,128)(2,1)S(1)}, u32[]{:S(2)}, u32[]{:S(2)}) collective-permute-start(bf16[2,128,1024]{2,1,0:T(8,128)(2,1)S(1)} %get-tuple-element.18), channel_id=1, source_target_pairs={{0,2},{2,4},{4,6},{6,8},{8,10},{10,12},{12,14},{14,0},{1,3},{3,5},... | collective-permute-start | bytes 1572872 | tf_op jit(solution)/shard_map/ppermute | solution.py:29
  126.2 6.8 %collective-permute-done.10 = bf16[2,128,1024]{2,1,0:T(8,128)(2,1)S(1)} collective-permute-done((bf16[2,128,1024]{2,1,0:T(8,128)(2,1)S(1)}, bf16[2,128,1024]{2,1,0:T(8,128)(2,1)S(1)}, u32[]{:S(2)}, u32[]{:S(2)}) %collective-permute-start.10) | collective-permute-done | bytes 524320 | tf_op jit(solution)/shard_map/ppermute | solution.py:29
  132.9 5.6 %collective-permute-start.12 = (bf16[2,128,1024]{2,1,0:T(8,128)(2,1)S(1)}, bf16[2,128,1024]{2,1,0:T(8,128)(2,1)S(1)}, u32[]{:S(2)}, u32[]{:S(2)}) collective-permute-start(bf16[2,128,1024]{2,1,0:T(8,128)(2,1)S(1)} %collective-permute-done.10), channel_id=1, source_target_pairs={{0,2},{2,4},{4,6},{6,8},{8,10},{10,12},{12,14},{14,0},{1,3},{3,5},... | collective-permute-start | bytes 1572872 | tf_op jit(solution)/shard_map/ppermute | solution.py:29
  141.4 6.9 %collective-permute-done.12 = bf16[2,128,1024]{2,1,0:T(8,128)(2,1)S(1)} collective-permute-done((bf16[2,128,1024]{2,1,0:T(8,128)(2,1)S(1)}, bf16[2,128,1024]{2,1,0:T(8,128)(2,1)S(1)}, u32[]{:S(2)}, u32[]{:S(2)}) %collective-permute-start.12) | collective-permute-done | bytes 524320 | tf_op jit(solution)/shard_map/ppermute | solution.py:29
  148.3 5.6 %collective-permute-start.14 = (bf16[2,128,1024]{2,1,0:T(8,128)(2,1)S(1)}, bf16[2,128,1024]{2,1,0:T(8,128)(2,1)S(1)}, u32[]{:S(2)}, u32[]{:S(2)}) collective-permute-start(bf16[2,128,1024]{2,1,0:T(8,128)(2,1)S(1)} %collective-permute-done.12), channel_id=1, source_target_pairs={{0,2},{2,4},{4,6},{6,8},{8,10},{10,12},{12,14},{14,0},{1,3},{3,5},... | collective-permute-start | bytes 1572872 | tf_op jit(solution)/shard_map/ppermute | solution.py:29
  156.6 6.9 %collective-permute-done.14 = bf16[2,128,1024]{2,1,0:T(8,128)(2,1)S(1)} collective-permute-done((bf16[2,128,1024]{2,1,0:T(8,128)(2,1)S(1)}, bf16[2,128,1024]{2,1,0:T(8,128)(2,1)S(1)}, u32[]{:S(2)}, u32[]{:S(2)}) %collective-permute-start.14) | collective-permute-done | bytes 524320 | tf_op jit(solution)/shard_map/ppermute | solution.py:29
  163.4 5.6 %collective-permute-start.16 = (bf16[1,128,1024]{2,1,0:T(8,128)(2,1)S(1)}, bf16[1,128,1024]{2,1,0:T(8,128)(2,1)S(1)}, u32[]{:S(2)}, u32[]{:S(2)}) collective-permute-start(bf16[1,128,1024]{2,1,0:T(8,128)(2,1)S(1)} %slice.21), channel_id=1, source_target_pairs={{0,2},{2,4},{4,6},{6,8},{8,10},{10,12},{12,14},{14,0},{1,3},{3,5},... | collective-permute-start | bytes 786440 | tf_op jit(solution)/shard_map/ppermute | solution.py:29
  172.9 6.1 %collective-permute-done.17 = bf16[1,128,1024]{2,1,0:T(8,128)(2,1)S(1)} collective-permute-done((bf16[1,128,1024]{2,1,0:T(8,128)(2,1)S(1)}, bf16[1,128,1024]{2,1,0:T(8,128)(2,1)S(1)}, u32[]{:S(2)}, u32[]{:S(2)}) %collective-permute-start.17) | collective-permute-done | bytes 262176 | tf_op jit(solution)/shard_map/ppermute | solution.py:29
  (66 shorter events, 33.3 us)
Async XLA Ops:
  7.2 71.4 %all-gather.5.cloned.1.call-start = ((), (), s32[]{:S(2)}) async-start(), calls=%async_computation.2 | async-start | bytes 2359296 | tf_op jit(solution)/shard_map/all_gather | solution.py:154
  7.9 71.5 %copy-start.4 = (f32[2,64,1024]{2,1,0:T(8,128)S(1)}, f32[2,64,1024]{2,1,0:T(8,128)}, u32[]{:S(2)}) copy-start(f32[2,64,1024]{2,1,0:T(8,128)} %second.1) | copy-start | bytes 1572868
  7.9 26.8 %all-to-all-start = ((bf16[64,2,1024]{2,1,0:T(2,128)(2,1)}), bf16[64,2,1024]{2,1,0:T(2,128)(2,1)S(1)}, u32[]{:S(2)}, u32[]{:S(2)}) async-start(bf16[64,2,1024]{2,1,0:T(2,128)(2,1)} %param.6), calls=%async_computation | async-start | bytes 524288 | tf_op jit(solution)/shard_map/all_to_all | solution.py:163
  22.8 60.8 %copy-start.3 = (bf16[2,64,1024]{2,1,0:T(8,128)(2,1)S(1)}, bf16[2,64,1024]{2,1,0:T(8,128)(2,1)}, u32[]{:S(2)}) copy-start(bf16[2,64,1024]{2,1,0:T(8,128)(2,1)} %refs_1_.1) | copy-start | bytes 786436
  24.3 30.5 %collective-permute-start = (bf16[320,1024]{1,0:T(8,128)(2,1)S(1)}, bf16[320,1024]{1,0:T(8,128)(2,1)S(1)}, u32[]{:S(2)}, u32[]{:S(2)}) collective-permute-start(bf16[320,1024]{1,0:T(8,128)(2,1)S(1)} %bitcast.45), channel_id=1, source_target_pairs={{0,1},{1,0},{2,3},{3,2},{4,5},{5,4},{6,7},{7,6},{8,9},{9,8},{10,11... | collective-permute-start | bytes 1966088 | tf_op jit(solution)/shard_map/ppermute | solution.py:25
  35.5 16.2 %collective-permute-start.1 = (bf16[128,1024]{1,0:T(8,128)(2,1)S(1)}, bf16[128,1024]{1,0:T(8,128)(2,1)S(1)}, u32[]{:S(2)}, u32[]{:S(2)}) collective-permute-start(bf16[128,1024]{1,0:T(8,128)(2,1)S(1)} %shard_map.93.mine.refs_3_), channel_id=1, source_target_pairs={{0,2},{2,4},{4,6},{6,8},{8,10},{10,12},{12,14},{14,0},{1,3},{3,5},... | collective-permute-start | bytes 786440 | tf_op jit(solution)/shard_map/ppermute | solution.py:29
  37.4 17.4 %collective-permute-start.2 = (bf16[128,1024]{1,0:T(8,128)(2,1)S(1)}, bf16[128,1024]{1,0:T(8,128)(2,1)S(1)}, u32[]{:S(2)}, u32[]{:S(2)}) collective-permute-start(bf16[128,1024]{1,0:T(8,128)(2,1)S(1)} %shard_map.93.mine.refs_3_), channel_id=1, source_target_pairs={{0,14},{2,0},{4,2},{6,4},{8,6},{10,8},{12,10},{14,12},{1,15},{3,1}... | collective-permute-start | bytes 786440 | tf_op jit(solution)/shard_map/ppermute | solution.py:29
  51.7 11.2 %collective-permute-start.3 = (bf16[128,1024]{1,0:T(8,128)(2,1)S(1)}, bf16[128,1024]{1,0:T(8,128)(2,1)S(1)}, u32[]{:S(2)}, u32[]{:S(2)}) collective-permute-start(bf16[128,1024]{1,0:T(8,128)(2,1)S(1)} %collective-permute-done.1.refs_4_), channel_id=1, source_target_pairs={{0,2},{2,4},{4,6},{6,8},{8,10},{10,12},{12,14},{14,0},{1,3},{3,5},... | collective-permute-start | bytes 786440 | tf_op jit(solution)/shard_map/ppermute | solution.py:29
  55.4 61.9 %copy-start.1 = (f32[2,64,1024]{2,1,0:T(8,128)S(1)}, f32[2,64,1024]{2,1,0:T(8,128)}, u32[]{:S(2)}) copy-start(f32[2,64,1024]{2,1,0:T(8,128)} %master.1) | copy-start | bytes 1572868
  55.4 61.9 %copy-start.2 = (f32[2,64,1024]{2,1,0:T(8,128)S(1)}, f32[2,64,1024]{2,1,0:T(8,128)}, u32[]{:S(2)}) copy-start(f32[2,64,1024]{2,1,0:T(8,128)} %momentum.1) | copy-start | bytes 1572868
  55.4 16.0 %collective-permute-start.4 = (bf16[128,1024]{1,0:T(8,128)(2,1)S(1)}, bf16[128,1024]{1,0:T(8,128)(2,1)}, u32[]{:S(2)}, u32[]{:S(2)}) collective-permute-start(bf16[128,1024]{1,0:T(8,128)(2,1)S(1)} %shard_map.94.refs_5_), channel_id=1, source_target_pairs={{0,14},{2,0},{4,2},{6,4},{8,6},{10,8},{12,10},{14,12},{1,15},{3,1}... | collective-permute-start | bytes 786440 | tf_op jit(solution)/shard_map/ppermute | solution.py:29
  62.9 10.5 %collective-permute-start.5 = (bf16[128,1024]{1,0:T(8,128)(2,1)S(1)}, bf16[128,1024]{1,0:T(8,128)(2,1)}, u32[]{:S(2)}, u32[]{:S(2)}) collective-permute-start(bf16[128,1024]{1,0:T(8,128)(2,1)S(1)} %collective-permute-done.3.refs_6_), channel_id=1, source_target_pairs={{0,2},{2,4},{4,6},{6,8},{8,10},{10,12},{12,14},{14,0},{1,3},{3,5},... | collective-permute-start | bytes 786440 | tf_op jit(solution)/shard_map/ppermute | solution.py:29
  68.1 11.3 %collective-permute-start.8 = (bf16[128,1024]{1,0:T(8,128)(2,1)S(1)}, bf16[128,1024]{1,0:T(8,128)(2,1)}, u32[]{:S(2)}, u32[]{:S(2)}) collective-permute-start(bf16[128,1024]{1,0:T(8,128)(2,1)S(1)} %shard_map.93.mine.refs_3_), channel_id=1, source_target_pairs={{0,1},{1,0},{2,3},{3,2},{4,5},{5,4},{6,7},{7,6},{8,9},{9,8},{10,11... | collective-permute-start | bytes 786440 | tf_op jit(solution)/shard_map/ppermute | solution.py:25
  71.5 11.0 %collective-permute-start.6 = (bf16[128,1024]{1,0:T(8,128)(2,1)}, bf16[128,1024]{1,0:T(8,128)(2,1)}, u32[]{:S(2)}, u32[]{:S(2)}) collective-permute-start(bf16[128,1024]{1,0:T(8,128)(2,1)} %collective-permute-done.4.refs_7_), channel_id=1, source_target_pairs={{0,14},{2,0},{4,2},{6,4},{8,6},{10,8},{12,10},{14,12},{1,15},{3,1}... | collective-permute-start | bytes 786440 | tf_op jit(solution)/shard_map/ppermute | solution.py:29
  73.4 10.3 %collective-permute-start.7 = (bf16[128,1024]{1,0:T(8,128)(2,1)}, bf16[128,1024]{1,0:T(8,128)(2,1)}, u32[]{:S(2)}, u32[]{:S(2)}) collective-permute-start(bf16[128,1024]{1,0:T(8,128)(2,1)} %collective-permute-done.5.refs_8_), channel_id=1, source_target_pairs={{0,2},{2,4},{4,6},{6,8},{8,10},{10,12},{12,14},{14,0},{1,3},{3,5},... | collective-permute-start | bytes 786440 | tf_op jit(solution)/shard_map/ppermute | solution.py:29
  100.9 16.3 %collective-permute-start.9 = (bf16[2,128,512]{2,1,0:T(8,128)(2,1)S(1)}, bf16[2,128,512]{2,1,0:T(8,128)(2,1)S(1)}, u32[]{:S(2)}, u32[]{:S(2)}) collective-permute-start(bf16[2,128,512]{2,1,0:T(8,128)(2,1)S(1)} %get-tuple-element.17.mine), channel_id=1, source_target_pairs={{0,1},{1,0},{2,3},{3,2},{4,5},{5,4},{6,7},{7,6},{8,9},{9,8},{10,11... | collective-permute-start | bytes 786440 | tf_op jit(solution)/shard_map/ppermute | solution.py:25
  119.4 13.6 %collective-permute-start.10 = (bf16[2,128,1024]{2,1,0:T(8,128)(2,1)S(1)}, bf16[2,128,1024]{2,1,0:T(8,128)(2,1)S(1)}, u32[]{:S(2)}, u32[]{:S(2)}) collective-permute-start(bf16[2,128,1024]{2,1,0:T(8,128)(2,1)S(1)} %get-tuple-element.18), channel_id=1, source_target_pairs={{0,2},{2,4},{4,6},{6,8},{8,10},{10,12},{12,14},{14,0},{1,3},{3,5},... | collective-permute-start | bytes 1572872 | tf_op jit(solution)/shard_map/ppermute | solution.py:29
  124.2 14.6 %collective-permute-start.11 = (bf16[2,128,1024]{2,1,0:T(8,128)(2,1)S(1)}, bf16[2,128,1024]{2,1,0:T(8,128)(2,1)S(1)}, u32[]{:S(2)}, u32[]{:S(2)}) collective-permute-start(bf16[2,128,1024]{2,1,0:T(8,128)(2,1)S(1)} %get-tuple-element.18), channel_id=1, source_target_pairs={{0,14},{2,0},{4,2},{6,4},{8,6},{10,8},{12,10},{14,12},{1,15},{3,1}... | collective-permute-start | bytes 1572872 | tf_op jit(solution)/shard_map/ppermute | solution.py:29
  132.9 15.4 %collective-permute-start.12 = (bf16[2,128,1024]{2,1,0:T(8,128)(2,1)S(1)}, bf16[2,128,1024]{2,1,0:T(8,128)(2,1)S(1)}, u32[]{:S(2)}, u32[]{:S(2)}) collective-permute-start(bf16[2,128,1024]{2,1,0:T(8,128)(2,1)S(1)} %collective-permute-done.10), channel_id=1, source_target_pairs={{0,2},{2,4},{4,6},{6,8},{8,10},{10,12},{12,14},{14,0},{1,3},{3,5},... | collective-permute-start | bytes 1572872 | tf_op jit(solution)/shard_map/ppermute | solution.py:29
  138.8 15.6 %collective-permute-start.13 = (bf16[2,128,1024]{2,1,0:T(8,128)(2,1)S(1)}, bf16[2,128,1024]{2,1,0:T(8,128)(2,1)S(1)}, u32[]{:S(2)}, u32[]{:S(2)}) collective-permute-start(bf16[2,128,1024]{2,1,0:T(8,128)(2,1)S(1)} %collective-permute-done.11), channel_id=1, source_target_pairs={{0,14},{2,0},{4,2},{6,4},{8,6},{10,8},{12,10},{14,12},{1,15},{3,1}... | collective-permute-start | bytes 1572872 | tf_op jit(solution)/shard_map/ppermute | solution.py:29
  148.3 15.1 %collective-permute-start.14 = (bf16[2,128,1024]{2,1,0:T(8,128)(2,1)S(1)}, bf16[2,128,1024]{2,1,0:T(8,128)(2,1)S(1)}, u32[]{:S(2)}, u32[]{:S(2)}) collective-permute-start(bf16[2,128,1024]{2,1,0:T(8,128)(2,1)S(1)} %collective-permute-done.12), channel_id=1, source_target_pairs={{0,2},{2,4},{4,6},{6,8},{8,10},{10,12},{12,14},{14,0},{1,3},{3,5},... | collective-permute-start | bytes 1572872 | tf_op jit(solution)/shard_map/ppermute | solution.py:29
  154.5 15.1 %collective-permute-start.15 = (bf16[2,128,1024]{2,1,0:T(8,128)(2,1)S(1)}, bf16[2,128,1024]{2,1,0:T(8,128)(2,1)S(1)}, u32[]{:S(2)}, u32[]{:S(2)}) collective-permute-start(bf16[2,128,1024]{2,1,0:T(8,128)(2,1)S(1)} %collective-permute-done.13), channel_id=1, source_target_pairs={{0,14},{2,0},{4,2},{6,4},{8,6},{10,8},{12,10},{14,12},{1,15},{3,1}... | collective-permute-start | bytes 1572872 | tf_op jit(solution)/shard_map/ppermute | solution.py:29
  163.4 9.5 %collective-permute-start.16 = (bf16[1,128,1024]{2,1,0:T(8,128)(2,1)S(1)}, bf16[1,128,1024]{2,1,0:T(8,128)(2,1)S(1)}, u32[]{:S(2)}, u32[]{:S(2)}) collective-permute-start(bf16[1,128,1024]{2,1,0:T(8,128)(2,1)S(1)} %slice.21), channel_id=1, source_target_pairs={{0,2},{2,4},{4,6},{6,8},{8,10},{10,12},{12,14},{14,0},{1,3},{3,5},... | collective-permute-start | bytes 786440 | tf_op jit(solution)/shard_map/ppermute | solution.py:29
  169.6 9.5 %collective-permute-start.17 = (bf16[1,128,1024]{2,1,0:T(8,128)(2,1)S(1)}, bf16[1,128,1024]{2,1,0:T(8,128)(2,1)S(1)}, u32[]{:S(2)}, u32[]{:S(2)}) collective-permute-start(bf16[1,128,1024]{2,1,0:T(8,128)(2,1)S(1)} %slice.22), channel_id=1, source_target_pairs={{0,14},{2,0},{4,2},{6,4},{8,6},{10,8},{12,10},{14,12},{1,15},{3,1}... | collective-permute-start | bytes 786440 | tf_op jit(solution)/shard_map/ppermute | solution.py:29
  (6 other events, 40.2 us)
Sparse Core Ops, SparseCore 0:
  10.1 50.7 all-gather.4

commit v6 on v4

--- a/solution.py
+++ b/solution.py
@@ -43,18 +43,30 @@
         squares[block] = jnp.full(squares.shape[1:], jnp.sum(step * step), jnp.float32)
 
 
-def left_kernel(distances, place, left_own, swapped, *refs):
-    chunks, out = refs[: len(distances)], refs[-1]
+def left_products(distances, place, left_own, swapped, chunks, total):
     rows = left_own.shape[1]
     depth = chunks[0].shape[0]
     half = place[1]
-    total = jnp.zeros((2 * rows, out.shape[1]), jnp.float32)
     for distance, chunk in zip(distances, chunks):
         at = pl.multiple_of(lax.rem(place[0] + distance + Y, Y) * depth, depth)
         columns = jnp.concatenate(
             [left_own[half, :, pl.ds(at, depth)], swapped[:rows, pl.ds(at, depth)]], axis=0
         )
-        total += jnp.dot(columns, chunk[...], preferred_element_type=jnp.float32)
+        part = jnp.dot(columns, chunk[...], preferred_element_type=jnp.float32)
+        total = part if total is None else total + part
+    return total
+
+
+def early_kernel(distances, place, left_own, swapped, *refs):
+    out = refs[len(distances)]
+    out[...] = left_products(distances, place, left_own, swapped, refs[: len(distances)], None)
+
+
+def late_kernel(distances, place, left_own, swapped, early, *refs):
+    out = refs[-1]
+    rows = left_own.shape[1]
+    half = place[1]
+    total = left_products(distances, place, left_own, swapped, refs[: len(distances)], early[...])
     rounded = total.astype(jnp.bfloat16)
     out[pl.ds(pl.multiple_of(half * rows, rows), rows), :] = rounded[:rows]
     out[pl.ds(pl.multiple_of((1 - half) * rows, rows), rows), :] = rounded[rows:]
@@ -95,20 +107,25 @@
         precond[:, (2 * i + 1) * 128 : (2 * i + 2) * 128] = graft * odd
 
 
-def update_kernel(
-    place, sums, mine, theirs, base, swapped, master, momentum, params, new_master, new_momentum, precond
-):
-    rows = master.shape[1]
+def params_kernel(place, sums, mine, theirs, base, swapped, params, precond):
+    rows = base.shape[1]
     own = pl.ds(pl.multiple_of(place[1] * rows, rows), rows)
     other = pl.ds(pl.multiple_of((1 - place[1]) * rows, rows), rows)
     for block in range(2):
         grafted(place, sums, mine, theirs, block, precond)
-        ours = precond[own, :]
-        params[block, own, :] = (base[block] - learn_rate * ours).astype(jnp.bfloat16)
+        params[block, own, :] = (base[block] - learn_rate * precond[own, :]).astype(jnp.bfloat16)
         high = swapped[(1 + block) * rows : (2 + block) * rows, :].astype(jnp.float32)
         low = swapped[(3 + block) * rows : (4 + block) * rows, :].astype(jnp.float32)
         params[block, other, :] = (high + low - learn_rate * precond[other, :]).astype(jnp.bfloat16)
-        moved = momentum_decay * momentum[block] + ours
+
+
+def state_kernel(place, sums, mine, theirs, master, momentum, both, new_master, new_momentum, params, precond):
+    rows = master.shape[1]
+    own = pl.ds(pl.multiple_of(place[1] * rows, rows), rows)
+    for block in range(2):
+        params[block, place[0]] = both[block]
+        grafted(place, sums, mine, theirs, block, precond)
+        moved = momentum_decay * momentum[block] + precond[own, :]
         new_momentum[block] = moved
         new_master[block] = master[block] - learn_rate * moved
 
@@ -159,8 +176,6 @@
     up2, down2 = hop(up1, 1), hop(down1, -1)
     up3, down3 = hop(up2, 1), hop(down2, -1)
     up4 = hop(up3, 1)
-    chunks = (pair, up1, down1, up2, down2, up3, down3, up4)
-    distances = (0, -1, 1, -2, 2, -3, 3, -4)
     new_second, squares = call(
         adam_kernel,
         (shape(second.shape, f32), shape((2, 8, 128), f32)),
@@ -169,10 +184,16 @@
     )
 
     flops = 4 * rows * width * width
+    (early,) = call(
+        lambda *refs: early_kernel((0, -1, 1, -2, 2, -3), *refs),
+        (shape((2 * rows, width), f32),),
+        (place, left_root, swapped, pair, up1, down1, up2, down2, up3),
+        flops,
+    )
     (left_grad,) = call(
-        lambda *refs: left_kernel(distances, *refs),
+        lambda *refs: late_kernel((3, -4), *refs),
         (shape((2 * rows, width), bf16),),
-        (place, left_root, swapped, *chunks),
+        (place, left_root, swapped, early, down3, up4),
         flops,
         ready=(squares,),
     )
@@ -185,27 +206,34 @@
     part_other = swap(part)
     sums = lax.all_to_all(sums, GROUP, split_axis=0, concat_axis=0, tiled=True)
 
-    both, new_master, new_momentum = call(
-        update_kernel,
-        (shape((2, 2 * rows, width), bf16), shape(master.shape, f32), shape(master.shape, f32)),
-        (place, sums, part, part_other, base, swapped, master, momentum),
-        scratch_shapes=[pltpu.VMEM((2 * rows, width), f32)],
-    )
-
-    params = jnp.zeros((2, Y, 2 * rows, width), bf16)
-
-    def put(params, chunk, block, distance):
+    scratch = [pltpu.VMEM((2 * rows, width), f32)]
+    (both,) = call(
+        params_kernel,
+        (shape((2, 2 * rows, width), bf16),),
+        (place, sums, part, part_other, base, swapped),
+        scratch_shapes=scratch,
+    )
+    new_master, new_momentum, params = call(
+        state_kernel,
+        (shape(master.shape, f32), shape(master.shape, f32), shape((2, Y, 2 * rows, width), bf16)),
+        (place, sums, part, part_other, master, momentum, both),
+        scratch_shapes=scratch,
+    )
+
+    def put(params, chunk, block, distance, row=0):
         at = lax.rem(place[0] + distance + Y, Y)
-        return lax.dynamic_update_slice(params, chunk[:, None], (block, at, 0, 0))
-
-    params = put(params, both, 0, 0)
+        return lax.dynamic_update_slice(params, chunk[:, None], (block, at, row, 0))
+
     up = down = both
     for step in range(1, 4):
         up, down = hop(up, 1), hop(down, -1)
         params = put(params, up, 0, -step)
         params = put(params, down, 0, step)
-    params = put(params, hop(up[:1], 1), 0, 4)
-    params = put(params, hop(down[1:], -1), 1, 4)
+    up = hop(up.reshape(4, rows, width)[:3], 1)
+    down = hop(down.reshape(4, rows, width)[3:], -1)
+    params = put(params, up[:2].reshape(1, 2 * rows, width), 0, 4)
+    params = put(params, up[2:], 1, 4)
+    params = put(params, down, 1, 4, rows)
     params = params.reshape(2, 2 * Y * rows, width)
     return (params, new_master, new_momentum, new_second)
 

time: 182 us -> 180 us (0.989)
  the two profiles are of different devices: /device:TPU:56 before, /device:TPU:68 now
where the time goes in v6:
time: 180 us; the launch traced here: 179 us
  starting transfers between devices  74.2 us (41%)
  waiting for transfers between devices  44.1 us (24%)
  blocking collectives  20.6 us (11%)
  between operations  14.4 us (8%)
  local copies, waits for them, and re-layouts  11.9 us (7%)
  Pallas kernels  10.7 us (6%)
  other arithmetic  3.3 us (2%)
    ppermute x15, starting transfers between devices, hop(): return lax.ppermute(x, 'y', [(i, (i + way) % Y) for i in range(Y)])  51.9 us
    ppermute x15, waiting for transfers between devices, hop(): return lax.ppermute(x, 'y', [(i, (i + way) % Y) for i in range(Y)])  33.2 us
    all_to_all x1, blocking collectives, on_device(): sums = lax.all_to_all(sums, GROUP, split_axis=0, concat_axis=0, tiled=True)  13.6 us
    all_to_all x1, starting transfers between devices, on_device(): lax.all_to_all(grad, OWNERS + ('xl',), split_axis=0, concat_axis=1, tiled...  13.1 us
    pallas_call x6, Pallas kernels, call(): pl.pallas_call(kernel, out_shape=out_shape, in_specs=in_specs, out_specs=...  10.7 us
    all_to_all x1, waiting for transfers between devices, on_device(): lax.all_to_all(grad, OWNERS + ('xl',), split_axis=0, concat_axis=1, tiled...  10.3 us
    dynamic_update_slice x9, local copies, waits for them, and re-layouts, put(): return lax.dynamic_update_slice(params, chunk[:, None], (block, at, row, 0))  9.11 us
    ppermute x3, starting transfers between devices, swap(): return lax.ppermute(x, 'xl', SWAP)  9.1 us
  transfers between devices with their start and end apart: 20, of which 10 were waited for; matrix products, arithmetic and copies ran while one was open for 7% of the time, Pallas kernels for 4%

profile of v6, /device:TPU:68, one launch (start us, length us, event | category | flops | bytes accessed | tf_op | source)
XLA Modules:
  0.0 179.2 jit_solution(17747300137216788925)
XLA Ops:
  7.9 13.1 %all-to-all-start = ((bf16[64,2,1024]{2,1,0:T(2,128)(2,1)}), bf16[64,2,1024]{2,1,0:T(2,128)(2,1)S(1)}, u32[]{:S(2)}, u32[]{:S(2)}) async-start(bf16[64,2,1024]{2,1,0:T(2,128)(2,1)} %param.6), calls=%async_computation | async-start | bytes 524288 | tf_op jit(solution)/shard_map/all_to_all | solution.py:172
  22.3 10.3 %all-to-all-done = bf16[64,2,1024]{2,1,0:T(2,128)(2,1)S(1)} async-done(((bf16[64,2,1024]{2,1,0:T(2,128)(2,1)}), bf16[64,2,1024]{2,1,0:T(2,128)(2,1)S(1)}, u32[]{:S(2)}, u32[]{:S(2)}) %all-to-all-start) | async-done | bytes 262176 | tf_op jit(solution)/shard_map/all_to_all | solution.py:172
  32.9 3.5 %collective-permute-start.1 = (bf16[128,1024]{1,0:T(8,128)(2,1)S(1)}, bf16[128,1024]{1,0:T(8,128)(2,1)S(1)}, u32[]{:S(2)}, u32[]{:S(2)}) collective-permute-start(bf16[128,1024]{1,0:T(8,128)(2,1)S(1)} %reshape.32.refs_3_.mine), channel_id=1, source_target_pairs={{0,2},{2,4},{4,6},{6,8},{8,10},{10,12},{12,14},{14,0},{1,3},{3,5},... | collective-permute-start | bytes 786440 | tf_op jit(solution)/shard_map/ppermute | solution.py:29
  38.3 3.1 %collective-permute-start = (bf16[320,1024]{1,0:T(8,128)(2,1)}, bf16[320,1024]{1,0:T(8,128)(2,1)S(1)}, u32[]{:S(2)}, u32[]{:S(2)}) collective-permute-start(bf16[320,1024]{1,0:T(8,128)(2,1)} %bitcast.2), channel_id=1, source_target_pairs={{0,1},{1,0},{2,3},{3,2},{4,5},{5,4},{6,7},{7,6},{8,9},{9,8},{10,11... | collective-permute-start | bytes 1966088 | tf_op jit(solution)/shard_map/ppermute | solution.py:25
  41.4 3.8 %collective-permute-start.2 = (bf16[128,1024]{1,0:T(8,128)(2,1)S(1)}, bf16[128,1024]{1,0:T(8,128)(2,1)S(1)}, u32[]{:S(2)}, u32[]{:S(2)}) collective-permute-start(bf16[128,1024]{1,0:T(8,128)(2,1)S(1)} %reshape.32.refs_3_.mine), channel_id=1, source_target_pairs={{0,14},{2,0},{4,2},{6,4},{8,6},{10,8},{12,10},{14,12},{1,15},{3,1}... | collective-permute-start | bytes 786440 | tf_op jit(solution)/shard_map/ppermute | solution.py:29
  45.2 4.9 %collective-permute-done.1.refs_4_ = bf16[128,1024]{1,0:T(8,128)(2,1)S(1)} collective-permute-done((bf16[128,1024]{1,0:T(8,128)(2,1)S(1)}, bf16[128,1024]{1,0:T(8,128)(2,1)S(1)}, u32[]{:S(2)}, u32[]{:S(2)}) %collective-permute-start.1) | collective-permute-done | bytes 262176 | tf_op jit(solution)/shard_map/ppermute | solution.py:29
  52.0 4.7 %collective-permute-done.2.refs_5_ = bf16[128,1024]{1,0:T(8,128)(2,1)S(1)} collective-permute-done((bf16[128,1024]{1,0:T(8,128)(2,1)S(1)}, bf16[128,1024]{1,0:T(8,128)(2,1)S(1)}, u32[]{:S(2)}, u32[]{:S(2)}) %collective-permute-start.2) | collective-permute-done | bytes 262176 | tf_op jit(solution)/shard_map/ppermute | solution.py:29
  56.7 5.0 %collective-permute-start.4 = (bf16[128,1024]{1,0:T(8,128)(2,1)S(1)}, bf16[128,1024]{1,0:T(8,128)(2,1)S(1)}, u32[]{:S(2)}, u32[]{:S(2)}) collective-permute-start(bf16[128,1024]{1,0:T(8,128)(2,1)S(1)} %collective-permute-done.2.refs_5_), channel_id=1, source_target_pairs={{0,14},{2,0},{4,2},{6,4},{8,6},{10,8},{12,10},{14,12},{1,15},{3,1}... | collective-permute-start | bytes 786440 | tf_op jit(solution)/shard_map/ppermute | solution.py:29
  61.7 2.7 %collective-permute-done.3.refs_6_ = bf16[128,1024]{1,0:T(8,128)(2,1)S(1)} collective-permute-done((bf16[128,1024]{1,0:T(8,128)(2,1)S(1)}, bf16[128,1024]{1,0:T(8,128)(2,1)S(1)}, u32[]{:S(2)}, u32[]{:S(2)}) %collective-permute-start.3) | collective-permute-done | bytes 262176 | tf_op jit(solution)/shard_map/ppermute | solution.py:29
  64.4 2.2 %collective-permute-start.5 = (bf16[128,1024]{1,0:T(8,128)(2,1)S(1)}, bf16[128,1024]{1,0:T(8,128)(2,1)}, u32[]{:S(2)}, u32[]{:S(2)}) collective-permute-start(bf16[128,1024]{1,0:T(8,128)(2,1)S(1)} %collective-permute-done.3.refs_6_), channel_id=1, source_target_pairs={{0,2},{2,4},{4,6},{6,8},{8,10},{10,12},{12,14},{14,0},{1,3},{3,5},... | collective-permute-start | bytes 786440 | tf_op jit(solution)/shard_map/ppermute | solution.py:29
  67.3 3.1 %collective-permute-start.8 = (bf16[128,1024]{1,0:T(8,128)(2,1)S(1)}, bf16[128,1024]{1,0:T(8,128)(2,1)}, u32[]{:S(2)}, u32[]{:S(2)}) collective-permute-start(bf16[128,1024]{1,0:T(8,128)(2,1)S(1)} %reshape.32.refs_3_.mine), channel_id=1, source_target_pairs={{0,1},{1,0},{2,3},{3,2},{4,5},{5,4},{6,7},{7,6},{8,9},{9,8},{10,11... | collective-permute-start | bytes 786440 | tf_op jit(solution)/shard_map/ppermute | solution.py:25
  70.5 4.8 %collective-permute-start.6 = (bf16[128,1024]{1,0:T(8,128)(2,1)S(1)}, bf16[128,1024]{1,0:T(8,128)(2,1)}, u32[]{:S(2)}, u32[]{:S(2)}) collective-permute-start(bf16[128,1024]{1,0:T(8,128)(2,1)S(1)} %collective-permute-done.4.refs_7_), channel_id=1, source_target_pairs={{0,14},{2,0},{4,2},{6,4},{8,6},{10,8},{12,10},{14,12},{1,15},{3,1}... | collective-permute-start | bytes 786440 | tf_op jit(solution)/shard_map/ppermute | solution.py:29
  82.7 2.7 %collective-permute-done.7.refs_5_ = bf16[128,1024]{1,0:T(8,128)(2,1)} collective-permute-done((bf16[128,1024]{1,0:T(8,128)(2,1)}, bf16[128,1024]{1,0:T(8,128)(2,1)}, u32[]{:S(2)}, u32[]{:S(2)}) %collective-permute-start.7) | collective-permute-done | bytes 262176 | tf_op jit(solution)/shard_map/ppermute | solution.py:29
  86.7 7.0 %all-gather.1 = bf16[256,1024]{1,0:T(8,128)(2,1)S(1)} all-gather(bf16[128,1024]{1,0:T(8,128)(2,1)S(1)} %shard_map.95), channel_id=3, replica_groups=mesh['z'=8,'xh'=2,'c'=2,'y'=8,'xl'=2] {'xl'}, dimensions={0}, use_global_device_ids=true | all-gather | bytes 786432 | tf_op jit(solution)/shard_map/all_gather | solution.py:203
  95.3 2.9 %collective-permute-start.9 = (bf16[2,128,512]{2,1,0:T(8,128)(2,1)S(1)}, bf16[2,128,512]{2,1,0:T(8,128)(2,1)S(1)}, u32[]{:S(2)}, u32[]{:S(2)}) collective-permute-start(bf16[2,128,512]{2,1,0:T(8,128)(2,1)S(1)} %get-tuple-element.13.mine), channel_id=1, source_target_pairs={{0,1},{1,0},{2,3},{3,2},{4,5},{5,4},{6,7},{7,6},{8,9},{9,8},{10,11... | collective-permute-start | bytes 786440 | tf_op jit(solution)/shard_map/ppermute | solution.py:25
  98.2 13.6 %all_to_all.14.sums = f32[16,8,128]{2,1,0:T(8,128)S(1)} all-to-all(f32[16,8,128]{2,1,0:T(8,128)S(1)} %get-tuple-element.12), channel_id=1, replica_groups=mesh['z'=8,'xh'=2,'c'=2,'y'=8,'xl'=2] {'y','xl'}, dimensions={0} | all-to-all | bytes 131072 | tf_op jit(solution)/shard_map/all_to_all | solution.py:207
  114.9 5.0 %collective-permute-start.11 = (bf16[2,128,1024]{2,1,0:T(8,128)(2,1)S(1)}, bf16[2,128,1024]{2,1,0:T(8,128)(2,1)}, u32[]{:S(2)}, u32[]{:S(2)}) collective-permute-start(bf16[2,128,1024]{2,1,0:T(8,128)(2,1)S(1)} %shard_map.97.both), channel_id=1, source_target_pairs={{0,14},{2,0},{4,2},{6,4},{8,6},{10,8},{12,10},{14,12},{1,15},{3,1}... | collective-permute-start | bytes 1572872 | tf_op jit(solution)/shard_map/ppermute | solution.py:29
  119.8 7.3 %collective-permute-done.10 = bf16[2,128,1024]{2,1,0:T(8,128)(2,1)} collective-permute-done((bf16[2,128,1024]{2,1,0:T(8,128)(2,1)S(1)}, bf16[2,128,1024]{2,1,0:T(8,128)(2,1)}, u32[]{:S(2)}, u32[]{:S(2)}) %collective-permute-start.10) | collective-permute-done | bytes 524320 | tf_op jit(solution)/shard_map/ppermute | solution.py:29
  129.0 5.4 %collective-permute-start.13 = (bf16[2,128,1024]{2,1,0:T(8,128)(2,1)}, bf16[2,128,1024]{2,1,0:T(8,128)(2,1)S(1)}, u32[]{:S(2)}, u32[]{:S(2)}) collective-permute-start(bf16[2,128,1024]{2,1,0:T(8,128)(2,1)} %collective-permute-done.11), channel_id=1, source_target_pairs={{0,14},{2,0},{4,2},{6,4},{8,6},{10,8},{12,10},{14,12},{1,15},{3,1}... | collective-permute-start | bytes 1572872 | tf_op jit(solution)/shard_map/ppermute | solution.py:29
  134.5 3.3 %shard_map.98 = (f32[2,64,1024]{2,1,0:T(8,128)}, f32[2,64,1024]{2,1,0:T(8,128)}, bf16[2,8,128,1024]{3,2,1,0:T(8,128)(2,1)}) custom-call(s32[2]{0:T(128)S(1)} %pad_add_fusion.refs_0_.place, f32[16,8,128]{2,1,0:T(8,128)S(1)} %all_to_all.14.sums, bf16[2,128,512]{2,1,0:T(8,128)(2,1)S(1)} %get-tuple-element.13.mine, ...), custom_call_target="tpu_custom_call" | custom-call | bytes 4325392 | tf_op jit(solution)/shard_map/pallas_call | solution.py:145
  139.6 3.3 %collective-permute-done.12 = bf16[2,128,1024]{2,1,0:T(8,128)(2,1)S(1)} collective-permute-done((bf16[2,128,1024]{2,1,0:T(8,128)(2,1)}, bf16[2,128,1024]{2,1,0:T(8,128)(2,1)S(1)}, u32[]{:S(2)}, u32[]{:S(2)}) %collective-permute-start.12) | collective-permute-done | bytes 524320 | tf_op jit(solution)/shard_map/ppermute | solution.py:29
  145.0 5.5 %collective-permute-start.15 = (bf16[2,128,1024]{2,1,0:T(8,128)(2,1)S(1)}, bf16[2,128,1024]{2,1,0:T(8,128)(2,1)S(1)}, u32[]{:S(2)}, u32[]{:S(2)}) collective-permute-start(bf16[2,128,1024]{2,1,0:T(8,128)(2,1)S(1)} %collective-permute-done.13), channel_id=1, source_target_pairs={{0,14},{2,0},{4,2},{6,4},{8,6},{10,8},{12,10},{14,12},{1,15},{3,1}... | collective-permute-start | bytes 1572872 | tf_op jit(solution)/shard_map/ppermute | solution.py:29
  154.0 5.4 %collective-permute-done.14 = bf16[2,128,1024]{2,1,0:T(8,128)(2,1)S(1)} collective-permute-done((bf16[2,128,1024]{2,1,0:T(8,128)(2,1)S(1)}, bf16[2,128,1024]{2,1,0:T(8,128)(2,1)S(1)}, u32[]{:S(2)}, u32[]{:S(2)}) %collective-permute-start.14) | collective-permute-done | bytes 524320 | tf_op jit(solution)/shard_map/ppermute | solution.py:29
  161.4 5.1 %collective-permute-start.17 = (bf16[1,64,1024]{2,1,0:T(8,128)(2,1)S(1)}, bf16[1,64,1024]{2,1,0:T(8,128)(2,1)S(1)}, u32[]{:S(2)}, u32[]{:S(2)}) collective-permute-start(bf16[1,64,1024]{2,1,0:T(8,128)(2,1)S(1)} %slice.32), channel_id=1, source_target_pairs={{0,14},{2,0},{4,2},{6,4},{8,6},{10,8},{12,10},{14,12},{1,15},{3,1}... | collective-permute-start | bytes 393224 | tf_op jit(solution)/shard_map/ppermute | solution.py:29
  (58 shorter events, 37.4 us)
Async XLA Ops:
  7.2 70.2 %copy-start = (bf16[2,64,1024]{2,1,0:T(8,128)(2,1)S(1)}, bf16[2,64,1024]{2,1,0:T(8,128)(2,1)}, u32[]{:S(2)}) copy-start(bf16[2,64,1024]{2,1,0:T(8,128)(2,1)} %refs_1_.3) | copy-start | bytes 786436
  7.2 72.6 %all-gather.4.cloned.1.call-start = ((), (), s32[]{:S(2)}) async-start(), calls=%async_computation.2 | async-start | bytes 2359296 | tf_op jit(solution)/shard_map/all_gather | solution.py:163
  7.9 72.8 %copy-start.4 = (f32[2,64,1024]{2,1,0:T(8,128)S(1)}, f32[2,64,1024]{2,1,0:T(8,128)}, u32[]{:S(2)}) copy-start(f32[2,64,1024]{2,1,0:T(8,128)} %second.1) | copy-start | bytes 1572868
  7.9 24.7 %all-to-all-start = ((bf16[64,2,1024]{2,1,0:T(2,128)(2,1)}), bf16[64,2,1024]{2,1,0:T(2,128)(2,1)S(1)}, u32[]{:S(2)}, u32[]{:S(2)}) async-start(bf16[64,2,1024]{2,1,0:T(2,128)(2,1)} %param.6), calls=%async_computation | async-start | bytes 524288 | tf_op jit(solution)/shard_map/all_to_all | solution.py:172
  32.9 17.2 %collective-permute-start.1 = (bf16[128,1024]{1,0:T(8,128)(2,1)S(1)}, bf16[128,1024]{1,0:T(8,128)(2,1)S(1)}, u32[]{:S(2)}, u32[]{:S(2)}) collective-permute-start(bf16[128,1024]{1,0:T(8,128)(2,1)S(1)} %reshape.32.refs_3_.mine), channel_id=1, source_target_pairs={{0,2},{2,4},{4,6},{6,8},{8,10},{10,12},{12,14},{14,0},{1,3},{3,5},... | collective-permute-start | bytes 786440 | tf_op jit(solution)/shard_map/ppermute | solution.py:29
  38.3 39.0 %collective-permute-start = (bf16[320,1024]{1,0:T(8,128)(2,1)}, bf16[320,1024]{1,0:T(8,128)(2,1)S(1)}, u32[]{:S(2)}, u32[]{:S(2)}) collective-permute-start(bf16[320,1024]{1,0:T(8,128)(2,1)} %bitcast.2), channel_id=1, source_target_pairs={{0,1},{1,0},{2,3},{3,2},{4,5},{5,4},{6,7},{7,6},{8,9},{9,8},{10,11... | collective-permute-start | bytes 1966088 | tf_op jit(solution)/shard_map/ppermute | solution.py:25
  41.4 15.3 %collective-permute-start.2 = (bf16[128,1024]{1,0:T(8,128)(2,1)S(1)}, bf16[128,1024]{1,0:T(8,128)(2,1)S(1)}, u32[]{:S(2)}, u32[]{:S(2)}) collective-permute-start(bf16[128,1024]{1,0:T(8,128)(2,1)S(1)} %reshape.32.refs_3_.mine), channel_id=1, source_target_pairs={{0,14},{2,0},{4,2},{6,4},{8,6},{10,8},{12,10},{14,12},{1,15},{3,1}... | collective-permute-start | bytes 786440 | tf_op jit(solution)/shard_map/ppermute | solution.py:29
  50.1 14.3 %collective-permute-start.3 = (bf16[128,1024]{1,0:T(8,128)(2,1)S(1)}, bf16[128,1024]{1,0:T(8,128)(2,1)S(1)}, u32[]{:S(2)}, u32[]{:S(2)}) collective-permute-start(bf16[128,1024]{1,0:T(8,128)(2,1)S(1)} %collective-permute-done.1.refs_4_), channel_id=1, source_target_pairs={{0,2},{2,4},{4,6},{6,8},{8,10},{10,12},{12,14},{14,0},{1,3},{3,5},... | collective-permute-start | bytes 786440 | tf_op jit(solution)/shard_map/ppermute | solution.py:29
  56.7 13.8 %collective-permute-start.4 = (bf16[128,1024]{1,0:T(8,128)(2,1)S(1)}, bf16[128,1024]{1,0:T(8,128)(2,1)S(1)}, u32[]{:S(2)}, u32[]{:S(2)}) collective-permute-start(bf16[128,1024]{1,0:T(8,128)(2,1)S(1)} %collective-permute-done.2.refs_5_), channel_id=1, source_target_pairs={{0,14},{2,0},{4,2},{6,4},{8,6},{10,8},{12,10},{14,12},{1,15},{3,1}... | collective-permute-start | bytes 786440 | tf_op jit(solution)/shard_map/ppermute | solution.py:29
  64.4 10.9 %collective-permute-start.5 = (bf16[128,1024]{1,0:T(8,128)(2,1)S(1)}, bf16[128,1024]{1,0:T(8,128)(2,1)}, u32[]{:S(2)}, u32[]{:S(2)}) collective-permute-start(bf16[128,1024]{1,0:T(8,128)(2,1)S(1)} %collective-permute-done.3.refs_6_), channel_id=1, source_target_pairs={{0,2},{2,4},{4,6},{6,8},{8,10},{10,12},{12,14},{14,0},{1,3},{3,5},... | collective-permute-start | bytes 786440 | tf_op jit(solution)/shard_map/ppermute | solution.py:29
  67.3 13.3 %collective-permute-start.8 = (bf16[128,1024]{1,0:T(8,128)(2,1)S(1)}, bf16[128,1024]{1,0:T(8,128)(2,1)}, u32[]{:S(2)}, u32[]{:S(2)}) collective-permute-start(bf16[128,1024]{1,0:T(8,128)(2,1)S(1)} %reshape.32.refs_3_.mine), channel_id=1, source_target_pairs={{0,1},{1,0},{2,3},{3,2},{4,5},{5,4},{6,7},{7,6},{8,9},{9,8},{10,11... | collective-permute-start | bytes 786440 | tf_op jit(solution)/shard_map/ppermute | solution.py:25
  70.5 12.2 %collective-permute-start.6 = (bf16[128,1024]{1,0:T(8,128)(2,1)S(1)}, bf16[128,1024]{1,0:T(8,128)(2,1)}, u32[]{:S(2)}, u32[]{:S(2)}) collective-permute-start(bf16[128,1024]{1,0:T(8,128)(2,1)S(1)} %collective-permute-done.4.refs_7_), channel_id=1, source_target_pairs={{0,14},{2,0},{4,2},{6,4},{8,6},{10,8},{12,10},{14,12},{1,15},{3,1}... | collective-permute-start | bytes 786440 | tf_op jit(solution)/shard_map/ppermute | solution.py:29
  75.3 10.1 %collective-permute-start.7 = (bf16[128,1024]{1,0:T(8,128)(2,1)}, bf16[128,1024]{1,0:T(8,128)(2,1)}, u32[]{:S(2)}, u32[]{:S(2)}) collective-permute-start(bf16[128,1024]{1,0:T(8,128)(2,1)} %collective-permute-done.5.refs_8_), channel_id=1, source_target_pairs={{0,2},{2,4},{4,6},{6,8},{8,10},{10,12},{12,14},{14,0},{1,3},{3,5},... | collective-permute-start | bytes 786440 | tf_op jit(solution)/shard_map/ppermute | solution.py:29
  82.7 51.8 %copy-start.2 = (f32[2,64,1024]{2,1,0:T(8,128)S(1)}, f32[2,64,1024]{2,1,0:T(8,128)}, u32[]{:S(2)}) copy-start(f32[2,64,1024]{2,1,0:T(8,128)} %master.1) | copy-start | bytes 1572868
  82.7 51.8 %copy-start.3 = (f32[2,64,1024]{2,1,0:T(8,128)S(1)}, f32[2,64,1024]{2,1,0:T(8,128)}, u32[]{:S(2)}) copy-start(f32[2,64,1024]{2,1,0:T(8,128)} %momentum.1) | copy-start | bytes 1572868
  95.3 16.5 %collective-permute-start.9 = (bf16[2,128,512]{2,1,0:T(8,128)(2,1)S(1)}, bf16[2,128,512]{2,1,0:T(8,128)(2,1)S(1)}, u32[]{:S(2)}, u32[]{:S(2)}) collective-permute-start(bf16[2,128,512]{2,1,0:T(8,128)(2,1)S(1)} %get-tuple-element.13.mine), channel_id=1, source_target_pairs={{0,1},{1,0},{2,3},{3,2},{4,5},{5,4},{6,7},{7,6},{8,9},{9,8},{10,11... | collective-permute-start | bytes 786440 | tf_op jit(solution)/shard_map/ppermute | solution.py:25
  112.8 14.3 %collective-permute-start.10 = (bf16[2,128,1024]{2,1,0:T(8,128)(2,1)S(1)}, bf16[2,128,1024]{2,1,0:T(8,128)(2,1)}, u32[]{:S(2)}, u32[]{:S(2)}) collective-permute-start(bf16[2,128,1024]{2,1,0:T(8,128)(2,1)S(1)} %shard_map.97.both), channel_id=1, source_target_pairs={{0,2},{2,4},{4,6},{6,8},{8,10},{10,12},{12,14},{14,0},{1,3},{3,5},... | collective-permute-start | bytes 1572872 | tf_op jit(solution)/shard_map/ppermute | solution.py:29
  114.9 14.1 %collective-permute-start.11 = (bf16[2,128,1024]{2,1,0:T(8,128)(2,1)S(1)}, bf16[2,128,1024]{2,1,0:T(8,128)(2,1)}, u32[]{:S(2)}, u32[]{:S(2)}) collective-permute-start(bf16[2,128,1024]{2,1,0:T(8,128)(2,1)S(1)} %shard_map.97.both), channel_id=1, source_target_pairs={{0,14},{2,0},{4,2},{6,4},{8,6},{10,8},{12,10},{14,12},{1,15},{3,1}... | collective-permute-start | bytes 1572872 | tf_op jit(solution)/shard_map/ppermute | solution.py:29
  127.1 15.8 %collective-permute-start.12 = (bf16[2,128,1024]{2,1,0:T(8,128)(2,1)}, bf16[2,128,1024]{2,1,0:T(8,128)(2,1)S(1)}, u32[]{:S(2)}, u32[]{:S(2)}) collective-permute-start(bf16[2,128,1024]{2,1,0:T(8,128)(2,1)} %collective-permute-done.10), channel_id=1, source_target_pairs={{0,2},{2,4},{4,6},{6,8},{8,10},{10,12},{12,14},{14,0},{1,3},{3,5},... | collective-permute-start | bytes 1572872 | tf_op jit(solution)/shard_map/ppermute | solution.py:29
  129.0 16.0 %collective-permute-start.13 = (bf16[2,128,1024]{2,1,0:T(8,128)(2,1)}, bf16[2,128,1024]{2,1,0:T(8,128)(2,1)S(1)}, u32[]{:S(2)}, u32[]{:S(2)}) collective-permute-start(bf16[2,128,1024]{2,1,0:T(8,128)(2,1)} %collective-permute-done.11), channel_id=1, source_target_pairs={{0,14},{2,0},{4,2},{6,4},{8,6},{10,8},{12,10},{14,12},{1,15},{3,1}... | collective-permute-start | bytes 1572872 | tf_op jit(solution)/shard_map/ppermute | solution.py:29
  142.9 16.5 %collective-permute-start.14 = (bf16[2,128,1024]{2,1,0:T(8,128)(2,1)S(1)}, bf16[2,128,1024]{2,1,0:T(8,128)(2,1)S(1)}, u32[]{:S(2)}, u32[]{:S(2)}) collective-permute-start(bf16[2,128,1024]{2,1,0:T(8,128)(2,1)S(1)} %collective-permute-done.12), channel_id=1, source_target_pairs={{0,2},{2,4},{4,6},{6,8},{8,10},{10,12},{12,14},{14,0},{1,3},{3,5},... | collective-permute-start | bytes 1572872 | tf_op jit(solution)/shard_map/ppermute | solution.py:29
  145.0 16.3 %collective-permute-start.15 = (bf16[2,128,1024]{2,1,0:T(8,128)(2,1)S(1)}, bf16[2,128,1024]{2,1,0:T(8,128)(2,1)S(1)}, u32[]{:S(2)}, u32[]{:S(2)}) collective-permute-start(bf16[2,128,1024]{2,1,0:T(8,128)(2,1)S(1)} %collective-permute-done.13), channel_id=1, source_target_pairs={{0,14},{2,0},{4,2},{6,4},{8,6},{10,8},{12,10},{14,12},{1,15},{3,1}... | collective-permute-start | bytes 1572872 | tf_op jit(solution)/shard_map/ppermute | solution.py:29
  159.4 10.9 %collective-permute-start.16 = (bf16[3,64,1024]{2,1,0:T(8,128)(2,1)S(1)}, bf16[3,64,1024]{2,1,0:T(8,128)(2,1)S(1)}, u32[]{:S(2)}, u32[]{:S(2)}) collective-permute-start(bf16[3,64,1024]{2,1,0:T(8,128)(2,1)S(1)} %slice.29), channel_id=1, source_target_pairs={{0,2},{2,4},{4,6},{6,8},{8,10},{10,12},{12,14},{14,0},{1,3},{3,5},... | collective-permute-start | bytes 1179656 | tf_op jit(solution)/shard_map/ppermute | solution.py:29
  161.4 10.3 %collective-permute-start.17 = (bf16[1,64,1024]{2,1,0:T(8,128)(2,1)S(1)}, bf16[1,64,1024]{2,1,0:T(8,128)(2,1)S(1)}, u32[]{:S(2)}, u32[]{:S(2)}) collective-permute-start(bf16[1,64,1024]{2,1,0:T(8,128)(2,1)S(1)} %slice.32), channel_id=1, source_target_pairs={{0,14},{2,0},{4,2},{6,4},{8,6},{10,8},{12,10},{14,12},{1,15},{3,1}... | collective-permute-start | bytes 393224 | tf_op jit(solution)/shard_map/ppermute | solution.py:29
  (3 other events, 15.6 us)
Sparse Core Ops, SparseCore 0:
  10.1 53.6 all-gather.3

commit v7 on v6

--- a/solution.py
+++ b/solution.py
@@ -29,12 +29,12 @@
     return lax.ppermute(x, "y", [(i, (i + way) % Y) for i in range(Y)])
 
 
-def adam_kernel(place, mine, theirs, second, *refs):
+def adam_kernel(place, mine, swapped, second, *refs):
     new_second, squares = refs[-2:]
     rows = second.shape[1]
     half = place[1]
     ours = mine[pl.ds(pl.multiple_of(half * rows, rows), rows), :]
-    others = theirs[pl.ds(pl.multiple_of(half * rows, rows), rows), :]
+    others = swapped[5 * rows :, :]
     for block in range(2):
         grad = jnp.where(half == block, ours, others).astype(jnp.float32)
         moment = second_decay * second[block] + (1.0 - second_decay) * grad * grad
@@ -154,6 +154,10 @@
     )(*operands)
 
 
+def later(place, x, *ready):
+    return call(lambda *refs: None, (), (place,), ready=ready, through=x)[0]
+
+
 def on_device(grad, left_root, right_root, master, momentum, second):
     place = jnp.stack([lax.axis_index("y"), lax.axis_index("xl")])
     _, rows, width = master.shape
@@ -167,19 +171,22 @@
     low = (value - high.astype(f32)).astype(bf16)
     base = high.astype(f32) + low.astype(f32)
     left_away = jnp.where(place[1] == 0, left_root[1], left_root[0])
-    swapped = swap(jnp.concatenate([left_away[None], high, low]).reshape(5 * rows, width))
 
     spread = lax.all_to_all(grad, OWNERS + ("xl",), split_axis=0, concat_axis=1, tiled=True)
     pair = spread.reshape(-1, 2, grad.shape[1], width).swapaxes(0, 1).reshape(2 * rows, width)
 
+    pair = later(place, pair, left_away, high, low, base)
     up1, down1 = hop(pair, 1), hop(pair, -1)
+    halves = pair.reshape(2, rows, width)
+    pair_away = jnp.where(place[1] == 0, halves[1], halves[0])
+    swapped = swap(jnp.concatenate([left_away[None], high, low, pair_away[None]]).reshape(6 * rows, width))
     up2, down2 = hop(up1, 1), hop(down1, -1)
     up3, down3 = hop(up2, 1), hop(down2, -1)
     up4 = hop(up3, 1)
     new_second, squares = call(
         adam_kernel,
         (shape(second.shape, f32), shape((2, 8, 128), f32)),
-        (place, pair, swap(pair), second),
+        (place, pair, swapped, second),
         ready=(right[0, 0, :16, :128],),
     )
 

time: 180 us -> 178 us (0.989)
  the two profiles are of different devices: /device:TPU:68 before, /device:TPU:56 now
where the time goes in v7:
time: 178 us; the launch traced here: 175 us
  starting transfers between devices  71.7 us (40%)
  waiting for transfers between devices  42.1 us (24%)
  blocking collectives  22.5 us (13%)
  between operations  14.4 us (8%)
  Pallas kernels  10.9 us (6%)
  local copies, waits for them, and re-layouts  10.3 us (6%)
  other arithmetic  3.49 us (2%)
    ppermute x15, starting transfers between devices, hop(): return lax.ppermute(x, 'y', [(i, (i + way) % Y) for i in range(Y)])  52.4 us
    ppermute x15, waiting for transfers between devices, hop(): return lax.ppermute(x, 'y', [(i, (i + way) % Y) for i in range(Y)])  32 us
    all_to_all x1, blocking collectives, on_device(): sums = lax.all_to_all(sums, GROUP, split_axis=0, concat_axis=0, tiled=True)  15.4 us
    all_to_all x1, starting transfers between devices, on_device(): lax.all_to_all(grad, OWNERS + ('xl',), split_axis=0, concat_axis=1, tiled...  13.8 us
    pallas_call x7, Pallas kernels, call(): pl.pallas_call(kernel, out_shape=out_shape, in_specs=in_specs, out_specs=...  10.9 us
    all_to_all x1, waiting for transfers between devices, on_device(): lax.all_to_all(grad, OWNERS + ('xl',), split_axis=0, concat_axis=1, tiled...  9.37 us
    dynamic_update_slice x9, local copies, waits for them, and re-layouts, put(): return lax.dynamic_update_slice(params, chunk[:, None], (block, at, row, 0))  9.11 us
    all_gather x1, blocking collectives, on_device(): lax.all_gather(left_grad, 'xl', axis=0, tiled=False)  7.05 us
  transfers between devices with their start and end apart: 19, of which 13 were waited for; matrix products, arithmetic and copies ran while one was open for 7% of the time, Pallas kernels for 4%

profile of v7, /device:TPU:56, one launch (start us, length us, event | category | flops | bytes accessed | tf_op | source)
XLA Modules:
  0.0 175.4 jit_solution(5839829604872348127)
XLA Ops:
  7.9 13.8 %all-to-all-start = ((bf16[64,2,1024]{2,1,0:T(2,128)(2,1)}), bf16[64,2,1024]{2,1,0:T(2,128)(2,1)S(1)}, u32[]{:S(2)}, u32[]{:S(2)}) async-start(bf16[64,2,1024]{2,1,0:T(2,128)(2,1)} %param.6), calls=%async_computation | async-start | bytes 524288 | tf_op jit(solution)/shard_map/all_to_all | solution.py:175
  25.1 9.4 %all-to-all-done = bf16[64,2,1024]{2,1,0:T(2,128)(2,1)S(1)} async-done(((bf16[64,2,1024]{2,1,0:T(2,128)(2,1)}), bf16[64,2,1024]{2,1,0:T(2,128)(2,1)S(1)}, u32[]{:S(2)}, u32[]{:S(2)}) %all-to-all-start) | async-done | bytes 262176 | tf_op jit(solution)/shard_map/all_to_all | solution.py:175
  37.4 2.6 %collective-permute-start = (bf16[384,1024]{1,0:T(8,128)(2,1)S(1)}, bf16[384,1024]{1,0:T(8,128)(2,1)S(1)}, u32[]{:S(2)}, u32[]{:S(2)}) collective-permute-start(bf16[384,1024]{1,0:T(8,128)(2,1)S(1)} %bitcast.53), channel_id=1, source_target_pairs={{0,1},{1,0},{2,3},{3,2},{4,5},{5,4},{6,7},{7,6},{8,9},{9,8},{10,11... | collective-permute-start | bytes 2359304 | tf_op jit(solution)/shard_map/ppermute | solution.py:25
  40.0 3.9 %collective-permute-start.2 = (bf16[128,1024]{1,0:T(8,128)(2,1)S(1)}, bf16[128,1024]{1,0:T(8,128)(2,1)S(1)}, u32[]{:S(2)}, u32[]{:S(2)}) collective-permute-start(bf16[128,1024]{1,0:T(8,128)(2,1)S(1)} %shard_map.93.refs_3_.mine), channel_id=1, source_target_pairs={{0,14},{2,0},{4,2},{6,4},{8,6},{10,8},{12,10},{14,12},{1,15},{3,1}... | collective-permute-start | bytes 786440 | tf_op jit(solution)/shard_map/ppermute | solution.py:29
  44.0 7.5 %collective-permute-done.1.refs_4_ = bf16[128,1024]{1,0:T(8,128)(2,1)S(1)} collective-permute-done((bf16[128,1024]{1,0:T(8,128)(2,1)S(1)}, bf16[128,1024]{1,0:T(8,128)(2,1)S(1)}, u32[]{:S(2)}, u32[]{:S(2)}) %collective-permute-start.1) | collective-permute-done | bytes 262176 | tf_op jit(solution)/shard_map/ppermute | solution.py:29
  51.5 3.3 %collective-permute-start.3 = (bf16[128,1024]{1,0:T(8,128)(2,1)S(1)}, bf16[128,1024]{1,0:T(8,128)(2,1)S(1)}, u32[]{:S(2)}, u32[]{:S(2)}) collective-permute-start(bf16[128,1024]{1,0:T(8,128)(2,1)S(1)} %collective-permute-done.1.refs_4_), channel_id=1, source_target_pairs={{0,2},{2,4},{4,6},{6,8},{8,10},{10,12},{12,14},{14,0},{1,3},{3,5},... | collective-permute-start | bytes 786440 | tf_op jit(solution)/shard_map/ppermute | solution.py:29
  54.8 2.2 %collective-permute-done.2.refs_5_ = bf16[128,1024]{1,0:T(8,128)(2,1)S(1)} collective-permute-done((bf16[128,1024]{1,0:T(8,128)(2,1)S(1)}, bf16[128,1024]{1,0:T(8,128)(2,1)S(1)}, u32[]{:S(2)}, u32[]{:S(2)}) %collective-permute-start.2) | collective-permute-done | bytes 262176 | tf_op jit(solution)/shard_map/ppermute | solution.py:29
  57.0 2.5 %collective-permute-start.4 = (bf16[128,1024]{1,0:T(8,128)(2,1)S(1)}, bf16[128,1024]{1,0:T(8,128)(2,1)S(1)}, u32[]{:S(2)}, u32[]{:S(2)}) collective-permute-start(bf16[128,1024]{1,0:T(8,128)(2,1)S(1)} %collective-permute-done.2.refs_5_), channel_id=1, source_target_pairs={{0,14},{2,0},{4,2},{6,4},{8,6},{10,8},{12,10},{14,12},{1,15},{3,1}... | collective-permute-start | bytes 786440 | tf_op jit(solution)/shard_map/ppermute | solution.py:29
  59.5 3.3 %collective-permute-done.3.refs_6_ = bf16[128,1024]{1,0:T(8,128)(2,1)S(1)} collective-permute-done((bf16[128,1024]{1,0:T(8,128)(2,1)S(1)}, bf16[128,1024]{1,0:T(8,128)(2,1)S(1)}, u32[]{:S(2)}, u32[]{:S(2)}) %collective-permute-start.3) | collective-permute-done | bytes 262176 | tf_op jit(solution)/shard_map/ppermute | solution.py:29
  62.8 4.6 %collective-permute-start.5 = (bf16[128,1024]{1,0:T(8,128)(2,1)S(1)}, bf16[128,1024]{1,0:T(8,128)(2,1)}, u32[]{:S(2)}, u32[]{:S(2)}) collective-permute-start(bf16[128,1024]{1,0:T(8,128)(2,1)S(1)} %collective-permute-done.3.refs_6_), channel_id=1, source_target_pairs={{0,2},{2,4},{4,6},{6,8},{8,10},{10,12},{12,14},{14,0},{1,3},{3,5},... | collective-permute-start | bytes 786440 | tf_op jit(solution)/shard_map/ppermute | solution.py:29
  67.4 1.9 %collective-permute-start.6 = (bf16[128,1024]{1,0:T(8,128)(2,1)S(1)}, bf16[128,1024]{1,0:T(8,128)(2,1)}, u32[]{:S(2)}, u32[]{:S(2)}) collective-permute-start(bf16[128,1024]{1,0:T(8,128)(2,1)S(1)} %collective-permute-done.4.refs_7_), channel_id=1, source_target_pairs={{0,14},{2,0},{4,2},{6,4},{8,6},{10,8},{12,10},{14,12},{1,15},{3,1}... | collective-permute-start | bytes 786440 | tf_op jit(solution)/shard_map/ppermute | solution.py:29
  69.4 3.6 %collective-permute-done.5.refs_8_ = bf16[128,1024]{1,0:T(8,128)(2,1)} collective-permute-done((bf16[128,1024]{1,0:T(8,128)(2,1)S(1)}, bf16[128,1024]{1,0:T(8,128)(2,1)}, u32[]{:S(2)}, u32[]{:S(2)}) %collective-permute-start.5) | collective-permute-done | bytes 262176 | tf_op jit(solution)/shard_map/ppermute | solution.py:29
  72.9 5.7 %collective-permute-start.7 = (bf16[128,1024]{1,0:T(8,128)(2,1)}, bf16[128,1024]{1,0:T(8,128)(2,1)}, u32[]{:S(2)}, u32[]{:S(2)}) collective-permute-start(bf16[128,1024]{1,0:T(8,128)(2,1)} %collective-permute-done.5.refs_8_), channel_id=1, source_target_pairs={{0,2},{2,4},{4,6},{6,8},{8,10},{10,12},{12,14},{14,0},{1,3},{3,5},... | collective-permute-start | bytes 786440 | tf_op jit(solution)/shard_map/ppermute | solution.py:29
  85.0 7.0 %all-gather.1 = bf16[256,1024]{1,0:T(8,128)(2,1)S(1)} all-gather(bf16[128,1024]{1,0:T(8,128)(2,1)S(1)} %shard_map.96), channel_id=3, replica_groups=mesh['z'=8,'xh'=2,'c'=2,'y'=8,'xl'=2] {'xl'}, dimensions={0}, use_global_device_ids=true | all-gather | bytes 786432 | tf_op jit(solution)/shard_map/all_gather | solution.py:210
  93.5 2.9 %collective-permute-start.8 = (bf16[2,128,512]{2,1,0:T(8,128)(2,1)S(1)}, bf16[2,128,512]{2,1,0:T(8,128)(2,1)S(1)}, u32[]{:S(2)}, u32[]{:S(2)}) collective-permute-start(bf16[2,128,512]{2,1,0:T(8,128)(2,1)S(1)} %get-tuple-element.13.mine), channel_id=1, source_target_pairs={{0,1},{1,0},{2,3},{3,2},{4,5},{5,4},{6,7},{7,6},{8,9},{9,8},{10,11... | collective-permute-start | bytes 786440 | tf_op jit(solution)/shard_map/ppermute | solution.py:25
  96.4 15.4 %all_to_all.14.sums = f32[16,8,128]{2,1,0:T(8,128)S(1)} all-to-all(f32[16,8,128]{2,1,0:T(8,128)S(1)} %get-tuple-element.12), channel_id=1, replica_groups=mesh['z'=8,'xh'=2,'c'=2,'y'=8,'xl'=2] {'y','xl'}, dimensions={0} | all-to-all | bytes 131072 | tf_op jit(solution)/shard_map/all_to_all | solution.py:214
  112.9 4.7 %collective-permute-start.9 = (bf16[2,128,1024]{2,1,0:T(8,128)(2,1)S(1)}, bf16[2,128,1024]{2,1,0:T(8,128)(2,1)}, u32[]{:S(2)}, u32[]{:S(2)}) collective-permute-start(bf16[2,128,1024]{2,1,0:T(8,128)(2,1)S(1)} %shard_map.98.both), channel_id=1, source_target_pairs={{0,2},{2,4},{4,6},{6,8},{8,10},{10,12},{12,14},{14,0},{1,3},{3,5},... | collective-permute-start | bytes 1572872 | tf_op jit(solution)/shard_map/ppermute | solution.py:29
  117.5 1.9 %collective-permute-start.10 = (bf16[2,128,1024]{2,1,0:T(8,128)(2,1)S(1)}, bf16[2,128,1024]{2,1,0:T(8,128)(2,1)}, u32[]{:S(2)}, u32[]{:S(2)}) collective-permute-start(bf16[2,128,1024]{2,1,0:T(8,128)(2,1)S(1)} %shard_map.98.both), channel_id=1, source_target_pairs={{0,14},{2,0},{4,2},{6,4},{8,6},{10,8},{12,10},{14,12},{1,15},{3,1}... | collective-permute-start | bytes 1572872 | tf_op jit(solution)/shard_map/ppermute | solution.py:29
  119.5 5.7 %collective-permute-done.9 = bf16[2,128,1024]{2,1,0:T(8,128)(2,1)} collective-permute-done((bf16[2,128,1024]{2,1,0:T(8,128)(2,1)S(1)}, bf16[2,128,1024]{2,1,0:T(8,128)(2,1)}, u32[]{:S(2)}, u32[]{:S(2)}) %collective-permute-start.9) | collective-permute-done | bytes 524320 | tf_op jit(solution)/shard_map/ppermute | solution.py:29
  125.2 5.1 %collective-permute-start.11 = (bf16[2,128,1024]{2,1,0:T(8,128)(2,1)}, bf16[2,128,1024]{2,1,0:T(8,128)(2,1)S(1)}, u32[]{:S(2)}, u32[]{:S(2)}) collective-permute-start(bf16[2,128,1024]{2,1,0:T(8,128)(2,1)} %collective-permute-done.9), channel_id=1, source_target_pairs={{0,2},{2,4},{4,6},{6,8},{8,10},{10,12},{12,14},{14,0},{1,3},{3,5},... | collective-permute-start | bytes 1572872 | tf_op jit(solution)/shard_map/ppermute | solution.py:29
  132.6 3.3 %shard_map.99 = (f32[2,64,1024]{2,1,0:T(8,128)}, f32[2,64,1024]{2,1,0:T(8,128)}, bf16[2,8,128,1024]{3,2,1,0:T(8,128)(2,1)}) custom-call(s32[2]{0:T(128)S(1)} %pad_add_fusion.refs_0_.place, f32[16,8,128]{2,1,0:T(8,128)S(1)} %all_to_all.14.sums, bf16[2,128,512]{2,1,0:T(8,128)(2,1)S(1)} %get-tuple-element.13.mine, ...), custom_call_target="tpu_custom_call" | custom-call | bytes 4325392 | tf_op jit(solution)/shard_map/pallas_call | solution.py:145
  139.1 5.5 %collective-permute-start.13 = (bf16[2,128,1024]{2,1,0:T(8,128)(2,1)S(1)}, bf16[2,128,1024]{2,1,0:T(8,128)(2,1)S(1)}, u32[]{:S(2)}, u32[]{:S(2)}) collective-permute-start(bf16[2,128,1024]{2,1,0:T(8,128)(2,1)S(1)} %collective-permute-done.11), channel_id=1, source_target_pairs={{0,2},{2,4},{4,6},{6,8},{8,10},{10,12},{12,14},{14,0},{1,3},{3,5},... | collective-permute-start | bytes 1572872 | tf_op jit(solution)/shard_map/ppermute | solution.py:29
  150.6 3.5 %collective-permute-done.13 = bf16[2,128,1024]{2,1,0:T(8,128)(2,1)S(1)} collective-permute-done((bf16[2,128,1024]{2,1,0:T(8,128)(2,1)S(1)}, bf16[2,128,1024]{2,1,0:T(8,128)(2,1)S(1)}, u32[]{:S(2)}, u32[]{:S(2)}) %collective-permute-start.13) | collective-permute-done | bytes 524320 | tf_op jit(solution)/shard_map/ppermute | solution.py:29
  154.2 5.6 %collective-permute-start.15 = (bf16[3,64,1024]{2,1,0:T(8,128)(2,1)S(1)}, bf16[3,64,1024]{2,1,0:T(8,128)(2,1)S(1)}, u32[]{:S(2)}, u32[]{:S(2)}) collective-permute-start(bf16[3,64,1024]{2,1,0:T(8,128)(2,1)S(1)} %slice.41), channel_id=1, source_target_pairs={{0,2},{2,4},{4,6},{6,8},{8,10},{10,12},{12,14},{14,0},{1,3},{3,5},... | collective-permute-start | bytes 1179656 | tf_op jit(solution)/shard_map/ppermute | solution.py:29
  (55 shorter events, 36.0 us)
Async XLA Ops:
  7.2 71.5 %copy-start = (bf16[2,64,1024]{2,1,0:T(8,128)(2,1)S(1)}, bf16[2,64,1024]{2,1,0:T(8,128)(2,1)}, u32[]{:S(2)}) copy-start(bf16[2,64,1024]{2,1,0:T(8,128)(2,1)} %refs_1_.3) | copy-start | bytes 786436
  7.2 73.0 %all-gather.4.cloned.1.call-start = ((), (), s32[]{:S(2)}) async-start(), calls=%async_computation.2 | async-start | bytes 2359296 | tf_op jit(solution)/shard_map/all_gather | solution.py:167
  7.9 26.6 %all-to-all-start = ((bf16[64,2,1024]{2,1,0:T(2,128)(2,1)}), bf16[64,2,1024]{2,1,0:T(2,128)(2,1)S(1)}, u32[]{:S(2)}, u32[]{:S(2)}) async-start(bf16[64,2,1024]{2,1,0:T(2,128)(2,1)} %param.6), calls=%async_computation | async-start | bytes 524288 | tf_op jit(solution)/shard_map/all_to_all | solution.py:175
  25.1 55.9 %copy-start.4 = (f32[2,64,1024]{2,1,0:T(8,128)S(1)}, f32[2,64,1024]{2,1,0:T(8,128)}, u32[]{:S(2)}) copy-start(f32[2,64,1024]{2,1,0:T(8,128)} %second.1) | copy-start | bytes 1572868
  35.3 16.2 %collective-permute-start.1 = (bf16[128,1024]{1,0:T(8,128)(2,1)S(1)}, bf16[128,1024]{1,0:T(8,128)(2,1)S(1)}, u32[]{:S(2)}, u32[]{:S(2)}) collective-permute-start(bf16[128,1024]{1,0:T(8,128)(2,1)S(1)} %shard_map.93.refs_3_.mine), channel_id=1, source_target_pairs={{0,2},{2,4},{4,6},{6,8},{8,10},{10,12},{12,14},{14,0},{1,3},{3,5},... | collective-permute-start | bytes 786440 | tf_op jit(solution)/shard_map/ppermute | solution.py:29
  37.4 41.2 %collective-permute-start = (bf16[384,1024]{1,0:T(8,128)(2,1)S(1)}, bf16[384,1024]{1,0:T(8,128)(2,1)S(1)}, u32[]{:S(2)}, u32[]{:S(2)}) collective-permute-start(bf16[384,1024]{1,0:T(8,128)(2,1)S(1)} %bitcast.53), channel_id=1, source_target_pairs={{0,1},{1,0},{2,3},{3,2},{4,5},{5,4},{6,7},{7,6},{8,9},{9,8},{10,11... | collective-permute-start | bytes 2359304 | tf_op jit(solution)/shard_map/ppermute | solution.py:25
  40.0 16.9 %collective-permute-start.2 = (bf16[128,1024]{1,0:T(8,128)(2,1)S(1)}, bf16[128,1024]{1,0:T(8,128)(2,1)S(1)}, u32[]{:S(2)}, u32[]{:S(2)}) collective-permute-start(bf16[128,1024]{1,0:T(8,128)(2,1)S(1)} %shard_map.93.refs_3_.mine), channel_id=1, source_target_pairs={{0,14},{2,0},{4,2},{6,4},{8,6},{10,8},{12,10},{14,12},{1,15},{3,1}... | collective-permute-start | bytes 786440 | tf_op jit(solution)/shard_map/ppermute | solution.py:29
  51.5 11.3 %collective-permute-start.3 = (bf16[128,1024]{1,0:T(8,128)(2,1)S(1)}, bf16[128,1024]{1,0:T(8,128)(2,1)S(1)}, u32[]{:S(2)}, u32[]{:S(2)}) collective-permute-start(bf16[128,1024]{1,0:T(8,128)(2,1)S(1)} %collective-permute-done.1.refs_4_), channel_id=1, source_target_pairs={{0,2},{2,4},{4,6},{6,8},{8,10},{10,12},{12,14},{14,0},{1,3},{3,5},... | collective-permute-start | bytes 786440 | tf_op jit(solution)/shard_map/ppermute | solution.py:29
  57.0 10.4 %collective-permute-start.4 = (bf16[128,1024]{1,0:T(8,128)(2,1)S(1)}, bf16[128,1024]{1,0:T(8,128)(2,1)S(1)}, u32[]{:S(2)}, u32[]{:S(2)}) collective-permute-start(bf16[128,1024]{1,0:T(8,128)(2,1)S(1)} %collective-permute-done.2.refs_5_), channel_id=1, source_target_pairs={{0,14},{2,0},{4,2},{6,4},{8,6},{10,8},{12,10},{14,12},{1,15},{3,1}... | collective-permute-start | bytes 786440 | tf_op jit(solution)/shard_map/ppermute | solution.py:29
  62.8 10.1 %collective-permute-start.5 = (bf16[128,1024]{1,0:T(8,128)(2,1)S(1)}, bf16[128,1024]{1,0:T(8,128)(2,1)}, u32[]{:S(2)}, u32[]{:S(2)}) collective-permute-start(bf16[128,1024]{1,0:T(8,128)(2,1)S(1)} %collective-permute-done.3.refs_6_), channel_id=1, source_target_pairs={{0,2},{2,4},{4,6},{6,8},{8,10},{10,12},{12,14},{14,0},{1,3},{3,5},... | collective-permute-start | bytes 786440 | tf_op jit(solution)/shard_map/ppermute | solution.py:29
  67.4 15.2 %collective-permute-start.6 = (bf16[128,1024]{1,0:T(8,128)(2,1)S(1)}, bf16[128,1024]{1,0:T(8,128)(2,1)}, u32[]{:S(2)}, u32[]{:S(2)}) collective-permute-start(bf16[128,1024]{1,0:T(8,128)(2,1)S(1)} %collective-permute-done.4.refs_7_), channel_id=1, source_target_pairs={{0,14},{2,0},{4,2},{6,4},{8,6},{10,8},{12,10},{14,12},{1,15},{3,1}... | collective-permute-start | bytes 786440 | tf_op jit(solution)/shard_map/ppermute | solution.py:29
  72.9 10.6 %collective-permute-start.7 = (bf16[128,1024]{1,0:T(8,128)(2,1)}, bf16[128,1024]{1,0:T(8,128)(2,1)}, u32[]{:S(2)}, u32[]{:S(2)}) collective-permute-start(bf16[128,1024]{1,0:T(8,128)(2,1)} %collective-permute-done.5.refs_8_), channel_id=1, source_target_pairs={{0,2},{2,4},{4,6},{6,8},{8,10},{10,12},{12,14},{14,0},{1,3},{3,5},... | collective-permute-start | bytes 786440 | tf_op jit(solution)/shard_map/ppermute | solution.py:29
  80.2 11.8 %copy-start.1 = (bf16[16,64,1024]{2,1,0:T(8,128)(2,1)S(1)}, bf16[16,64,1024]{2,1,0:T(8,128)(2,1)}, u32[]{:S(2)}) copy-start(bf16[16,64,1024]{2,1,0:T(8,128)(2,1)} %all-gather.4.cloned.1.call-done) | copy-start | bytes 6291460
  83.5 49.0 %copy-start.2 = (f32[2,64,1024]{2,1,0:T(8,128)S(1)}, f32[2,64,1024]{2,1,0:T(8,128)}, u32[]{:S(2)}) copy-start(f32[2,64,1024]{2,1,0:T(8,128)} %master.1) | copy-start | bytes 1572868
  83.5 49.0 %copy-start.3 = (f32[2,64,1024]{2,1,0:T(8,128)S(1)}, f32[2,64,1024]{2,1,0:T(8,128)}, u32[]{:S(2)}) copy-start(f32[2,64,1024]{2,1,0:T(8,128)} %momentum.1) | copy-start | bytes 1572868
  93.5 18.3 %collective-permute-start.8 = (bf16[2,128,512]{2,1,0:T(8,128)(2,1)S(1)}, bf16[2,128,512]{2,1,0:T(8,128)(2,1)S(1)}, u32[]{:S(2)}, u32[]{:S(2)}) collective-permute-start(bf16[2,128,512]{2,1,0:T(8,128)(2,1)S(1)} %get-tuple-element.13.mine), channel_id=1, source_target_pairs={{0,1},{1,0},{2,3},{3,2},{4,5},{5,4},{6,7},{7,6},{8,9},{9,8},{10,11... | collective-permute-start | bytes 786440 | tf_op jit(solution)/shard_map/ppermute | solution.py:25
  112.9 12.3 %collective-permute-start.9 = (bf16[2,128,1024]{2,1,0:T(8,128)(2,1)S(1)}, bf16[2,128,1024]{2,1,0:T(8,128)(2,1)}, u32[]{:S(2)}, u32[]{:S(2)}) collective-permute-start(bf16[2,128,1024]{2,1,0:T(8,128)(2,1)S(1)} %shard_map.98.both), channel_id=1, source_target_pairs={{0,2},{2,4},{4,6},{6,8},{8,10},{10,12},{12,14},{14,0},{1,3},{3,5},... | collective-permute-start | bytes 1572872 | tf_op jit(solution)/shard_map/ppermute | solution.py:29
  117.5 13.1 %collective-permute-start.10 = (bf16[2,128,1024]{2,1,0:T(8,128)(2,1)S(1)}, bf16[2,128,1024]{2,1,0:T(8,128)(2,1)}, u32[]{:S(2)}, u32[]{:S(2)}) collective-permute-start(bf16[2,128,1024]{2,1,0:T(8,128)(2,1)S(1)} %shard_map.98.both), channel_id=1, source_target_pairs={{0,14},{2,0},{4,2},{6,4},{8,6},{10,8},{12,10},{14,12},{1,15},{3,1}... | collective-permute-start | bytes 1572872 | tf_op jit(solution)/shard_map/ppermute | solution.py:29
  125.2 13.9 %collective-permute-start.11 = (bf16[2,128,1024]{2,1,0:T(8,128)(2,1)}, bf16[2,128,1024]{2,1,0:T(8,128)(2,1)S(1)}, u32[]{:S(2)}, u32[]{:S(2)}) collective-permute-start(bf16[2,128,1024]{2,1,0:T(8,128)(2,1)} %collective-permute-done.9), channel_id=1, source_target_pairs={{0,2},{2,4},{4,6},{6,8},{8,10},{10,12},{12,14},{14,0},{1,3},{3,5},... | collective-permute-start | bytes 1572872 | tf_op jit(solution)/shard_map/ppermute | solution.py:29
  130.6 14.6 %collective-permute-start.12 = (bf16[2,128,1024]{2,1,0:T(8,128)(2,1)}, bf16[2,128,1024]{2,1,0:T(8,128)(2,1)S(1)}, u32[]{:S(2)}, u32[]{:S(2)}) collective-permute-start(bf16[2,128,1024]{2,1,0:T(8,128)(2,1)} %collective-permute-done.10), channel_id=1, source_target_pairs={{0,14},{2,0},{4,2},{6,4},{8,6},{10,8},{12,10},{14,12},{1,15},{3,1}... | collective-permute-start | bytes 1572872 | tf_op jit(solution)/shard_map/ppermute | solution.py:29
  139.1 15.0 %collective-permute-start.13 = (bf16[2,128,1024]{2,1,0:T(8,128)(2,1)S(1)}, bf16[2,128,1024]{2,1,0:T(8,128)(2,1)S(1)}, u32[]{:S(2)}, u32[]{:S(2)}) collective-permute-start(bf16[2,128,1024]{2,1,0:T(8,128)(2,1)S(1)} %collective-permute-done.11), channel_id=1, source_target_pairs={{0,2},{2,4},{4,6},{6,8},{8,10},{10,12},{12,14},{14,0},{1,3},{3,5},... | collective-permute-start | bytes 1572872 | tf_op jit(solution)/shard_map/ppermute | solution.py:29
  145.2 14.6 %collective-permute-start.14 = (bf16[2,128,1024]{2,1,0:T(8,128)(2,1)S(1)}, bf16[2,128,1024]{2,1,0:T(8,128)(2,1)S(1)}, u32[]{:S(2)}, u32[]{:S(2)}) collective-permute-start(bf16[2,128,1024]{2,1,0:T(8,128)(2,1)S(1)} %collective-permute-done.12), channel_id=1, source_target_pairs={{0,14},{2,0},{4,2},{6,4},{8,6},{10,8},{12,10},{14,12},{1,15},{3,1}... | collective-permute-start | bytes 1572872 | tf_op jit(solution)/shard_map/ppermute | solution.py:29
  154.2 10.9 %collective-permute-start.15 = (bf16[3,64,1024]{2,1,0:T(8,128)(2,1)S(1)}, bf16[3,64,1024]{2,1,0:T(8,128)(2,1)S(1)}, u32[]{:S(2)}, u32[]{:S(2)}) collective-permute-start(bf16[3,64,1024]{2,1,0:T(8,128)(2,1)S(1)} %slice.41), channel_id=1, source_target_pairs={{0,2},{2,4},{4,6},{6,8},{8,10},{10,12},{12,14},{14,0},{1,3},{3,5},... | collective-permute-start | bytes 1179656 | tf_op jit(solution)/shard_map/ppermute | solution.py:29
  159.8 8.1 %collective-permute-start.16 = (bf16[1,64,1024]{2,1,0:T(8,128)(2,1)S(1)}, bf16[1,64,1024]{2,1,0:T(8,128)(2,1)S(1)}, u32[]{:S(2)}, u32[]{:S(2)}) collective-permute-start(bf16[1,64,1024]{2,1,0:T(8,128)(2,1)S(1)} %slice.44), channel_id=1, source_target_pairs={{0,14},{2,0},{4,2},{6,4},{8,6},{10,8},{12,10},{14,12},{1,15},{3,1}... | collective-permute-start | bytes 393224 | tf_op jit(solution)/shard_map/ppermute | solution.py:29
Sparse Core Ops, SparseCore 0:
  10.1 50.6 all-gather.3

commit v8 on v7

--- a/solution.py
+++ b/solution.py
@@ -82,9 +82,9 @@
         )
         out[block] = part.astype(jnp.bfloat16)
         squares.append(jnp.sum(part * part))
-    row = lax.broadcasted_iota(jnp.int32, (8, 128), 0)
+    lane = lax.broadcasted_iota(jnp.int32, (1, 128), 1)
     values = jnp.where(
-        row < 2, jnp.where(row == 0, squares[0], squares[1]), jnp.where(row == 2, adam[0][:1], adam[1][:1])
+        lane < 2, jnp.where(lane == 0, squares[0], squares[1]), jnp.where(lane == 2, adam[0][:1], adam[1][:1])
     )
     for i in range(sums.shape[0]):
         sums[i] = values
@@ -93,7 +93,12 @@
 def grafted(place, sums, mine, theirs, block, precond):
     half = place[1]
     total = jnp.sum(sums[...], axis=0)
-    graft = jnp.sqrt(total[2 + block : 3 + block] / (total[block : block + 1] + norm_eps))
+    lane = lax.broadcasted_iota(jnp.int32, total.shape, 1)
+
+    def spread(i):
+        return jnp.full(total.shape, jnp.sum(jnp.where(lane == i, total, 0.0)), jnp.float32)
+
+    graft = jnp.sqrt(spread(2 + block) / (spread(block) + norm_eps))
     low = lax.broadcasted_iota(jnp.int32, (precond.shape[0], 128), 1) < 64
     for i in range(Y // 2):
         cut = slice(i * 128, (i + 1) * 128)
@@ -206,7 +211,7 @@
     )
     part, sums = call(
         right_kernel,
-        (shape((2, 2 * rows, width // 2), bf16), shape((2 * Y, 8, 128), f32)),
+        (shape((2, 2 * rows, width // 2), bf16), shape((2 * Y, 1, 128), f32)),
         (place, lax.all_gather(left_grad, "xl", axis=0, tiled=False), squares, right),
         flops,
     )
@@ -227,20 +232,17 @@
         scratch_shapes=scratch,
     )
 
-    def put(params, chunk, block, distance, row=0):
+    def put(params, chunk, block, distance):
         at = lax.rem(place[0] + distance + Y, Y)
-        return lax.dynamic_update_slice(params, chunk[:, None], (block, at, row, 0))
+        return lax.dynamic_update_slice(params, chunk[:, None], (block, at, 0, 0))
 
     up = down = both
     for step in range(1, 4):
         up, down = hop(up, 1), hop(down, -1)
         params = put(params, up, 0, -step)
         params = put(params, down, 0, step)
-    up = hop(up.reshape(4, rows, width)[:3], 1)
-    down = hop(down.reshape(4, rows, width)[3:], -1)
-    params = put(params, up[:2].reshape(1, 2 * rows, width), 0, 4)
-    params = put(params, up[2:], 1, 4)
-    params = put(params, down, 1, 4, rows)
+    for block in range(2):
+        params = put(params, hop(up[block : block + 1], 1), block, 4)
     params = params.reshape(2, 2 * Y * rows, width)
     return (params, new_master, new_momentum, new_second)
 

time: 178 us -> 177 us (level)
    dynamic_update_slice x9 -> x8, local copies, waits for them, and re-layouts: 9.11 us -> 8.5 us  [put(): return lax.dynamic_update_slice(params, chunk[:, None], (block, at, 0, 0))]
  transfers between devices with their start and end apart: 19 -> 19, of which waited for: 13 -> 12; matrix products, arithmetic and copies ran while one was open for 7% -> 7% of each run, Pallas kernels for 4% -> 4%
where the time goes in v8:
time: 177 us; the launch traced here: 175 us
  starting transfers between devices  71.5 us (40%)
  waiting for transfers between devices  43 us (24%)
  blocking collectives  22 us (12%)
  between operations  14.4 us (8%)
  Pallas kernels  11 us (6%)
  local copies, waits for them, and re-layouts  9.68 us (5%)
  other arithmetic  3.49 us (2%)
    ppermute x15, starting transfers between devices, hop(): return lax.ppermute(x, 'y', [(i, (i + way) % Y) for i in range(Y)])  52.1 us
    ppermute x15, waiting for transfers between devices, hop(): return lax.ppermute(x, 'y', [(i, (i + way) % Y) for i in range(Y)])  32.9 us
    all_to_all x1, blocking collectives, on_device(): sums = lax.all_to_all(sums, GROUP, split_axis=0, concat_axis=0, tiled=True)  15 us
    all_to_all x1, starting transfers between devices, on_device(): lax.all_to_all(grad, OWNERS + ('xl',), split_axis=0, concat_axis=1, tiled...  13.8 us
    pallas_call x7, Pallas kernels, call(): pl.pallas_call(kernel, out_shape=out_shape, in_specs=in_specs, out_specs=...  11 us
    all_to_all x1, waiting for transfers between devices, on_device(): lax.all_to_all(grad, OWNERS + ('xl',), split_axis=0, concat_axis=1, tiled...  9.37 us
    dynamic_update_slice x8, local copies, waits for them, and re-layouts, put(): return lax.dynamic_update_slice(params, chunk[:, None], (block, at, 0, 0))  8.5 us
    all_gather x1, blocking collectives, on_device(): lax.all_gather(left_grad, 'xl', axis=0, tiled=False)  7.05 us
  transfers between devices with their start and end apart: 19, of which 12 were waited for; matrix products, arithmetic and copies ran while one was open for 7% of the time, Pallas kernels for 4%

profile of v8, /device:TPU:56, one launch (start us, length us, event | category | flops | bytes accessed | tf_op | source)
XLA Modules:
  0.0 175.0 jit_solution(4571563716190426469)
XLA Ops:
  7.9 13.8 %all-to-all-start = ((bf16[64,2,1024]{2,1,0:T(2,128)(2,1)}), bf16[64,2,1024]{2,1,0:T(2,128)(2,1)S(1)}, u32[]{:S(2)}, u32[]{:S(2)}) async-start(bf16[64,2,1024]{2,1,0:T(2,128)(2,1)} %param.6), calls=%async_computation | async-start | bytes 524288 | tf_op jit(solution)/shard_map/all_to_all | solution.py:180
  25.1 9.4 %all-to-all-done = bf16[64,2,1024]{2,1,0:T(2,128)(2,1)S(1)} async-done(((bf16[64,2,1024]{2,1,0:T(2,128)(2,1)}), bf16[64,2,1024]{2,1,0:T(2,128)(2,1)S(1)}, u32[]{:S(2)}, u32[]{:S(2)}) %all-to-all-start) | async-done | bytes 262176 | tf_op jit(solution)/shard_map/all_to_all | solution.py:180
  37.4 2.6 %collective-permute-start = (bf16[384,1024]{1,0:T(8,128)(2,1)S(1)}, bf16[384,1024]{1,0:T(8,128)(2,1)S(1)}, u32[]{:S(2)}, u32[]{:S(2)}) collective-permute-start(bf16[384,1024]{1,0:T(8,128)(2,1)S(1)} %bitcast.47), channel_id=1, source_target_pairs={{0,1},{1,0},{2,3},{3,2},{4,5},{5,4},{6,7},{7,6},{8,9},{9,8},{10,11... | collective-permute-start | bytes 2359304 | tf_op jit(solution)/shard_map/ppermute | solution.py:25
  40.0 3.9 %collective-permute-start.2 = (bf16[128,1024]{1,0:T(8,128)(2,1)S(1)}, bf16[128,1024]{1,0:T(8,128)(2,1)S(1)}, u32[]{:S(2)}, u32[]{:S(2)}) collective-permute-start(bf16[128,1024]{1,0:T(8,128)(2,1)S(1)} %shard_map.93.refs_3_.mine), channel_id=1, source_target_pairs={{0,14},{2,0},{4,2},{6,4},{8,6},{10,8},{12,10},{14,12},{1,15},{3,1}... | collective-permute-start | bytes 786440 | tf_op jit(solution)/shard_map/ppermute | solution.py:29
  44.0 7.5 %collective-permute-done.1.refs_4_ = bf16[128,1024]{1,0:T(8,128)(2,1)S(1)} collective-permute-done((bf16[128,1024]{1,0:T(8,128)(2,1)S(1)}, bf16[128,1024]{1,0:T(8,128)(2,1)S(1)}, u32[]{:S(2)}, u32[]{:S(2)}) %collective-permute-start.1) | collective-permute-done | bytes 262176 | tf_op jit(solution)/shard_map/ppermute | solution.py:29
  51.5 3.3 %collective-permute-start.3 = (bf16[128,1024]{1,0:T(8,128)(2,1)S(1)}, bf16[128,1024]{1,0:T(8,128)(2,1)S(1)}, u32[]{:S(2)}, u32[]{:S(2)}) collective-permute-start(bf16[128,1024]{1,0:T(8,128)(2,1)S(1)} %collective-permute-done.1.refs_4_), channel_id=1, source_target_pairs={{0,2},{2,4},{4,6},{6,8},{8,10},{10,12},{12,14},{14,0},{1,3},{3,5},... | collective-permute-start | bytes 786440 | tf_op jit(solution)/shard_map/ppermute | solution.py:29
  54.8 2.2 %collective-permute-done.2.refs_5_ = bf16[128,1024]{1,0:T(8,128)(2,1)S(1)} collective-permute-done((bf16[128,1024]{1,0:T(8,128)(2,1)S(1)}, bf16[128,1024]{1,0:T(8,128)(2,1)S(1)}, u32[]{:S(2)}, u32[]{:S(2)}) %collective-permute-start.2) | collective-permute-done | bytes 262176 | tf_op jit(solution)/shard_map/ppermute | solution.py:29
  57.0 2.5 %collective-permute-start.4 = (bf16[128,1024]{1,0:T(8,128)(2,1)S(1)}, bf16[128,1024]{1,0:T(8,128)(2,1)S(1)}, u32[]{:S(2)}, u32[]{:S(2)}) collective-permute-start(bf16[128,1024]{1,0:T(8,128)(2,1)S(1)} %collective-permute-done.2.refs_5_), channel_id=1, source_target_pairs={{0,14},{2,0},{4,2},{6,4},{8,6},{10,8},{12,10},{14,12},{1,15},{3,1}... | collective-permute-start | bytes 786440 | tf_op jit(solution)/shard_map/ppermute | solution.py:29
  59.5 3.3 %collective-permute-done.3.refs_6_ = bf16[128,1024]{1,0:T(8,128)(2,1)S(1)} collective-permute-done((bf16[128,1024]{1,0:T(8,128)(2,1)S(1)}, bf16[128,1024]{1,0:T(8,128)(2,1)S(1)}, u32[]{:S(2)}, u32[]{:S(2)}) %collective-permute-start.3) | collective-permute-done | bytes 262176 | tf_op jit(solution)/shard_map/ppermute | solution.py:29
  62.8 4.6 %collective-permute-start.5 = (bf16[128,1024]{1,0:T(8,128)(2,1)S(1)}, bf16[128,1024]{1,0:T(8,128)(2,1)}, u32[]{:S(2)}, u32[]{:S(2)}) collective-permute-start(bf16[128,1024]{1,0:T(8,128)(2,1)S(1)} %collective-permute-done.3.refs_6_), channel_id=1, source_target_pairs={{0,2},{2,4},{4,6},{6,8},{8,10},{10,12},{12,14},{14,0},{1,3},{3,5},... | collective-permute-start | bytes 786440 | tf_op jit(solution)/shard_map/ppermute | solution.py:29
  67.4 1.9 %collective-permute-start.6 = (bf16[128,1024]{1,0:T(8,128)(2,1)S(1)}, bf16[128,1024]{1,0:T(8,128)(2,1)}, u32[]{:S(2)}, u32[]{:S(2)}) collective-permute-start(bf16[128,1024]{1,0:T(8,128)(2,1)S(1)} %collective-permute-done.4.refs_7_), channel_id=1, source_target_pairs={{0,14},{2,0},{4,2},{6,4},{8,6},{10,8},{12,10},{14,12},{1,15},{3,1}... | collective-permute-start | bytes 786440 | tf_op jit(solution)/shard_map/ppermute | solution.py:29
  69.4 3.6 %collective-permute-done.5.refs_8_ = bf16[128,1024]{1,0:T(8,128)(2,1)} collective-permute-done((bf16[128,1024]{1,0:T(8,128)(2,1)S(1)}, bf16[128,1024]{1,0:T(8,128)(2,1)}, u32[]{:S(2)}, u32[]{:S(2)}) %collective-permute-start.5) | collective-permute-done | bytes 262176 | tf_op jit(solution)/shard_map/ppermute | solution.py:29
  72.9 5.7 %collective-permute-start.7 = (bf16[128,1024]{1,0:T(8,128)(2,1)}, bf16[128,1024]{1,0:T(8,128)(2,1)}, u32[]{:S(2)}, u32[]{:S(2)}) collective-permute-start(bf16[128,1024]{1,0:T(8,128)(2,1)} %collective-permute-done.5.refs_8_), channel_id=1, source_target_pairs={{0,2},{2,4},{4,6},{6,8},{8,10},{10,12},{12,14},{14,0},{1,3},{3,5},... | collective-permute-start | bytes 786440 | tf_op jit(solution)/shard_map/ppermute | solution.py:29
  84.9 7.0 %all-gather.1 = bf16[256,1024]{1,0:T(8,128)(2,1)S(1)} all-gather(bf16[128,1024]{1,0:T(8,128)(2,1)S(1)} %shard_map.96), channel_id=3, replica_groups=mesh['z'=8,'xh'=2,'c'=2,'y'=8,'xl'=2] {'xl'}, dimensions={0}, use_global_device_ids=true | all-gather | bytes 786432 | tf_op jit(solution)/shard_map/all_gather | solution.py:215
  93.4 2.9 %collective-permute-start.8 = (bf16[2,128,512]{2,1,0:T(8,128)(2,1)S(1)}, bf16[2,128,512]{2,1,0:T(8,128)(2,1)S(1)}, u32[]{:S(2)}, u32[]{:S(2)}) collective-permute-start(bf16[2,128,512]{2,1,0:T(8,128)(2,1)S(1)} %get-tuple-element.13.mine), channel_id=1, source_target_pairs={{0,1},{1,0},{2,3},{3,2},{4,5},{5,4},{6,7},{7,6},{8,9},{9,8},{10,11... | collective-permute-start | bytes 786440 | tf_op jit(solution)/shard_map/ppermute | solution.py:25
  96.3 15.0 %all_to_all.14.sums = f32[16,1,128]{2,1,0:T(1,128)S(1)} all-to-all(f32[16,1,128]{2,1,0:T(1,128)S(1)} %get-tuple-element.12), channel_id=1, replica_groups=mesh['z'=8,'xh'=2,'c'=2,'y'=8,'xl'=2] {'y','xl'}, dimensions={0} | all-to-all | bytes 16384 | tf_op jit(solution)/shard_map/all_to_all | solution.py:219
  112.4 4.6 %collective-permute-start.9 = (bf16[2,128,1024]{2,1,0:T(8,128)(2,1)S(1)}, bf16[2,128,1024]{2,1,0:T(8,128)(2,1)}, u32[]{:S(2)}, u32[]{:S(2)}) collective-permute-start(bf16[2,128,1024]{2,1,0:T(8,128)(2,1)S(1)} %shard_map.98.both), channel_id=1, source_target_pairs={{0,2},{2,4},{4,6},{6,8},{8,10},{10,12},{12,14},{14,0},{1,3},{3,5},... | collective-permute-start | bytes 1572872 | tf_op jit(solution)/shard_map/ppermute | solution.py:29
  118.9 5.9 %collective-permute-done.9 = bf16[2,128,1024]{2,1,0:T(8,128)(2,1)} collective-permute-done((bf16[2,128,1024]{2,1,0:T(8,128)(2,1)S(1)}, bf16[2,128,1024]{2,1,0:T(8,128)(2,1)}, u32[]{:S(2)}, u32[]{:S(2)}) %collective-permute-start.9) | collective-permute-done | bytes 524320 | tf_op jit(solution)/shard_map/ppermute | solution.py:29
  124.8 5.0 %collective-permute-start.11 = (bf16[2,128,1024]{2,1,0:T(8,128)(2,1)}, bf16[2,128,1024]{2,1,0:T(8,128)(2,1)S(1)}, u32[]{:S(2)}, u32[]{:S(2)}) collective-permute-start(bf16[2,128,1024]{2,1,0:T(8,128)(2,1)} %collective-permute-done.9), channel_id=1, source_target_pairs={{0,2},{2,4},{4,6},{6,8},{8,10},{10,12},{12,14},{14,0},{1,3},{3,5},... | collective-permute-start | bytes 1572872 | tf_op jit(solution)/shard_map/ppermute | solution.py:29
  132.0 3.4 %shard_map.99 = (f32[2,64,1024]{2,1,0:T(8,128)}, f32[2,64,1024]{2,1,0:T(8,128)}, bf16[2,8,128,1024]{3,2,1,0:T(8,128)(2,1)}) custom-call(s32[2]{0:T(128)S(1)} %pad_add_fusion.refs_0_.place, f32[16,1,128]{2,1,0:T(1,128)S(1)} %all_to_all.14.sums, bf16[2,128,512]{2,1,0:T(8,128)(2,1)S(1)} %get-tuple-element.13.mine, ...), custom_call_target="tpu_custom_call" | custom-call | bytes 4210704 | tf_op jit(solution)/shard_map/pallas_call | solution.py:150
  138.5 5.5 %collective-permute-start.13 = (bf16[2,128,1024]{2,1,0:T(8,128)(2,1)S(1)}, bf16[2,128,1024]{2,1,0:T(8,128)(2,1)S(1)}, u32[]{:S(2)}, u32[]{:S(2)}) collective-permute-start(bf16[2,128,1024]{2,1,0:T(8,128)(2,1)S(1)} %collective-permute-done.11), channel_id=1, source_target_pairs={{0,2},{2,4},{4,6},{6,8},{8,10},{10,12},{12,14},{14,0},{1,3},{3,5},... | collective-permute-start | bytes 1572872 | tf_op jit(solution)/shard_map/ppermute | solution.py:29
  149.5 4.1 %collective-permute-done.13 = bf16[2,128,1024]{2,1,0:T(8,128)(2,1)S(1)} collective-permute-done((bf16[2,128,1024]{2,1,0:T(8,128)(2,1)S(1)}, bf16[2,128,1024]{2,1,0:T(8,128)(2,1)S(1)}, u32[]{:S(2)}, u32[]{:S(2)}) %collective-permute-start.13) | collective-permute-done | bytes 524320 | tf_op jit(solution)/shard_map/ppermute | solution.py:29
  153.6 5.6 %collective-permute-start.15 = (bf16[1,128,1024]{2,1,0:T(8,128)(2,1)S(1)}, bf16[1,128,1024]{2,1,0:T(8,128)(2,1)S(1)}, u32[]{:S(2)}, u32[]{:S(2)}) collective-permute-start(bf16[1,128,1024]{2,1,0:T(8,128)(2,1)S(1)} %get-tuple-element.22), channel_id=1, source_target_pairs={{0,2},{2,4},{4,6},{6,8},{8,10},{10,12},{12,14},{14,0},{1,3},{3,5},... | collective-permute-start | bytes 786440 | tf_op jit(solution)/shard_map/ppermute | solution.py:29
  163.8 3.7 %collective-permute-done.16 = bf16[1,128,1024]{2,1,0:T(8,128)(2,1)S(1)} collective-permute-done((bf16[1,128,1024]{2,1,0:T(8,128)(2,1)S(1)}, bf16[1,128,1024]{2,1,0:T(8,128)(2,1)S(1)}, u32[]{:S(2)}, u32[]{:S(2)}) %collective-permute-start.16) | collective-permute-done | bytes 262176 | tf_op jit(solution)/shard_map/ppermute | solution.py:29
  (52 shorter events, 33.8 us)
Async XLA Ops:
  7.2 71.5 %copy-start = (bf16[2,64,1024]{2,1,0:T(8,128)(2,1)S(1)}, bf16[2,64,1024]{2,1,0:T(8,128)(2,1)}, u32[]{:S(2)}) copy-start(bf16[2,64,1024]{2,1,0:T(8,128)(2,1)} %refs_1_.3) | copy-start | bytes 786436
  7.2 73.0 %all-gather.4.cloned.1.call-start = ((), (), s32[]{:S(2)}) async-start(), calls=%async_computation.2 | async-start | bytes 2359296 | tf_op jit(solution)/shard_map/all_gather | solution.py:172
  7.9 26.6 %all-to-all-start = ((bf16[64,2,1024]{2,1,0:T(2,128)(2,1)}), bf16[64,2,1024]{2,1,0:T(2,128)(2,1)S(1)}, u32[]{:S(2)}, u32[]{:S(2)}) async-start(bf16[64,2,1024]{2,1,0:T(2,128)(2,1)} %param.6), calls=%async_computation | async-start | bytes 524288 | tf_op jit(solution)/shard_map/all_to_all | solution.py:180
  25.1 55.9 %copy-start.4 = (f32[2,64,1024]{2,1,0:T(8,128)S(1)}, f32[2,64,1024]{2,1,0:T(8,128)}, u32[]{:S(2)}) copy-start(f32[2,64,1024]{2,1,0:T(8,128)} %second.1) | copy-start | bytes 1572868
  35.3 16.2 %collective-permute-start.1 = (bf16[128,1024]{1,0:T(8,128)(2,1)S(1)}, bf16[128,1024]{1,0:T(8,128)(2,1)S(1)}, u32[]{:S(2)}, u32[]{:S(2)}) collective-permute-start(bf16[128,1024]{1,0:T(8,128)(2,1)S(1)} %shard_map.93.refs_3_.mine), channel_id=1, source_target_pairs={{0,2},{2,4},{4,6},{6,8},{8,10},{10,12},{12,14},{14,0},{1,3},{3,5},... | collective-permute-start | bytes 786440 | tf_op jit(solution)/shard_map/ppermute | solution.py:29
  37.4 41.2 %collective-permute-start = (bf16[384,1024]{1,0:T(8,128)(2,1)S(1)}, bf16[384,1024]{1,0:T(8,128)(2,1)S(1)}, u32[]{:S(2)}, u32[]{:S(2)}) collective-permute-start(bf16[384,1024]{1,0:T(8,128)(2,1)S(1)} %bitcast.47), channel_id=1, source_target_pairs={{0,1},{1,0},{2,3},{3,2},{4,5},{5,4},{6,7},{7,6},{8,9},{9,8},{10,11... | collective-permute-start | bytes 2359304 | tf_op jit(solution)/shard_map/ppermute | solution.py:25
  40.0 16.9 %collective-permute-start.2 = (bf16[128,1024]{1,0:T(8,128)(2,1)S(1)}, bf16[128,1024]{1,0:T(8,128)(2,1)S(1)}, u32[]{:S(2)}, u32[]{:S(2)}) collective-permute-start(bf16[128,1024]{1,0:T(8,128)(2,1)S(1)} %shard_map.93.refs_3_.mine), channel_id=1, source_target_pairs={{0,14},{2,0},{4,2},{6,4},{8,6},{10,8},{12,10},{14,12},{1,15},{3,1}... | collective-permute-start | bytes 786440 | tf_op jit(solution)/shard_map/ppermute | solution.py:29
  51.5 11.3 %collective-permute-start.3 = (bf16[128,1024]{1,0:T(8,128)(2,1)S(1)}, bf16[128,1024]{1,0:T(8,128)(2,1)S(1)}, u32[]{:S(2)}, u32[]{:S(2)}) collective-permute-start(bf16[128,1024]{1,0:T(8,128)(2,1)S(1)} %collective-permute-done.1.refs_4_), channel_id=1, source_target_pairs={{0,2},{2,4},{4,6},{6,8},{8,10},{10,12},{12,14},{14,0},{1,3},{3,5},... | collective-permute-start | bytes 786440 | tf_op jit(solution)/shard_map/ppermute | solution.py:29
  57.0 10.4 %collective-permute-start.4 = (bf16[128,1024]{1,0:T(8,128)(2,1)S(1)}, bf16[128,1024]{1,0:T(8,128)(2,1)S(1)}, u32[]{:S(2)}, u32[]{:S(2)}) collective-permute-start(bf16[128,1024]{1,0:T(8,128)(2,1)S(1)} %collective-permute-done.2.refs_5_), channel_id=1, source_target_pairs={{0,14},{2,0},{4,2},{6,4},{8,6},{10,8},{12,10},{14,12},{1,15},{3,1}... | collective-permute-start | bytes 786440 | tf_op jit(solution)/shard_map/ppermute | solution.py:29
  62.8 10.1 %collective-permute-start.5 = (bf16[128,1024]{1,0:T(8,128)(2,1)S(1)}, bf16[128,1024]{1,0:T(8,128)(2,1)}, u32[]{:S(2)}, u32[]{:S(2)}) collective-permute-start(bf16[128,1024]{1,0:T(8,128)(2,1)S(1)} %collective-permute-done.3.refs_6_), channel_id=1, source_target_pairs={{0,2},{2,4},{4,6},{6,8},{8,10},{10,12},{12,14},{14,0},{1,3},{3,5},... | collective-permute-start | bytes 786440 | tf_op jit(solution)/shard_map/ppermute | solution.py:29
  67.4 15.3 %collective-permute-start.6 = (bf16[128,1024]{1,0:T(8,128)(2,1)S(1)}, bf16[128,1024]{1,0:T(8,128)(2,1)}, u32[]{:S(2)}, u32[]{:S(2)}) collective-permute-start(bf16[128,1024]{1,0:T(8,128)(2,1)S(1)} %collective-permute-done.4.refs_7_), channel_id=1, source_target_pairs={{0,14},{2,0},{4,2},{6,4},{8,6},{10,8},{12,10},{14,12},{1,15},{3,1}... | collective-permute-start | bytes 786440 | tf_op jit(solution)/shard_map/ppermute | solution.py:29
  72.9 10.6 %collective-permute-start.7 = (bf16[128,1024]{1,0:T(8,128)(2,1)}, bf16[128,1024]{1,0:T(8,128)(2,1)}, u32[]{:S(2)}, u32[]{:S(2)}) collective-permute-start(bf16[128,1024]{1,0:T(8,128)(2,1)} %collective-permute-done.5.refs_8_), channel_id=1, source_target_pairs={{0,2},{2,4},{4,6},{6,8},{8,10},{10,12},{12,14},{14,0},{1,3},{3,5},... | collective-permute-start | bytes 786440 | tf_op jit(solution)/shard_map/ppermute | solution.py:29
  80.2 11.7 %copy-start.1 = (bf16[16,64,1024]{2,1,0:T(8,128)(2,1)S(1)}, bf16[16,64,1024]{2,1,0:T(8,128)(2,1)}, u32[]{:S(2)}) copy-start(bf16[16,64,1024]{2,1,0:T(8,128)(2,1)} %all-gather.4.cloned.1.call-done) | copy-start | bytes 6291460
  82.7 49.3 %copy-start.2 = (f32[2,64,1024]{2,1,0:T(8,128)S(1)}, f32[2,64,1024]{2,1,0:T(8,128)}, u32[]{:S(2)}) copy-start(f32[2,64,1024]{2,1,0:T(8,128)} %master.1) | copy-start | bytes 1572868
  82.7 49.3 %copy-start.3 = (f32[2,64,1024]{2,1,0:T(8,128)S(1)}, f32[2,64,1024]{2,1,0:T(8,128)}, u32[]{:S(2)}) copy-start(f32[2,64,1024]{2,1,0:T(8,128)} %momentum.1) | copy-start | bytes 1572868
  93.4 17.8 %collective-permute-start.8 = (bf16[2,128,512]{2,1,0:T(8,128)(2,1)S(1)}, bf16[2,128,512]{2,1,0:T(8,128)(2,1)S(1)}, u32[]{:S(2)}, u32[]{:S(2)}) collective-permute-start(bf16[2,128,512]{2,1,0:T(8,128)(2,1)S(1)} %get-tuple-element.13.mine), channel_id=1, source_target_pairs={{0,1},{1,0},{2,3},{3,2},{4,5},{5,4},{6,7},{7,6},{8,9},{9,8},{10,11... | collective-permute-start | bytes 786440 | tf_op jit(solution)/shard_map/ppermute | solution.py:25
  112.4 12.4 %collective-permute-start.9 = (bf16[2,128,1024]{2,1,0:T(8,128)(2,1)S(1)}, bf16[2,128,1024]{2,1,0:T(8,128)(2,1)}, u32[]{:S(2)}, u32[]{:S(2)}) collective-permute-start(bf16[2,128,1024]{2,1,0:T(8,128)(2,1)S(1)} %shard_map.98.both), channel_id=1, source_target_pairs={{0,2},{2,4},{4,6},{6,8},{8,10},{10,12},{12,14},{14,0},{1,3},{3,5},... | collective-permute-start | bytes 1572872 | tf_op jit(solution)/shard_map/ppermute | solution.py:29
  117.0 13.1 %collective-permute-start.10 = (bf16[2,128,1024]{2,1,0:T(8,128)(2,1)S(1)}, bf16[2,128,1024]{2,1,0:T(8,128)(2,1)}, u32[]{:S(2)}, u32[]{:S(2)}) collective-permute-start(bf16[2,128,1024]{2,1,0:T(8,128)(2,1)S(1)} %shard_map.98.both), channel_id=1, source_target_pairs={{0,14},{2,0},{4,2},{6,4},{8,6},{10,8},{12,10},{14,12},{1,15},{3,1}... | collective-permute-start | bytes 1572872 | tf_op jit(solution)/shard_map/ppermute | solution.py:29
  124.8 13.8 %collective-permute-start.11 = (bf16[2,128,1024]{2,1,0:T(8,128)(2,1)}, bf16[2,128,1024]{2,1,0:T(8,128)(2,1)S(1)}, u32[]{:S(2)}, u32[]{:S(2)}) collective-permute-start(bf16[2,128,1024]{2,1,0:T(8,128)(2,1)} %collective-permute-done.9), channel_id=1, source_target_pairs={{0,2},{2,4},{4,6},{6,8},{8,10},{10,12},{12,14},{14,0},{1,3},{3,5},... | collective-permute-start | bytes 1572872 | tf_op jit(solution)/shard_map/ppermute | solution.py:29
  130.0 15.9 %collective-permute-start.12 = (bf16[2,128,1024]{2,1,0:T(8,128)(2,1)}, bf16[2,128,1024]{2,1,0:T(8,128)(2,1)S(1)}, u32[]{:S(2)}, u32[]{:S(2)}) collective-permute-start(bf16[2,128,1024]{2,1,0:T(8,128)(2,1)} %collective-permute-done.10), channel_id=1, source_target_pairs={{0,14},{2,0},{4,2},{6,4},{8,6},{10,8},{12,10},{14,12},{1,15},{3,1}... | collective-permute-start | bytes 1572872 | tf_op jit(solution)/shard_map/ppermute | solution.py:29
  138.5 15.0 %collective-permute-start.13 = (bf16[2,128,1024]{2,1,0:T(8,128)(2,1)S(1)}, bf16[2,128,1024]{2,1,0:T(8,128)(2,1)S(1)}, u32[]{:S(2)}, u32[]{:S(2)}) collective-permute-start(bf16[2,128,1024]{2,1,0:T(8,128)(2,1)S(1)} %collective-permute-done.11), channel_id=1, source_target_pairs={{0,2},{2,4},{4,6},{6,8},{8,10},{10,12},{12,14},{14,0},{1,3},{3,5},... | collective-permute-start | bytes 1572872 | tf_op jit(solution)/shard_map/ppermute | solution.py:29
  145.9 16.0 %collective-permute-start.14 = (bf16[2,128,1024]{2,1,0:T(8,128)(2,1)S(1)}, bf16[2,128,1024]{2,1,0:T(8,128)(2,1)S(1)}, u32[]{:S(2)}, u32[]{:S(2)}) collective-permute-start(bf16[2,128,1024]{2,1,0:T(8,128)(2,1)S(1)} %collective-permute-done.12), channel_id=1, source_target_pairs={{0,14},{2,0},{4,2},{6,4},{8,6},{10,8},{12,10},{14,12},{1,15},{3,1}... | collective-permute-start | bytes 1572872 | tf_op jit(solution)/shard_map/ppermute | solution.py:29
  153.6 9.5 %collective-permute-start.15 = (bf16[1,128,1024]{2,1,0:T(8,128)(2,1)S(1)}, bf16[1,128,1024]{2,1,0:T(8,128)(2,1)S(1)}, u32[]{:S(2)}, u32[]{:S(2)}) collective-permute-start(bf16[1,128,1024]{2,1,0:T(8,128)(2,1)S(1)} %get-tuple-element.22), channel_id=1, source_target_pairs={{0,2},{2,4},{4,6},{6,8},{8,10},{10,12},{12,14},{14,0},{1,3},{3,5},... | collective-permute-start | bytes 786440 | tf_op jit(solution)/shard_map/ppermute | solution.py:29
  159.2 8.3 %collective-permute-start.16 = (bf16[1,128,1024]{2,1,0:T(8,128)(2,1)S(1)}, bf16[1,128,1024]{2,1,0:T(8,128)(2,1)S(1)}, u32[]{:S(2)}, u32[]{:S(2)}) collective-permute-start(bf16[1,128,1024]{2,1,0:T(8,128)(2,1)S(1)} %get-tuple-element.21), channel_id=1, source_target_pairs={{0,2},{2,4},{4,6},{6,8},{8,10},{10,12},{12,14},{14,0},{1,3},{3,5},... | collective-permute-start | bytes 786440 | tf_op jit(solution)/shard_map/ppermute | solution.py:29
Sparse Core Ops, SparseCore 0:
  10.1 50.6 all-gather.3

commit v9 on v8

--- a/solution.py
+++ b/solution.py
@@ -236,13 +236,14 @@
         at = lax.rem(place[0] + distance + Y, Y)
         return lax.dynamic_update_slice(params, chunk[:, None], (block, at, 0, 0))
 
-    up = down = both
-    for step in range(1, 4):
-        up, down = hop(up, 1), hop(down, -1)
-        params = put(params, up, 0, -step)
-        params = put(params, down, 0, step)
-    for block in range(2):
-        params = put(params, hop(up[block : block + 1], 1), block, 4)
+    ups, down = [both[:1], both[1:]], both
+    for step in range(1, 5):
+        ups = [hop(up, 1) for up in ups]
+        if step < 4:
+            down = hop(down, -1)
+            params = put(params, down, 0, step)
+        for block in range(2):
+            params = put(params, ups[block], block, -step)
     params = params.reshape(2, 2 * Y * rows, width)
     return (params, new_master, new_momentum, new_second)
 

time: 177 us -> 188 us (1.062)
  starting transfers between devices: 71.5 us -> 82.7 us
    ppermute x15 -> x18, starting transfers between devices: 52.1 us -> 63.3 us  [hop(): return lax.ppermute(x, 'y', [(i, (i + way) % Y) for i in range(Y)])]
    dynamic_update_slice x8 -> x11, local copies, waits for them, and re-layouts: 8.5 us -> 9.2 us  [put(): return lax.dynamic_update_slice(params, chunk[:, None], (block, at, 0, 0))]
    ppermute x15 -> x18, waiting for transfers between devices: 32.9 us -> 32.6 us  [hop(): return lax.ppermute(x, 'y', [(i, (i + way) % Y) for i in range(Y)])]
  transfers between devices with their start and end apart: 19 -> 22, of which waited for: 12 -> 10; matrix products, arithmetic and copies ran while one was open for 7% -> 7% of each run, Pallas kernels for 4% -> 4%
where the time goes in v9:
time: 188 us; the launch traced here: 187 us
  starting transfers between devices  82.7 us (44%)
  waiting for transfers between devices  42.7 us (23%)
  blocking collectives  22 us (12%)
  between operations  14.4 us (8%)
  Pallas kernels  11.1 us (6%)
  local copies, waits for them, and re-layouts  10.4 us (6%)
  other arithmetic  3.49 us (2%)
    ppermute x18, starting transfers between devices, hop(): return lax.ppermute(x, 'y', [(i, (i + way) % Y) for i in range(Y)])  63.3 us
    ppermute x18, waiting for transfers between devices, hop(): return lax.ppermute(x, 'y', [(i, (i + way) % Y) for i in range(Y)])  32.6 us
    all_to_all x1, blocking collectives, on_device(): sums = lax.all_to_all(sums, GROUP, split_axis=0, concat_axis=0, tiled=True)  15 us
    all_to_all x1, starting transfers between devices, on_device(): lax.all_to_all(grad, OWNERS + ('xl',), split_axis=0, concat_axis=1, tiled...  13.8 us
    pallas_call x7, Pallas kernels, call(): pl.pallas_call(kernel, out_shape=out_shape, in_specs=in_specs, out_specs=...  11.1 us
    all_to_all x1, waiting for transfers between devices, on_device(): lax.all_to_all(grad, OWNERS + ('xl',), split_axis=0, concat_axis=1, tiled...  9.37 us
    dynamic_update_slice x11, local copies, waits for them, and re-layouts, put(): return lax.dynamic_update_slice(params, chunk[:, None], (block, at, 0, 0))  9.2 us
    all_gather x1, blocking collectives, on_device(): lax.all_gather(left_grad, 'xl', axis=0, tiled=False)  7.05 us
  transfers between devices with their start and end apart: 22, of which 10 were waited for; matrix products, arithmetic and copies ran while one was open for 7% of the time, Pallas kernels for 4%

profile of v9, /device:TPU:56, one launch (start us, length us, event | category | flops | bytes accessed | tf_op | source)
XLA Modules:
  0.0 186.8 jit_solution(17244811823953610312)
XLA Ops:
  7.9 13.8 %all-to-all-start = ((bf16[64,2,1024]{2,1,0:T(2,128)(2,1)}), bf16[64,2,1024]{2,1,0:T(2,128)(2,1)S(1)}, u32[]{:S(2)}, u32[]{:S(2)}) async-start(bf16[64,2,1024]{2,1,0:T(2,128)(2,1)} %param.6), calls=%async_computation | async-start | bytes 524288 | tf_op jit(solution)/shard_map/all_to_all | solution.py:180
  25.1 9.4 %all-to-all-done = bf16[64,2,1024]{2,1,0:T(2,128)(2,1)S(1)} async-done(((bf16[64,2,1024]{2,1,0:T(2,128)(2,1)}), bf16[64,2,1024]{2,1,0:T(2,128)(2,1)S(1)}, u32[]{:S(2)}, u32[]{:S(2)}) %all-to-all-start) | async-done | bytes 262176 | tf_op jit(solution)/shard_map/all_to_all | solution.py:180
  37.4 2.6 %collective-permute-start = (bf16[384,1024]{1,0:T(8,128)(2,1)S(1)}, bf16[384,1024]{1,0:T(8,128)(2,1)S(1)}, u32[]{:S(2)}, u32[]{:S(2)}) collective-permute-start(bf16[384,1024]{1,0:T(8,128)(2,1)S(1)} %bitcast.47), channel_id=1, source_target_pairs={{0,1},{1,0},{2,3},{3,2},{4,5},{5,4},{6,7},{7,6},{8,9},{9,8},{10,11... | collective-permute-start | bytes 2359304 | tf_op jit(solution)/shard_map/ppermute | solution.py:25
  40.0 3.9 %collective-permute-start.2 = (bf16[128,1024]{1,0:T(8,128)(2,1)S(1)}, bf16[128,1024]{1,0:T(8,128)(2,1)S(1)}, u32[]{:S(2)}, u32[]{:S(2)}) collective-permute-start(bf16[128,1024]{1,0:T(8,128)(2,1)S(1)} %shard_map.93.refs_3_.mine), channel_id=1, source_target_pairs={{0,14},{2,0},{4,2},{6,4},{8,6},{10,8},{12,10},{14,12},{1,15},{3,1}... | collective-permute-start | bytes 786440 | tf_op jit(solution)/shard_map/ppermute | solution.py:29
  44.0 7.5 %collective-permute-done.1.refs_4_ = bf16[128,1024]{1,0:T(8,128)(2,1)S(1)} collective-permute-done((bf16[128,1024]{1,0:T(8,128)(2,1)S(1)}, bf16[128,1024]{1,0:T(8,128)(2,1)S(1)}, u32[]{:S(2)}, u32[]{:S(2)}) %collective-permute-start.1) | collective-permute-done | bytes 262176 | tf_op jit(solution)/shard_map/ppermute | solution.py:29
  51.5 3.3 %collective-permute-start.3 = (bf16[128,1024]{1,0:T(8,128)(2,1)S(1)}, bf16[128,1024]{1,0:T(8,128)(2,1)S(1)}, u32[]{:S(2)}, u32[]{:S(2)}) collective-permute-start(bf16[128,1024]{1,0:T(8,128)(2,1)S(1)} %collective-permute-done.1.refs_4_), channel_id=1, source_target_pairs={{0,2},{2,4},{4,6},{6,8},{8,10},{10,12},{12,14},{14,0},{1,3},{3,5},... | collective-permute-start | bytes 786440 | tf_op jit(solution)/shard_map/ppermute | solution.py:29
  59.5 3.3 %collective-permute-done.3.refs_6_ = bf16[128,1024]{1,0:T(8,128)(2,1)S(1)} collective-permute-done((bf16[128,1024]{1,0:T(8,128)(2,1)S(1)}, bf16[128,1024]{1,0:T(8,128)(2,1)S(1)}, u32[]{:S(2)}, u32[]{:S(2)}) %collective-permute-start.3) | collective-permute-done | bytes 262176 | tf_op jit(solution)/shard_map/ppermute | solution.py:29
  62.8 4.6 %collective-permute-start.5 = (bf16[128,1024]{1,0:T(8,128)(2,1)S(1)}, bf16[128,1024]{1,0:T(8,128)(2,1)}, u32[]{:S(2)}, u32[]{:S(2)}) collective-permute-start(bf16[128,1024]{1,0:T(8,128)(2,1)S(1)} %collective-permute-done.3.refs_6_), channel_id=1, source_target_pairs={{0,2},{2,4},{4,6},{6,8},{8,10},{10,12},{12,14},{14,0},{1,3},{3,5},... | collective-permute-start | bytes 786440 | tf_op jit(solution)/shard_map/ppermute | solution.py:29
  69.4 3.7 %collective-permute-done.5.refs_8_ = bf16[128,1024]{1,0:T(8,128)(2,1)} collective-permute-done((bf16[128,1024]{1,0:T(8,128)(2,1)S(1)}, bf16[128,1024]{1,0:T(8,128)(2,1)}, u32[]{:S(2)}, u32[]{:S(2)}) %collective-permute-start.5) | collective-permute-done | bytes 262176 | tf_op jit(solution)/shard_map/ppermute | solution.py:29
  73.0 5.6 %collective-permute-start.7 = (bf16[128,1024]{1,0:T(8,128)(2,1)}, bf16[128,1024]{1,0:T(8,128)(2,1)}, u32[]{:S(2)}, u32[]{:S(2)}) collective-permute-start(bf16[128,1024]{1,0:T(8,128)(2,1)} %collective-permute-done.5.refs_8_), channel_id=1, source_target_pairs={{0,2},{2,4},{4,6},{6,8},{8,10},{10,12},{12,14},{14,0},{1,3},{3,5},... | collective-permute-start | bytes 786440 | tf_op jit(solution)/shard_map/ppermute | solution.py:29
  85.0 7.0 %all-gather.1 = bf16[256,1024]{1,0:T(8,128)(2,1)S(1)} all-gather(bf16[128,1024]{1,0:T(8,128)(2,1)S(1)} %shard_map.96), channel_id=3, replica_groups=mesh['z'=8,'xh'=2,'c'=2,'y'=8,'xl'=2] {'xl'}, dimensions={0}, use_global_device_ids=true | all-gather | bytes 786432 | tf_op jit(solution)/shard_map/all_gather | solution.py:215
  93.5 2.9 %collective-permute-start.8 = (bf16[2,128,512]{2,1,0:T(8,128)(2,1)S(1)}, bf16[2,128,512]{2,1,0:T(8,128)(2,1)S(1)}, u32[]{:S(2)}, u32[]{:S(2)}) collective-permute-start(bf16[2,128,512]{2,1,0:T(8,128)(2,1)S(1)} %get-tuple-element.13.mine), channel_id=1, source_target_pairs={{0,1},{1,0},{2,3},{3,2},{4,5},{5,4},{6,7},{7,6},{8,9},{9,8},{10,11... | collective-permute-start | bytes 786440 | tf_op jit(solution)/shard_map/ppermute | solution.py:25
  96.4 15.0 %all_to_all.14.sums = f32[16,1,128]{2,1,0:T(1,128)S(1)} all-to-all(f32[16,1,128]{2,1,0:T(1,128)S(1)} %get-tuple-element.12), channel_id=1, replica_groups=mesh['z'=8,'xh'=2,'c'=2,'y'=8,'xl'=2] {'y','xl'}, dimensions={0} | all-to-all | bytes 16384 | tf_op jit(solution)/shard_map/all_to_all | solution.py:219
  112.4 2.5 %collective-permute-start.9 = (bf16[2,128,1024]{2,1,0:T(8,128)(2,1)S(1)}, bf16[2,128,1024]{2,1,0:T(8,128)(2,1)S(1)}, u32[]{:S(2)}, u32[]{:S(2)}) collective-permute-start(bf16[2,128,1024]{2,1,0:T(8,128)(2,1)S(1)} %shard_map.98.both), channel_id=1, source_target_pairs={{0,14},{2,0},{4,2},{6,4},{8,6},{10,8},{12,10},{14,12},{1,15},{3,1}... | collective-permute-start | bytes 1572872 | tf_op jit(solution)/shard_map/ppermute | solution.py:29
  115.0 4.5 %collective-permute-start.10 = (bf16[1,128,1024]{2,1,0:T(8,128)(2,1)S(1)}, bf16[1,128,1024]{2,1,0:T(8,128)(2,1)S(1)}, u32[]{:S(2)}, u32[]{:S(2)}) collective-permute-start(bf16[1,128,1024]{2,1,0:T(8,128)(2,1)S(1)} %get-tuple-element.22), channel_id=1, source_target_pairs={{0,2},{2,4},{4,6},{6,8},{8,10},{10,12},{12,14},{14,0},{1,3},{3,5},... | collective-permute-start | bytes 786440 | tf_op jit(solution)/shard_map/ppermute | solution.py:29
  119.6 3.4 %collective-permute-start.11 = (bf16[1,128,1024]{2,1,0:T(8,128)(2,1)S(1)}, bf16[1,128,1024]{2,1,0:T(8,128)(2,1)}, u32[]{:S(2)}, u32[]{:S(2)}) collective-permute-start(bf16[1,128,1024]{2,1,0:T(8,128)(2,1)S(1)} %get-tuple-element.21), channel_id=1, source_target_pairs={{0,2},{2,4},{4,6},{6,8},{8,10},{10,12},{12,14},{14,0},{1,3},{3,5},... | collective-permute-start | bytes 786440 | tf_op jit(solution)/shard_map/ppermute | solution.py:29
  122.9 3.2 %collective-permute-done.10 = bf16[1,128,1024]{2,1,0:T(8,128)(2,1)S(1)} collective-permute-done((bf16[1,128,1024]{2,1,0:T(8,128)(2,1)S(1)}, bf16[1,128,1024]{2,1,0:T(8,128)(2,1)S(1)}, u32[]{:S(2)}, u32[]{:S(2)}) %collective-permute-start.10) | collective-permute-done | bytes 262176 | tf_op jit(solution)/shard_map/ppermute | solution.py:29
  126.1 3.9 %collective-permute-start.13 = (bf16[1,128,1024]{2,1,0:T(8,128)(2,1)S(1)}, bf16[1,128,1024]{2,1,0:T(8,128)(2,1)S(1)}, u32[]{:S(2)}, u32[]{:S(2)}) collective-permute-start(bf16[1,128,1024]{2,1,0:T(8,128)(2,1)S(1)} %collective-permute-done.10), channel_id=1, source_target_pairs={{0,2},{2,4},{4,6},{6,8},{8,10},{10,12},{12,14},{14,0},{1,3},{3,5},... | collective-permute-start | bytes 786440 | tf_op jit(solution)/shard_map/ppermute | solution.py:29
  131.8 3.9 %collective-permute-start.14 = (bf16[1,128,1024]{2,1,0:T(8,128)(2,1)}, bf16[1,128,1024]{2,1,0:T(8,128)(2,1)S(1)}, u32[]{:S(2)}, u32[]{:S(2)}) collective-permute-start(bf16[1,128,1024]{2,1,0:T(8,128)(2,1)} %collective-permute-done.11), channel_id=1, source_target_pairs={{0,2},{2,4},{4,6},{6,8},{8,10},{10,12},{12,14},{14,0},{1,3},{3,5},... | collective-permute-start | bytes 786440 | tf_op jit(solution)/shard_map/ppermute | solution.py:29
  135.8 3.4 %shard_map.99 = (f32[2,64,1024]{2,1,0:T(8,128)}, f32[2,64,1024]{2,1,0:T(8,128)}, bf16[2,8,128,1024]{3,2,1,0:T(8,128)(2,1)}) custom-call(s32[2]{0:T(128)S(1)} %pad_add_fusion.refs_0_.place, f32[16,1,128]{2,1,0:T(1,128)S(1)} %all_to_all.14.sums, bf16[2,128,512]{2,1,0:T(8,128)(2,1)S(1)} %get-tuple-element.13.mine, ...), custom_call_target="tpu_custom_call" | custom-call | bytes 4210704 | tf_op jit(solution)/shard_map/pallas_call | solution.py:150
  141.9 5.1 %collective-permute-start.16 = (bf16[1,128,1024]{2,1,0:T(8,128)(2,1)S(1)}, bf16[1,128,1024]{2,1,0:T(8,128)(2,1)S(1)}, u32[]{:S(2)}, u32[]{:S(2)}) collective-permute-start(bf16[1,128,1024]{2,1,0:T(8,128)(2,1)S(1)} %collective-permute-done.13), channel_id=1, source_target_pairs={{0,2},{2,4},{4,6},{6,8},{8,10},{10,12},{12,14},{14,0},{1,3},{3,5},... | collective-permute-start | bytes 786440 | tf_op jit(solution)/shard_map/ppermute | solution.py:29
  153.7 5.6 %collective-permute-start.18 = (bf16[1,128,1024]{2,1,0:T(8,128)(2,1)S(1)}, bf16[1,128,1024]{2,1,0:T(8,128)(2,1)S(1)}, u32[]{:S(2)}, u32[]{:S(2)}) collective-permute-start(bf16[1,128,1024]{2,1,0:T(8,128)(2,1)S(1)} %collective-permute-done.16), channel_id=1, source_target_pairs={{0,2},{2,4},{4,6},{6,8},{8,10},{10,12},{12,14},{14,0},{1,3},{3,5},... | collective-permute-start | bytes 786440 | tf_op jit(solution)/shard_map/ppermute | solution.py:29
  159.3 4.6 %collective-permute-start.19 = (bf16[1,128,1024]{2,1,0:T(8,128)(2,1)S(1)}, bf16[1,128,1024]{2,1,0:T(8,128)(2,1)S(1)}, u32[]{:S(2)}, u32[]{:S(2)}) collective-permute-start(bf16[1,128,1024]{2,1,0:T(8,128)(2,1)S(1)} %collective-permute-done.17), channel_id=1, source_target_pairs={{0,2},{2,4},{4,6},{6,8},{8,10},{10,12},{12,14},{14,0},{1,3},{3,5},... | collective-permute-start | bytes 786440 | tf_op jit(solution)/shard_map/ppermute | solution.py:29
  168.1 8.1 %collective-permute-done.15 = bf16[2,128,1024]{2,1,0:T(8,128)(2,1)S(1)} collective-permute-done((bf16[2,128,1024]{2,1,0:T(8,128)(2,1)S(1)}, bf16[2,128,1024]{2,1,0:T(8,128)(2,1)S(1)}, u32[]{:S(2)}, u32[]{:S(2)}) %collective-permute-start.15) | collective-permute-done | bytes 524320 | tf_op jit(solution)/shard_map/ppermute | solution.py:29
  (61 shorter events, 41.6 us)
Async XLA Ops:
  7.2 71.5 %copy-start = (bf16[2,64,1024]{2,1,0:T(8,128)(2,1)S(1)}, bf16[2,64,1024]{2,1,0:T(8,128)(2,1)}, u32[]{:S(2)}) copy-start(bf16[2,64,1024]{2,1,0:T(8,128)(2,1)} %refs_1_.3) | copy-start | bytes 786436
  7.2 73.1 %all-gather.4.cloned.1.call-start = ((), (), s32[]{:S(2)}) async-start(), calls=%async_computation.2 | async-start | bytes 2359296 | tf_op jit(solution)/shard_map/all_gather | solution.py:172
  7.9 26.6 %all-to-all-start = ((bf16[64,2,1024]{2,1,0:T(2,128)(2,1)}), bf16[64,2,1024]{2,1,0:T(2,128)(2,1)S(1)}, u32[]{:S(2)}, u32[]{:S(2)}) async-start(bf16[64,2,1024]{2,1,0:T(2,128)(2,1)} %param.6), calls=%async_computation | async-start | bytes 524288 | tf_op jit(solution)/shard_map/all_to_all | solution.py:180
  25.1 56.0 %copy-start.4 = (f32[2,64,1024]{2,1,0:T(8,128)S(1)}, f32[2,64,1024]{2,1,0:T(8,128)}, u32[]{:S(2)}) copy-start(f32[2,64,1024]{2,1,0:T(8,128)} %second.1) | copy-start | bytes 1572868
  35.3 16.2 %collective-permute-start.1 = (bf16[128,1024]{1,0:T(8,128)(2,1)S(1)}, bf16[128,1024]{1,0:T(8,128)(2,1)S(1)}, u32[]{:S(2)}, u32[]{:S(2)}) collective-permute-start(bf16[128,1024]{1,0:T(8,128)(2,1)S(1)} %shard_map.93.refs_3_.mine), channel_id=1, source_target_pairs={{0,2},{2,4},{4,6},{6,8},{8,10},{10,12},{12,14},{14,0},{1,3},{3,5},... | collective-permute-start | bytes 786440 | tf_op jit(solution)/shard_map/ppermute | solution.py:29
  37.4 41.2 %collective-permute-start = (bf16[384,1024]{1,0:T(8,128)(2,1)S(1)}, bf16[384,1024]{1,0:T(8,128)(2,1)S(1)}, u32[]{:S(2)}, u32[]{:S(2)}) collective-permute-start(bf16[384,1024]{1,0:T(8,128)(2,1)S(1)} %bitcast.47), channel_id=1, source_target_pairs={{0,1},{1,0},{2,3},{3,2},{4,5},{5,4},{6,7},{7,6},{8,9},{9,8},{10,11... | collective-permute-start | bytes 2359304 | tf_op jit(solution)/shard_map/ppermute | solution.py:25
  40.0 16.9 %collective-permute-start.2 = (bf16[128,1024]{1,0:T(8,128)(2,1)S(1)}, bf16[128,1024]{1,0:T(8,128)(2,1)S(1)}, u32[]{:S(2)}, u32[]{:S(2)}) collective-permute-start(bf16[128,1024]{1,0:T(8,128)(2,1)S(1)} %shard_map.93.refs_3_.mine), channel_id=1, source_target_pairs={{0,14},{2,0},{4,2},{6,4},{8,6},{10,8},{12,10},{14,12},{1,15},{3,1}... | collective-permute-start | bytes 786440 | tf_op jit(solution)/shard_map/ppermute | solution.py:29
  51.5 11.3 %collective-permute-start.3 = (bf16[128,1024]{1,0:T(8,128)(2,1)S(1)}, bf16[128,1024]{1,0:T(8,128)(2,1)S(1)}, u32[]{:S(2)}, u32[]{:S(2)}) collective-permute-start(bf16[128,1024]{1,0:T(8,128)(2,1)S(1)} %collective-permute-done.1.refs_4_), channel_id=1, source_target_pairs={{0,2},{2,4},{4,6},{6,8},{8,10},{10,12},{12,14},{14,0},{1,3},{3,5},... | collective-permute-start | bytes 786440 | tf_op jit(solution)/shard_map/ppermute | solution.py:29
  57.0 10.4 %collective-permute-start.4 = (bf16[128,1024]{1,0:T(8,128)(2,1)S(1)}, bf16[128,1024]{1,0:T(8,128)(2,1)}, u32[]{:S(2)}, u32[]{:S(2)}) collective-permute-start(bf16[128,1024]{1,0:T(8,128)(2,1)S(1)} %collective-permute-done.2.refs_5_), channel_id=1, source_target_pairs={{0,14},{2,0},{4,2},{6,4},{8,6},{10,8},{12,10},{14,12},{1,15},{3,1}... | collective-permute-start | bytes 786440 | tf_op jit(solution)/shard_map/ppermute | solution.py:29
  62.8 10.2 %collective-permute-start.5 = (bf16[128,1024]{1,0:T(8,128)(2,1)S(1)}, bf16[128,1024]{1,0:T(8,128)(2,1)}, u32[]{:S(2)}, u32[]{:S(2)}) collective-permute-start(bf16[128,1024]{1,0:T(8,128)(2,1)S(1)} %collective-permute-done.3.refs_6_), channel_id=1, source_target_pairs={{0,2},{2,4},{4,6},{6,8},{8,10},{10,12},{12,14},{14,0},{1,3},{3,5},... | collective-permute-start | bytes 786440 | tf_op jit(solution)/shard_map/ppermute | solution.py:29
  67.4 15.3 %collective-permute-start.6 = (bf16[128,1024]{1,0:T(8,128)(2,1)}, bf16[128,1024]{1,0:T(8,128)(2,1)}, u32[]{:S(2)}, u32[]{:S(2)}) collective-permute-start(bf16[128,1024]{1,0:T(8,128)(2,1)} %collective-permute-done.4.refs_7_), channel_id=1, source_target_pairs={{0,14},{2,0},{4,2},{6,4},{8,6},{10,8},{12,10},{14,12},{1,15},{3,1}... | collective-permute-start | bytes 786440 | tf_op jit(solution)/shard_map/ppermute | solution.py:29
  73.0 10.5 %collective-permute-start.7 = (bf16[128,1024]{1,0:T(8,128)(2,1)}, bf16[128,1024]{1,0:T(8,128)(2,1)}, u32[]{:S(2)}, u32[]{:S(2)}) collective-permute-start(bf16[128,1024]{1,0:T(8,128)(2,1)} %collective-permute-done.5.refs_8_), channel_id=1, source_target_pairs={{0,2},{2,4},{4,6},{6,8},{8,10},{10,12},{12,14},{14,0},{1,3},{3,5},... | collective-permute-start | bytes 786440 | tf_op jit(solution)/shard_map/ppermute | solution.py:29
  93.5 17.8 %collective-permute-start.8 = (bf16[2,128,512]{2,1,0:T(8,128)(2,1)S(1)}, bf16[2,128,512]{2,1,0:T(8,128)(2,1)S(1)}, u32[]{:S(2)}, u32[]{:S(2)}) collective-permute-start(bf16[2,128,512]{2,1,0:T(8,128)(2,1)S(1)} %get-tuple-element.13.mine), channel_id=1, source_target_pairs={{0,1},{1,0},{2,3},{3,2},{4,5},{5,4},{6,7},{7,6},{8,9},{9,8},{10,11... | collective-permute-start | bytes 786440 | tf_op jit(solution)/shard_map/ppermute | solution.py:25
  112.4 26.7 %collective-permute-start.9 = (bf16[2,128,1024]{2,1,0:T(8,128)(2,1)S(1)}, bf16[2,128,1024]{2,1,0:T(8,128)(2,1)S(1)}, u32[]{:S(2)}, u32[]{:S(2)}) collective-permute-start(bf16[2,128,1024]{2,1,0:T(8,128)(2,1)S(1)} %shard_map.98.both), channel_id=1, source_target_pairs={{0,14},{2,0},{4,2},{6,4},{8,6},{10,8},{12,10},{14,12},{1,15},{3,1}... | collective-permute-start | bytes 1572872 | tf_op jit(solution)/shard_map/ppermute | solution.py:29
  115.0 11.1 %collective-permute-start.10 = (bf16[1,128,1024]{2,1,0:T(8,128)(2,1)S(1)}, bf16[1,128,1024]{2,1,0:T(8,128)(2,1)S(1)}, u32[]{:S(2)}, u32[]{:S(2)}) collective-permute-start(bf16[1,128,1024]{2,1,0:T(8,128)(2,1)S(1)} %get-tuple-element.22), channel_id=1, source_target_pairs={{0,2},{2,4},{4,6},{6,8},{8,10},{10,12},{12,14},{14,0},{1,3},{3,5},... | collective-permute-start | bytes 786440 | tf_op jit(solution)/shard_map/ppermute | solution.py:29
  119.6 12.3 %collective-permute-start.11 = (bf16[1,128,1024]{2,1,0:T(8,128)(2,1)S(1)}, bf16[1,128,1024]{2,1,0:T(8,128)(2,1)}, u32[]{:S(2)}, u32[]{:S(2)}) collective-permute-start(bf16[1,128,1024]{2,1,0:T(8,128)(2,1)S(1)} %get-tuple-element.21), channel_id=1, source_target_pairs={{0,2},{2,4},{4,6},{6,8},{8,10},{10,12},{12,14},{14,0},{1,3},{3,5},... | collective-permute-start | bytes 786440 | tf_op jit(solution)/shard_map/ppermute | solution.py:29
  126.1 15.8 %collective-permute-start.13 = (bf16[1,128,1024]{2,1,0:T(8,128)(2,1)S(1)}, bf16[1,128,1024]{2,1,0:T(8,128)(2,1)S(1)}, u32[]{:S(2)}, u32[]{:S(2)}) collective-permute-start(bf16[1,128,1024]{2,1,0:T(8,128)(2,1)S(1)} %collective-permute-done.10), channel_id=1, source_target_pairs={{0,2},{2,4},{4,6},{6,8},{8,10},{10,12},{12,14},{14,0},{1,3},{3,5},... | collective-permute-start | bytes 786440 | tf_op jit(solution)/shard_map/ppermute | solution.py:29
  131.8 15.2 %collective-permute-start.14 = (bf16[1,128,1024]{2,1,0:T(8,128)(2,1)}, bf16[1,128,1024]{2,1,0:T(8,128)(2,1)S(1)}, u32[]{:S(2)}, u32[]{:S(2)}) collective-permute-start(bf16[1,128,1024]{2,1,0:T(8,128)(2,1)} %collective-permute-done.11), channel_id=1, source_target_pairs={{0,2},{2,4},{4,6},{6,8},{8,10},{10,12},{12,14},{14,0},{1,3},{3,5},... | collective-permute-start | bytes 786440 | tf_op jit(solution)/shard_map/ppermute | solution.py:29
  139.2 24.7 %collective-permute-start.12 = (bf16[2,128,1024]{2,1,0:T(8,128)(2,1)S(1)}, bf16[2,128,1024]{2,1,0:T(8,128)(2,1)S(1)}, u32[]{:S(2)}, u32[]{:S(2)}) collective-permute-start(bf16[2,128,1024]{2,1,0:T(8,128)(2,1)S(1)} %collective-permute-done.9), channel_id=1, source_target_pairs={{0,14},{2,0},{4,2},{6,4},{8,6},{10,8},{12,10},{14,12},{1,15},{3,1}... | collective-permute-start | bytes 1572872 | tf_op jit(solution)/shard_map/ppermute | solution.py:29
  141.9 11.8 %collective-permute-start.16 = (bf16[1,128,1024]{2,1,0:T(8,128)(2,1)S(1)}, bf16[1,128,1024]{2,1,0:T(8,128)(2,1)S(1)}, u32[]{:S(2)}, u32[]{:S(2)}) collective-permute-start(bf16[1,128,1024]{2,1,0:T(8,128)(2,1)S(1)} %collective-permute-done.13), channel_id=1, source_target_pairs={{0,2},{2,4},{4,6},{6,8},{8,10},{10,12},{12,14},{14,0},{1,3},{3,5},... | collective-permute-start | bytes 786440 | tf_op jit(solution)/shard_map/ppermute | solution.py:29
  147.1 12.3 %collective-permute-start.17 = (bf16[1,128,1024]{2,1,0:T(8,128)(2,1)S(1)}, bf16[1,128,1024]{2,1,0:T(8,128)(2,1)S(1)}, u32[]{:S(2)}, u32[]{:S(2)}) collective-permute-start(bf16[1,128,1024]{2,1,0:T(8,128)(2,1)S(1)} %collective-permute-done.14), channel_id=1, source_target_pairs={{0,2},{2,4},{4,6},{6,8},{8,10},{10,12},{12,14},{14,0},{1,3},{3,5},... | collective-permute-start | bytes 786440 | tf_op jit(solution)/shard_map/ppermute | solution.py:29
  153.7 24.7 %collective-permute-start.18 = (bf16[1,128,1024]{2,1,0:T(8,128)(2,1)S(1)}, bf16[1,128,1024]{2,1,0:T(8,128)(2,1)S(1)}, u32[]{:S(2)}, u32[]{:S(2)}) collective-permute-start(bf16[1,128,1024]{2,1,0:T(8,128)(2,1)S(1)} %collective-permute-done.16), channel_id=1, source_target_pairs={{0,2},{2,4},{4,6},{6,8},{8,10},{10,12},{12,14},{14,0},{1,3},{3,5},... | collective-permute-start | bytes 786440 | tf_op jit(solution)/shard_map/ppermute | solution.py:29
  159.3 19.9 %collective-permute-start.19 = (bf16[1,128,1024]{2,1,0:T(8,128)(2,1)S(1)}, bf16[1,128,1024]{2,1,0:T(8,128)(2,1)S(1)}, u32[]{:S(2)}, u32[]{:S(2)}) collective-permute-start(bf16[1,128,1024]{2,1,0:T(8,128)(2,1)S(1)} %collective-permute-done.17), channel_id=1, source_target_pairs={{0,2},{2,4},{4,6},{6,8},{8,10},{10,12},{12,14},{14,0},{1,3},{3,5},... | collective-permute-start | bytes 786440 | tf_op jit(solution)/shard_map/ppermute | solution.py:29
  163.9 12.3 %collective-permute-start.15 = (bf16[2,128,1024]{2,1,0:T(8,128)(2,1)S(1)}, bf16[2,128,1024]{2,1,0:T(8,128)(2,1)S(1)}, u32[]{:S(2)}, u32[]{:S(2)}) collective-permute-start(bf16[2,128,1024]{2,1,0:T(8,128)(2,1)S(1)} %collective-permute-done.12), channel_id=1, source_target_pairs={{0,14},{2,0},{4,2},{6,4},{8,6},{10,8},{12,10},{14,12},{1,15},{3,1}... | collective-permute-start | bytes 1572872 | tf_op jit(solution)/shard_map/ppermute | solution.py:29
  (3 other events, 116.3 us)
Sparse Core Ops, SparseCore 0:
  10.1 50.6 all-gather.3
